TPU v7x, 32 devices: a whole 2x2x4 slice. The times are simulated.
32 devices in a mesh: wide: 8 (over z, x), narrow: 4 (over y, core).
Axes of the slice: x: 2, y: 2, z: 4, core: 2. Of those that a mesh axis runs over, the one named last changes fastest.
Arguments:
- tokens: bfloat16 [32768, 768], P(('wide', 'narrow')), may hold values from -6 to 6
- out_grad: bfloat16 [32768, 768], P(('wide', 'narrow')), may hold values from -6 to 6
- doc_lengths: int32 [16], replicated, may hold values from 1 to 30713, as said below
- w_query: bfloat16 [768, 768], replicated, may hold values from -0.21875 to 0.21875
- b_query: bfloat16 [768], replicated, may hold values from -3 to 3
- w_key: bfloat16 [768, 768], replicated, may hold values from -0.21875 to 0.21875
- b_key: bfloat16 [768], replicated, may hold values from -3 to 3
- w_value: bfloat16 [768, 768], replicated, may hold values from -0.21875 to 0.21875
- b_value: bfloat16 [768], replicated, may hold values from -0.015625 to 0.015625
- w_output: bfloat16 [768, 768], replicated, may hold values from -28 to 28
- b_output: bfloat16 [768], replicated, may hold values from -0.625 to 0.625
- w_inner: bfloat16 [768, 3072], replicated, may hold values from -0.21875 to 0.21875
- b_inner: bfloat16 [3072], replicated, may hold values from -0.625 to 0.625
- w_outer: bfloat16 [3072, 768], replicated, may hold values from -0.109375 to 0.109375
- b_outer: bfloat16 [768], replicated, may hold values from -0.625 to 0.625
- gain_first: bfloat16 [768], replicated, may hold values from 0.5 to 1.5
- shift_first: bfloat16 [768], replicated, may hold values from -0.625 to 0.625
- gain_second: bfloat16 [768], replicated, may hold values from 0.5 to 1.5
- shift_second: bfloat16 [768], replicated, may hold values from -0.625 to 0.625
Outputs:
- block_out: bfloat16 [32768, 768], P(('wide', 'narrow'))
- grad_tokens: bfloat16 [32768, 768], P(('wide', 'narrow'))
- grad_w_query: float32 [768, 768], P(('wide', 'narrow'))
- grad_b_query: float32 [768], P(('wide', 'narrow'))
- grad_w_key: float32 [768, 768], P(('wide', 'narrow'))
- grad_b_key: float32 [768], P(('wide', 'narrow'))
- grad_w_value: float32 [768, 768], P(('wide', 'narrow'))
- grad_b_value: float32 [768], P(('wide', 'narrow'))
- grad_w_output: float32 [768, 768], P(('wide', 'narrow'))
- grad_b_output: float32 [768], P(('wide', 'narrow'))
- grad_w_inner: float32 [768, 3072], P(('wide', 'narrow'))
- grad_b_inner: float32 [3072], P(('wide', 'narrow'))
- grad_w_outer: float32 [3072, 768], P(('wide', 'narrow'))
- grad_b_outer: float32 [768], P(('wide', 'narrow'))
- grad_gain_first: float32 [768], P(('wide', 'narrow'))
- grad_shift_first: float32 [768], P(('wide', 'narrow'))
- grad_gain_second: float32 [768], P(('wide', 'narrow'))
- grad_shift_second: float32 [768], P(('wide', 'narrow'))
Inputs may be any that keep to these rules, and one draw needn't show every extreme that they name: `doc_lengths`: one document, at a place in the order drawn from the seed, holds 32768 - 256 - (16 - 2) // 2 * (256 + 1) tokens. Of the others, one has exactly 256 tokens and the rest come in pairs whose lengths sum to 256 + 1 (one pair is 1 and 256), in an order drawn from the seed. The lengths sum to 32768.
All inputs are finite; a program needn't handle non-finite values.
Results may differ from a plain program's by a relative error of at most 0.015.
Values may be sent and summed in bfloat16 or wider, within the bound.
No kernel may reach another device: no remote copies, remote signals or barrier semaphores. Data moves between devices by JAX's collectives and lax.ppermute only.
A program may use at most 192 MiB of HBM per device.

v0:
```python
import functools
import math

import jax
import jax.numpy as jnp
from jax import lax
from jax.experimental import pallas as pl
from jax.experimental.pallas import tpu as pltpu
from jax.sharding import PartitionSpec as P

DH = 64
LANES = 128
CHUNK = 256
SLICE = 16
EPS = 1e-05
HALF_PI = math.pi / 2.0
MIB = 1 << 20
VMEM = 60
COST = 10
FILL = 40
AXES = ("wide", "narrow")

f32 = jnp.float32
bf16 = jnp.bfloat16

R_BQ, R_BK, R_BV, R_BO, R_G1, R_E1, R_B2, R_G2, R_E2, R_B1 = range(10)
V_B2, V_G2, V_E2, V_G1, V_E1, V_BO, V_B1 = range(7)
VEC_ROWS = 16


def nn(a, b):
    return jnp.dot(a, b, preferred_element_type=f32)


def nt(a, b):
    return lax.dot_general(a, b, (((1,), (1,)), ((), ())), preferred_element_type=f32)


def tn(a, b):
    return lax.dot_general(a, b, (((0,), (0,)), ((), ())), preferred_element_type=f32)


def lane_iota(rows, lanes=LANES):
    return lax.broadcasted_iota(jnp.int32, (rows, lanes), 1)


def row_iota(rows, lanes=LANES):
    return lax.broadcasted_iota(jnp.int32, (rows, lanes), 0)


def swap_halves(x):
    return pltpu.roll(x, DH, 1)


def softplus(x):
    return jnp.maximum(x, 0.0) + jnp.log1p(jnp.exp(-jnp.abs(x)))


def sigmoid(x):
    return 1.0 / (1.0 + jnp.exp(-x))


def sine(b):
    s = b * b
    p = 1.0 / 6227020800.0
    for c in (-1.0 / 39916800.0, 1.0 / 362880.0, -1.0 / 5040.0, 1.0 / 120.0, -1.0 / 6.0):
        p = p * s + c
    return b + b * s * p


def features(pair, cs, lo):
    soft = softplus(pair)
    other = swap_halves(soft)
    return (
        (jnp.where(lo, soft, other) * cs).astype(bf16),
        (jnp.where(lo, other, soft) * cs).astype(bf16),
    )


def extended(v, lo):
    one = jnp.ones_like(v)
    return jnp.where(lo, v, one), jnp.where(lo, one, v)


def pairs_of(width):
    return width // LANES


def lookup(len_ref, pos):
    start = jnp.zeros(pos.shape, jnp.int32)
    end = jnp.zeros(pos.shape, jnp.int32)
    edge = jnp.int32(0)
    for doc in range(len_ref.shape[0]):
        here = pos >= edge
        after = edge + len_ref[doc]
        start = jnp.where(here, edge, start)
        end = jnp.where(here, after, end)
        edge = after
    return start, end


F_BEFORE, F_NEXT_B, F_AFTER, F_NEXT_A, F_CLOSING, F_OPENING = range(6)


def flag_table(len_ref, place, rows):
    bit, lane = row_iota(8), lane_iota(8)
    upper = jnp.bitwise_and(jnp.right_shift(jnp.full_like(bit, place), bit), 1) == 1
    base, close = place * rows, (place + 1) * rows
    is_before = (lane == F_BEFORE) | (lane == F_NEXT_B)
    is_after = (lane == F_AFTER) | (lane == F_NEXT_A)
    pos = jnp.where(
        is_before,
        base - 1,
        jnp.where(is_after, close, jnp.where(lane == F_CLOSING, close - 1, base)),
    )
    start, end = lookup(len_ref, pos)
    one, zero = jnp.ones(bit.shape, f32), jnp.zeros(bit.shape, f32)
    is_long = jnp.where((end - start) > rows, one, zero)
    near = jnp.where((pos >= 0) & (pos < end), 1.0 - is_long, zero)
    out = is_long
    out = jnp.where(lane == F_BEFORE, jnp.where(upper, is_long, zero), out)
    out = jnp.where(lane == F_AFTER, jnp.where(upper, zero, is_long), out)
    return jnp.where((lane == F_NEXT_B) | (lane == F_NEXT_A), near, out)


def key_kernel(
    spot_ref, len_ref, x_ref, wk_ref, wv_ref,
    bq, bk, bv, bo, g1, e1, b2, g2, e2, b1,
    k_ref, v_ref, kf_ref, cs_ref, st_ref, en_ref, state_ref, next_ref, flag_ref, vec_ref,
    total,
    *, rows,
):
    step = pl.program_id(0)
    base = spot_ref[0]
    width = x_ref.shape[1]
    first = base + step * CHUNK
    pos = first + row_iota(CHUNK)
    lane = lane_iota(CHUNK)
    lo = lane < DH

    @pl.when(step == 0)
    def _():
        total[...] = jnp.zeros_like(total)
        flag_ref[...] = flag_table(len_ref, spot_ref[1], rows)
        for r, ref in enumerate((bq, bk, bv, bo, g1, e1, b2, g2, e2)):
            vec_ref[r : r + 1, :] = ref[...].astype(f32).reshape(1, width)
        for r in range(b1.shape[0] // width):
            vec_ref[R_B1 + r : R_B1 + r + 1, :] = (
                b1[r * width : (r + 1) * width].astype(f32).reshape(1, width)
            )

    start, end = lookup(len_ref, pos)
    part = jnp.where(lo, end - pos, pos - start).astype(f32)
    cs = sine(HALF_PI * part / (end - start).astype(f32))
    cs_ref[...] = cs
    st_ref[...] = start
    en_ref[...] = end

    x = x_ref[...]
    k = (nn(x, wk_ref[...]) + vec_ref[R_BK : R_BK + 1, :]).astype(bf16)
    v = (nn(x, wv_ref[...]) + vec_ref[R_BV : R_BV + 1, :]).astype(bf16)
    k_ref[...] = k
    v_ref[...] = v
    closing = end >= base + rows
    slots = lane_iota(LANES)
    lo_state = slots < DH

    npair = pairs_of(width)
    zcol = jnp.zeros((LANES, LANES), f32)
    for g in range(npair):
        cols = slice(g * LANES, (g + 1) * LANES)
        fa, fb = features(k[:, cols].astype(f32), cs, lo)
        kf_ref[:, 2 * g * LANES : (2 * g + 1) * LANES] = fa
        kf_ref[:, (2 * g + 1) * LANES : (2 * g + 2) * LANES] = fb
        va, vb = extended(v[:, cols], lo)
        zero = jnp.zeros_like(fa)
        sa = tn(jnp.where(closing, fa, zero), va)
        sb = tn(jnp.where(closing, fb, zero), vb)
        total[g] += jnp.where(lo_state, sa, sb)
        zcol = jnp.where(slots == DH + g, sa, jnp.where(slots == g, sb, zcol))
    total[npair] += zcol

    @pl.when(step == pl.num_programs(0) - 1)
    def _():
        split_long(total[...], flag_ref[0:1, F_CLOSING : F_CLOSING + 1], state_ref, next_ref)


def split_long(total, flag, long_ref, next_ref):
    long_ref[...] = (total * flag).astype(bf16)
    next_ref[...] = (total * (1.0 - flag)).astype(bf16)


def taken_sum(refs, flags, lane):
    *scans, near = refs
    total = near[...].astype(f32) * flags[0:1, lane + 1 : lane + 2]
    for bit, ref in enumerate(scans):
        total = total + ref[...].astype(f32) * flags[bit : bit + 1, lane : lane + 1]
    return total.astype(bf16)


def unpack_state(state_ref, g, npair, lo, slots):
    pair = state_ref[g].astype(f32)
    z = state_ref[npair].astype(f32)
    za = z[:, DH + g : DH + g + 1]
    zb = z[:, g : g + 1]
    return jnp.where(lo, pair, za), jnp.where(lo, zb, pair)


def unpack_grad_state(state_ref, g, npair, lo, slots):
    pair = state_ref[g].astype(f32)
    z = state_ref[npair].astype(f32)
    za = jnp.where(slots == DH, z[:, DH + g : DH + g + 1], 0.0)
    zb = jnp.where(slots == 0, z[:, g : g + 1], 0.0)
    return jnp.where(lo, pair, za), jnp.where(lo, zb, pair)


def query_kernel(spot_ref, x_ref, wq_ref, vec_ref, cs_ref, q_ref, qf_ref):
    q = (nn(x_ref[...], wq_ref[...]) + vec_ref[R_BQ : R_BQ + 1, :]).astype(bf16)
    q_ref[...] = q
    lo = lane_iota(CHUNK) < DH
    cs = cs_ref[...]
    for g in range(pairs_of(q.shape[1])):
        fa, fb = features(q[:, g * LANES : (g + 1) * LANES].astype(f32), cs, lo)
        qf_ref[:, 2 * g * LANES : (2 * g + 1) * LANES] = fa
        qf_ref[:, (2 * g + 1) * LANES : (2 * g + 2) * LANES] = fb


def mixer_kernel(spot_ref, qf_ref, kf_ref, v_ref, st_ref, en_ref, o_ref, kept_ref, local):
    step = pl.program_id(0)
    first = spot_ref[0] + step * CHUNK
    start, end = st_ref[...], en_ref[...]
    start2 = jnp.concatenate([start, start], axis=1)
    ipos = first + row_iota(CHUNK, CHUNK)
    jpos = first + lane_iota(CHUNK, CHUNK)
    mask = (jpos <= ipos) & (jpos >= start2)
    carried = start < first
    closing = end >= first + CHUNK
    keep = start[CHUNK - 1 : CHUNK, :] < first
    lo = lane_iota(CHUNK) < DH

    @pl.when(step == 0)
    def _():
        local[...] = jnp.zeros_like(local)

    for g in range(pairs_of(v_ref.shape[1])):
        vs = extended(v_ref[:, g * LANES : (g + 1) * LANES], lo)
        for s in range(2):
            h = 2 * g + s
            cols = slice(h * LANES, (h + 1) * LANES)
            qf, kf, v = qf_ref[:, cols], kf_ref[:, cols], vs[s]
            probs = jnp.where(mask, nt(qf, kf), 0.0).astype(bf16)
            held = local[h].astype(bf16)
            kept_ref[0, h] = held
            o_ref[:, cols] = nn(probs, v) + jnp.where(carried, nn(qf, held), 0.0)
            local[h] = jnp.where(keep, local[h], 0.0) + tn(
                jnp.where(closing, kf, jnp.zeros_like(kf)), v
            )


def gelu_and_slope(u):
    z = jnp.abs(u) * (1.0 / math.sqrt(2.0))
    t = 1.0 / (1.0 + 0.3275911 * z)
    p = 0.5 * 1.061405429
    for c in (-1.453152027, 1.421413741, -0.284496736, 0.254829592):
        p = p * t + 0.5 * c
    e = jnp.exp(-0.5 * u * u)
    tail = p * t * e
    gauss = jnp.where(u >= 0.0, 1.0 - tail, tail)
    return u * gauss, gauss + u * e * (1.0 / math.sqrt(2.0 * math.pi))


def token_kernel(
    spot_ref, o0_ref, o1_ref, o2_ref, qf_ref, st_ref, x_ref, go_ref,
    wo_ref, w1_ref, w2_ref, vec_ref, flag_ref, *refs, split, scans,
):
    theirs = refs[:scans]
    (
        out_ref, mixed_ref, first_ref, act_ref, douter_ref, dinner_ref, dbranch_ref, dr1_ref,
        dn_ref, back_ref, near_ref, vgrad_ref, state_ref,
        states, ratio, rden_s, slope, back_s, flow, norm_s, rstd_s, sums,
    ) = refs[scans:]
    step = pl.program_id(0)
    base = spot_ref[0]
    chunk, width = x_ref.shape
    ff = w1_ref.shape[1]
    npair = pairs_of(width)
    lane = lane_iota(chunk)
    lo = lane < DH
    slots = lane_iota(LANES)
    lo_state = slots < DH
    start = st_ref[...]

    @pl.when(step == 0)
    def _():
        state_ref[...] = taken_sum(theirs, flag_ref[...], F_BEFORE)
        for g in range(npair):
            a, b = unpack_state(state_ref, g, npair, lo_state, slots)
            states[2 * g] = a.astype(bf16)
            states[2 * g + 1] = b.astype(bf16)
        back_s[...] = jnp.zeros_like(back_s)
        sums[...] = jnp.zeros_like(sums)

    carried = start < base
    o_refs = (o0_ref, o1_ref, o2_ref)
    for g in range(npair):
        both = []
        for s in range(2):
            h = 2 * g + s
            o_of = o_refs[h // 4]
            local = o_of[:, (h % 4) * LANES : (h % 4 + 1) * LANES]
            far = nn(qf_ref[:, h * LANES : (h + 1) * LANES], states[h])
            both.append(local + jnp.where(carried, far, 0.0))
        numer = jnp.where(lo, both[0], both[1])
        rden = 1.0 / swap_halves(jnp.where(lo, both[1], both[0]))
        cols = slice(g * LANES, (g + 1) * LANES)
        rden_s[:, cols] = rden
        mix = numer * rden
        ratio[:, cols] = mix
        mixed_ref[:, cols] = mix.astype(bf16)

    def row(r):
        return vec_ref[r : r + 1, :]

    def mean(v):
        return jnp.sum(v, axis=-1, keepdims=True) * (1.0 / width)

    def norm(resid):
        cent = resid - mean(resid)
        rstd = lax.rsqrt(mean(cent * cent) + EPS)
        return cent * rstd, rstd

    def norm_back(grad, normed, rstd, gain):
        d_n = grad * gain
        return rstd * (d_n - mean(d_n) - normed * mean(d_n * normed))

    def add_sum(r, v, cols=slice(None)):
        sums[8 * r : 8 * r + 8, cols] += v

    flow[...] = nn(mixed_ref[...], wo_ref[...])
    for at in range(0, chunk, SLICE):
        sl = slice(at, at + SLICE)
        n1, rstd1 = norm(x_ref[sl, :].astype(f32) + flow[sl, :] + row(R_BO))
        norm_s[sl, :] = n1
        rstd_s[sl, :] = jnp.broadcast_to(rstd1, (SLICE, LANES))
        first_ref[sl, :] = (n1 * row(R_G1) + row(R_E1)).astype(bf16)

    part = ff // split

    def inner_of(i):
        flat, off = i * part // width, i * part % width
        bias = vec_ref[R_B1 + flat : R_B1 + flat + 1, off : off + part]
        return nn(first_ref[...], w1_ref[:, i * part : (i + 1) * part]) + bias

    ahead = inner_of(0)
    outer = jnp.zeros((chunk, width), f32)
    last = None
    for i in range(split):
        cols = slice(i * part, (i + 1) * part)
        now = ahead
        if i + 1 < split:
            ahead = inner_of(i + 1)
        if last is not None:
            outer = outer + nn(last, w2_ref[(i - 1) * part : i * part, :])
        act, sl = gelu_and_slope(now)
        last = act.astype(bf16)
        act_ref[:, cols] = last
        slope[:, cols] = sl
    flow[...] = outer + nn(last, w2_ref[(split - 1) * part :, :])

    g2_sum = e2_sum = b2_sum = jnp.zeros((8, width), f32)
    for at in range(0, chunk, SLICE):
        sl = slice(at, at + SLICE)
        n2, rstd2 = norm(first_ref[sl, :].astype(f32) + flow[sl, :] + row(R_B2))
        out_ref[sl, :] = (n2 * row(R_G2) + row(R_E2)).astype(bf16)
        grad = go_ref[sl, :].astype(f32)
        g2_sum = g2_sum + fold_rows(grad * n2)
        e2_sum = e2_sum + fold_rows(grad)
        d_r2 = norm_back(grad, n2, rstd2, row(R_G2))
        b2_sum = b2_sum + fold_rows(d_r2)
        douter_ref[sl, :] = d_r2.astype(bf16)
        dr1_ref[sl, :] = d_r2
    add_sum(V_G2, g2_sum)
    add_sum(V_E2, e2_sum)
    add_sum(V_B2, b2_sum)

    for i in range(split):
        cols = slice(i * part, (i + 1) * part)
        flat = i * part // width
        off = i * part % width
        d_inner = nt(douter_ref[...], w2_ref[cols, :]) * slope[:, cols]
        dinner_ref[:, cols] = d_inner.astype(bf16)
        add_sum(V_B1 + flat, fold_rows(d_inner), slice(off, off + part))
    flow[...] = nt(dinner_ref[...], w1_ref[...])

    g1_sum = e1_sum = bo_sum = jnp.zeros((8, width), f32)
    for at in range(0, chunk, SLICE):
        sl = slice(at, at + SLICE)
        d_first = dr1_ref[sl, :] + flow[sl, :]
        n1 = norm_s[sl, :]
        g1_sum = g1_sum + fold_rows(d_first * n1)
        e1_sum = e1_sum + fold_rows(d_first)
        d_r1 = norm_back(d_first, n1, rstd_s[sl, 0:1], row(R_G1))
        bo_sum = bo_sum + fold_rows(d_r1)
        dr1_ref[sl, :] = d_r1
        dbranch_ref[sl, :] = d_r1.astype(bf16)
    add_sum(V_G1, g1_sum)
    add_sum(V_E1, e1_sum)
    add_sum(V_BO, bo_sum)

    flow[...] = nt(dbranch_ref[...], wo_ref[...])
    opening = start <= base
    zcol = jnp.zeros((LANES, LANES), f32)
    for g in range(npair):
        cols = slice(g * LANES, (g + 1) * LANES)
        dn = flow[:, cols] * rden_s[:, cols]
        prod = dn * ratio[:, cols]
        dda = -jnp.sum(jnp.where(lo, prod, 0.0), axis=1, keepdims=True)
        ddb = -jnp.sum(jnp.where(lo, 0.0, prod), axis=1, keepdims=True)
        hia, hib = dda.astype(bf16).astype(f32), ddb.astype(bf16).astype(f32)
        exa = jnp.where(lane == DH, hia, jnp.where(lane == DH + 1, dda - hia, 0.0))
        exb = jnp.where(lane == 0, hib, jnp.where(lane == 1, ddb - hib, 0.0))
        dna = jnp.where(lo, dn, exa).astype(bf16)
        dnb = jnp.where(lo, exb, dn).astype(bf16)
        ca = slice(2 * g * LANES, (2 * g + 1) * LANES)
        cb = slice((2 * g + 1) * LANES, (2 * g + 2) * LANES)
        dn_ref[:, ca] = dna
        dn_ref[:, cb] = dnb
        zero = jnp.zeros((chunk, LANES), bf16)
        ga = tn(jnp.where(opening, qf_ref[:, ca], zero), dna)
        gb = tn(jnp.where(opening, qf_ref[:, cb], zero), dnb)
        back_s[g] += jnp.where(lo_state, ga, gb)
        za = ga[:, DH : DH + 1] + ga[:, DH + 1 : DH + 2]
        zb = gb[:, 0:1] + gb[:, 1:2]
        zcol = jnp.where(slots == DH + g, za, jnp.where(slots == g, zb, zcol))
    back_s[npair] += zcol

    @pl.when(step == pl.num_programs(0) - 1)
    def _():
        split_long(back_s[...], flag_ref[0:1, F_OPENING : F_OPENING + 1], back_ref, near_ref)
        vgrad_ref[...] = jnp.zeros_like(vgrad_ref)
        for r in range(sums.shape[0] // 8):
            vgrad_ref[r : r + 1, :] = jnp.sum(sums[8 * r : 8 * r + 8, :], axis=0, keepdims=True)


def fold_rows(v):
    return jnp.sum(v.reshape(v.shape[0] // 8, 8, v.shape[1]), axis=0)


def store_pieces(own, value, rows, send_ref, keep_ref, at):
    count = value.shape[0] // rows
    value = value.astype(bf16)
    for bit in range(2):

        @pl.when(own == bit)
        def _():
            for d in range(count):
                ref = keep_ref if d % 2 == bit else send_ref
                ref[d // 2, at : at + rows, :] = value[d * rows : (d + 1) * rows, :]


def store_lines(line, send_ref, keep_ref, at):
    line = line.astype(bf16)
    for m in range(send_ref.shape[0]):
        send_ref[m, at : at + line.shape[0], :] = line
        keep_ref[m, at : at + line.shape[0], :] = line


def query_back_kernel(
    spot_ref, qf_ref, kf_ref, v_ref, dn_ref, q_ref, kept0, kept1, kept2, state_ref,
    st_ref, cs_ref, x_ref, mixed_ref, dbranch_ref, vec_ref,
    dq_ref, send_ref, keep_ref,
    grads, lines,
    *, npair, nchunk, piece,
):
    step = pl.program_id(0)
    base = spot_ref[0]
    keepers = (kept0, kept1, kept2)

    @pl.when(step == 0)
    def _():
        lines[...] = jnp.zeros_like(lines)

    @pl.when(step < nchunk)
    def _():
        lo = lane_iota(CHUNK) < DH
        slots = lane_iota(LANES)
        lo_state = slots < DH
        first = base + step * CHUNK
        start, cs = st_ref[...], cs_ref[...]
        start2 = jnp.concatenate([start, start], axis=1)
        ipos = first + row_iota(CHUNK, CHUNK)
        jpos = first + lane_iota(CHUNK, CHUNK)
        mask = (jpos <= ipos) & (jpos >= start2)
        carried = start < first
        from_far = start[0:1, :] < base
        at = pl.ds(pl.multiple_of(step * CHUNK, CHUNK), CHUNK)
        for g in range(npair):
            pair = slice(g * LANES, (g + 1) * LANES)
            vs = extended(v_ref[:, pair], lo)
            far = unpack_state(state_ref, g, npair, lo_state, slots)
            dns = [dn_ref[:, (2 * g + s) * LANES : (2 * g + s + 1) * LANES] for s in range(2)]
            d_probs = [nt(dns[s], vs[s]) for s in range(2)]
            d_probs = [jnp.where(mask, d, 0.0).astype(bf16) for d in d_probs]
            held = [
                (keepers[h // 4][0, h % 4].astype(f32) + jnp.where(from_far, far[h - 2 * g], 0.0)).astype(bf16)
                for h in (2 * g, 2 * g + 1)
            ]
            d_qf = [
                nn(d_probs[s], kf_ref[:, (2 * g + s) * LANES : (2 * g + s + 1) * LANES])
                + jnp.where(carried, nt(dns[s], held[s]), 0.0)
                for s in range(2)
            ]
            turned = [d * cs for d in d_qf]
            turned = [t + swap_halves(t) for t in turned]
            value = jnp.where(lo, turned[0], turned[1]) * sigmoid(q_ref[:, pair].astype(f32))
            lines[0:8, pair] += fold_rows(value)
            value = value.astype(bf16)
            dq_ref[:, pair] = value
            grads[at, pair] = value

    @pl.when(step == nchunk)
    def _():
        own = spot_ref[2]
        store_pieces(own, tn(x_ref[...], grads[...]), piece, send_ref, keep_ref, 0)
        store_pieces(own, tn(mixed_ref[...], dbranch_ref[...]), piece, send_ref, keep_ref, piece)
        total = jnp.sum(lines[...], axis=0, keepdims=True)
        vec = jnp.where(row_iota(VEC_ROWS, total.shape[1]) == VEC_ROWS - 1, total, vec_ref[...])
        store_lines(vec, send_ref, keep_ref, 2 * piece)


def value_back_kernel(
    spot_ref, qf_ref, kf_ref, v_ref, dn_ref, k_ref, back_ref, st_ref, en_ref, cs_ref, x_ref,
    dk_ref, dv_ref, send_ref, keep_ref,
    onward_state, grads, lines,
    *, pair0, npair, nchunk, piece, rows,
):
    base = spot_ref[0]
    wide = v_ref.shape[1]

    @pl.when(pl.program_id(0) == 0)
    def _():
        onward_state[...] = jnp.zeros_like(onward_state)
        lines[...] = jnp.zeros_like(lines)

    @pl.when(pl.program_id(0) < nchunk)
    def _():
        lo = lane_iota(CHUNK) < DH
        slots = lane_iota(LANES)
        lo_state = slots < DH
        step = nchunk - 1 - pl.program_id(0)
        first = base + step * CHUNK
        start, end, cs = st_ref[...], en_ref[...], cs_ref[...]
        end2 = jnp.concatenate([end, end], axis=1)
        jpos = first + row_iota(CHUNK, CHUNK)
        ipos = first + lane_iota(CHUNK, CHUNK)
        mask = (jpos <= ipos) & (ipos < end2)
        onward = end > first + CHUNK
        opening = start <= first
        to_far = end[CHUNK - 1 : CHUNK, :] > base + rows
        keep = end[0:1, :] > first + CHUNK
        at = pl.ds(pl.multiple_of(step * CHUNK, CHUNK), CHUNK)
        zero = jnp.zeros((CHUNK, LANES), bf16)
        two = range(2)
        for g in range(pairs_of(wide)):
            pair = slice(g * LANES, (g + 1) * LANES)
            cols = [slice((2 * g + s) * LANES, (2 * g + s + 1) * LANES) for s in two]
            vs = extended(v_ref[:, pair], lo)
            far = unpack_grad_state(back_ref, pair0 + g, npair, lo_state, slots)
            qf, kf = [qf_ref[:, c] for c in cols], [kf_ref[:, c] for c in cols]
            dn = [dn_ref[:, c] for c in cols]
            probs = [nt(kf[s], qf[s]) for s in two]
            d_probs = [nt(vs[s], dn[s]) for s in two]
            probs = [jnp.where(mask, p, 0.0).astype(bf16) for p in probs]
            d_probs = [jnp.where(mask, p, 0.0).astype(bf16) for p in d_probs]
            ahead = [onward_state[2 * g + s] for s in two]
            ahead16 = [(ahead[s] + jnp.where(to_far, far[s], 0.0)).astype(bf16) for s in two]
            more = [tn(jnp.where(opening, qf[s], zero), dn[s]) for s in two]
            d_kf = [nn(d_probs[s], qf[s]) + jnp.where(onward, nt(vs[s], ahead16[s]), 0.0) for s in two]
            d_v = [nn(probs[s], dn[s]) + jnp.where(onward, nn(kf[s], ahead16[s]), 0.0) for s in two]
            for s in two:
                onward_state[2 * g + s] = jnp.where(keep, ahead[s], 0.0) + more[s]
            turned = [d * cs for d in d_kf]
            turned = [t + swap_halves(t) for t in turned]
            both = (
                (jnp.where(lo, turned[0], turned[1]) * sigmoid(k_ref[:, pair].astype(f32)), dk_ref),
                (jnp.where(lo, d_v[0], d_v[1]), dv_ref),
            )
            for n, (value, ref) in enumerate(both):
                spread = slice(n * wide + g * LANES, n * wide + (g + 1) * LANES)
                lines[0:8, spread] += fold_rows(value)
                value = value.astype(bf16)
                ref[:, pair] = value
                grads[at, spread] = value

    @pl.when(pl.program_id(0) == nchunk)
    def _():
        store_pieces(spot_ref[2], tn(x_ref[...], grads[...]), piece, send_ref, keep_ref, 0)
        total = jnp.sum(lines[...], axis=0, keepdims=True)
        store_lines(jnp.broadcast_to(total, lines.shape), send_ref, keep_ref, piece)


def outer_grad_kernel(spot_ref, act_ref, d_ref, send_ref, keep_ref, *, piece):
    store_pieces(spot_ref[2], tn(act_ref[...], d_ref[...]), piece, send_ref, keep_ref, 0)


def inner_grad_kernel(spot_ref, first_ref, dinner_ref, send_ref, keep_ref, *, piece, parts):
    for i in range(parts):

        @pl.when(pl.program_id(0) == i)
        def _():
            value = tn(first_ref[...], dinner_ref[...])
            store_pieces(spot_ref[2], value, piece, send_ref, keep_ref, i * piece)


def tokens_grad_kernel(spot_ref, dr1_ref, q_ref, k0, k1, v0, v1, wq_ref, wk_ref, wv_ref, out_ref):
    total = dr1_ref[...] + nt(q_ref[...], wq_ref[...])
    for refs, w in (((k0, k1), wk_ref), ((v0, v1), wv_ref)):
        total = total + nt(jnp.concatenate([r[...] for r in refs], axis=1), w[...])
    out_ref[...] = total.astype(bf16)


def taken_kernel(spot_ref, *refs, lane):
    *theirs, flag_ref, out_ref = refs
    out_ref[...] = taken_sum(theirs, flag_ref[...], lane)


def exchange(x, mask, count):
    return lax.ppermute(x, AXES, [(i, i ^ mask) for i in range(count)])


def flip(x, bit, count):
    return exchange(x, 1 << bit, count)


class Halving:

    def __init__(self, send, keep, count, order):
        self.count = count
        self.left = list(range(count.bit_length() - 2, 0, -1))
        self.order = list(order)
        self.tail = send.shape[1:]
        self.keep = keep
        self.recv = flip(send, 0, count)

    def advance(self):
        self.bit = self.order.pop(0)
        axis = self.left.index(self.bit)
        self.a, self.b = 1 << axis, 1 << (len(self.left) - 1 - axis)
        self.left.remove(self.bit)
        view = (self.a, 2, self.b, *self.tail)
        full = jax.ShapeDtypeStruct((self.a, self.b, *self.tail), bf16)
        return self.keep.reshape(view), self.recv.reshape(view), full

    def specs(self, steps):
        keep, recv, full = self.advance()
        bit, rank = self.bit, len(self.tail)
        used = min(self.a * self.b, 4, steps)
        while used & (used - 1):
            used -= 1
        ca = min(self.a, used)
        cb = used // ca
        shape = (self.a // ca, None, self.b // cb, *self.tail)

        def index(i, spot, other):
            i = jnp.minimum(i, used - 1)
            own = spot[2 + bit]
            return (i // cb, 1 - own if other else own, i % cb) + (0,) * rank

        def out_index(i, spot):
            i = jnp.minimum(i, used - 1)
            return (i // cb, i % cb) + (0,) * rank

        ins = [pl.BlockSpec(shape, functools.partial(index, other=o)) for o in (True, True, False, False)]
        out = pl.BlockSpec((shape[0], shape[2], *self.tail), out_index)
        return ins, [keep, recv, keep, recv], [out, out], [full, full]

    def take(self, send, keep):
        self.keep = keep
        self.recv = flip(send, self.bit, self.count)

    def result(self):
        return self.keep.reshape(self.tail).astype(f32) + self.recv.reshape(self.tail).astype(f32)


def add_step(spot, sums, after=()):
    for one in sums:
        assert one.order
    views = [one.advance() for one in sums]

    def body(spot_ref, *refs):
        ins, outs = refs[: 2 * len(sums)], refs[2 * len(sums) + len(after) :]
        for n, one in enumerate(sums):
            keep, recv = ins[2 * n : 2 * n + 2]
            own = spot_ref[2 + one.bit]
            for half, ref in ((1 - own, outs[2 * n]), (own, outs[2 * n + 1])):
                ref[...] = (keep[:, half].astype(f32) + recv[:, half].astype(f32)).astype(bf16)

    vmem = pl.BlockSpec(memory_space=pltpu.VMEM)
    out = pl.pallas_call(
        body,
        in_specs=[pl.BlockSpec(memory_space=pltpu.SMEM)]
        + [vmem] * (2 * len(sums))
        + [pl.BlockSpec(memory_space=pl.ANY)] * len(after),
        out_specs=[vmem] * (2 * len(sums)),
        out_shape=[v[2] for v in views for _ in range(2)],
        compiler_params=pltpu.CompilerParams(vmem_limit_bytes=8 * MIB),
        cost_estimate=pl.CostEstimate(flops=int(1e5), bytes_accessed=int(1e5), transcendentals=0),
    )(spot, *[x for v in views for x in v[:2]], *after)
    for n, one in enumerate(sums):
        one.take(*out[2 * n : 2 * n + 2])
    return out[-1]


def block(shape, index):
    return pl.BlockSpec(shape, lambda i, spot: index(i))


def whole(shape):
    return pl.BlockSpec(shape, lambda i, spot: (0,) * len(shape), pipeline_mode=pl.Buffered(1))


SMEM = pl.BlockSpec(memory_space=pltpu.SMEM)


def call(kernel, grid, in_specs, outs, out_specs, scratch, spot, args, micros, rides=(), after=(), thread=(), vmem=VMEM):
    nin, nout, nafter, nthread = len(in_specs), len(outs), len(after), len(thread)
    in_specs, out_specs = list(in_specs), list(out_specs)
    out_shape = [jax.ShapeDtypeStruct(s, d) for s, d in outs]
    args = list(args)
    counts = []
    for ride in rides:
        i_specs, i_args, o_specs, o_shape = ride.specs(grid)
        in_specs += i_specs
        args += i_args
        out_specs += o_specs
        out_shape += o_shape
        counts.append(len(o_specs))
    nride = sum(counts)
    hbm = pl.BlockSpec(memory_space=pl.ANY)
    in_specs += [hbm] * (nafter + nthread)
    out_specs += [hbm] * nthread
    out_shape += [jax.ShapeDtypeStruct(t.shape, t.dtype) for t in thread]
    first_thread = 1 + nin + 2 * nride + nafter
    args += list(after) + list(thread)

    def body(spot_ref, *refs):
        ins = refs[:nin]
        ride_ins = refs[nin : nin + 2 * nride]
        rest = refs[nin + 2 * nride + nafter + nthread :]
        host_outs = rest[:nout]
        ride_outs = rest[nout : nout + nride]
        held = rest[nout + nride + nthread :]
        for n in range(nride):
            a, b = ride_ins[2 * n : 2 * n + 2]
            ride_outs[n][...] = (a[...].astype(f32) + b[...].astype(f32)).astype(bf16)
        kernel(spot_ref, *ins, *host_outs, *held)

    out = pl.pallas_call(
        body,
        grid_spec=pltpu.PrefetchScalarGridSpec(
            num_scalar_prefetch=1,
            grid=(grid,),
            in_specs=in_specs,
            out_specs=out_specs,
            scratch_shapes=scratch,
        ),
        out_shape=out_shape,
        input_output_aliases={first_thread + n: nout + nride + n for n in range(nthread)},
        compiler_params=pltpu.CompilerParams(
            dimension_semantics=("arbitrary",), vmem_limit_bytes=vmem * MIB
        ),
        cost_estimate=pl.CostEstimate(flops=int(COST * 1e9 * micros), bytes_accessed=int(1e4), transcendentals=0),
    )(spot, *args)
    at = nout
    for ride, n in zip(rides, counts):
        ride.take(*out[at : at + n])
        at += n
    return out[:nout] + out[at:]


def per_device(
    tokens, out_grad, doc_lengths, w_query, b_query, w_key, b_key, w_value, b_value, w_output, b_output,
    w_inner, b_inner, w_outer, b_outer, gain_first, shift_first, gain_second, shift_second,
):
    rows, width = tokens.shape
    ff = w_inner.shape[1]
    count = lax.axis_size("wide") * lax.axis_size("narrow")
    place = lax.axis_index("wide") * lax.axis_size("narrow") + lax.axis_index("narrow")
    place = place.astype(jnp.int32)
    nchunk = rows // CHUNK
    npair = width // LANES
    heads = 2 * npair
    feat = heads * LANES
    nbits = count.bit_length() - 1
    half = count // 2
    parts = ff // width
    spot = jnp.stack([place * rows, place] + [(place >> b) & 1 for b in range(nbits)])
    at = lambda i: (i, 0)
    tile = block((CHUNK, width), at)
    ftile = block((CHUNK, feat), at)
    col = block((CHUNK, LANES), at)
    square = whole((width, width))
    nvec = R_B1 + parts
    vspec = whole((nvec, width))
    packed = (npair + 1, LANES, LANES)
    pspec = whole(packed)
    fspec = whole((8, LANES))
    fixed = lambda shape: pl.BlockSpec(shape, lambda i, spot: (0,) * len(shape))
    up = list(range(1, nbits))
    swapped = up[:2][::-1] + up[2:]

    lines = (b_query, b_key, b_value, b_output, gain_first, shift_first, b_outer, gain_second, shift_second)
    k, v, kf, cs, st, en, total, near, flags, vecs = call(
        functools.partial(key_kernel, rows=rows),
        nchunk,
        [SMEM, tile, square, square] + [whole((width,))] * 9 + [whole((ff,))],
        [
            ((rows, width), bf16), ((rows, width), bf16), ((rows, feat), bf16),
            ((rows, LANES), f32), ((rows, LANES), jnp.int32), ((rows, LANES), jnp.int32), (packed, bf16), (packed, bf16),
            ((8, LANES), f32), ((nvec, width), f32),
        ],
        [tile, tile, ftile, col, col, col, fixed(packed), fixed(packed), fixed((8, LANES)), fixed((nvec, width))],
        [pltpu.VMEM(packed, f32)],
        spot,
        (doc_lengths, tokens, w_key, w_value, *lines, b_inner),
        12,
    )

    def run_query(sent):
        return call(
            query_kernel,
            nchunk,
            [tile, square, vspec, col],
            [((rows, width), bf16), ((rows, feat), bf16)],
            [tile, ftile],
            [],
            spot,
            (tokens, w_query, vecs, cs),
            4,
            after=(sent,),
            vmem=FILL,
        )

    groups = 3
    gh = heads // groups
    locals_, kepts = [], []

    def run_mixer(sent):
        n = len(kepts)
        fcol = block((CHUNK, gh * LANES), lambda i: (i, n))
        vcol = block((CHUNK, gh * DH), lambda i: (i, n))
        o, kept = call(
            mixer_kernel,
            nchunk,
            [fcol, fcol, vcol, col, col],
            [((rows, gh * LANES), f32), ((nchunk, gh, LANES, LANES), bf16)],
            [block((CHUNK, gh * LANES), at), block((1, gh, LANES, LANES), lambda i: (i, 0, 0, 0))],
            [pltpu.VMEM((gh, LANES, LANES), f32)],
            spot,
            (qf, kf, v, st, en),
            4,
            after=(sent,),
            vmem=FILL,
        )
        locals_.append(o)
        kepts.append(kept)
        return (o,)

    def joined(a, b, after=()):
        a, b, *after = lax.optimization_barrier((a, b, *after))
        return (a.astype(f32) + b.astype(f32)).astype(bf16)

    before = []
    done = ()
    for bit in range(nbits):
        before.append(flip(total, bit, count))
        if bit == 1:
            q, qf = run_query(total)
            done = (q,)
            from_last = lax.ppermute(near, AXES, [(i, i + 1) for i in range(count - 1)])
        elif bit >= 2 and len(kepts) < groups:
            done = run_mixer(total)
        if bit < nbits - 1:
            total = joined(total, before[-1], done)
    while len(kepts) < groups:
        run_mixer(total)
    before.append(from_last)

    ftile_ff = block((CHUNK, ff), at)
    otile = block((CHUNK, gh * LANES), at)
    (result, mixed, first, act, d_outer, d_inner, d_branch, d_r1, dn, back, near, vgrad, state_in) = call(
        functools.partial(token_kernel, split=12, scans=nbits + 1),
        nchunk,
        [
            otile, otile, otile, ftile, col, tile, tile,
            square, whole((width, ff)), whole((ff, width)), vspec, fspec,
        ] + [pspec] * (nbits + 1),
        [
            ((rows, width), bf16), ((rows, width), bf16), ((rows, width), bf16), ((rows, ff), bf16),
            ((rows, width), bf16), ((rows, ff), bf16), ((rows, width), bf16), ((rows, width), f32),
            ((rows, feat), bf16), (packed, bf16), (packed, bf16), ((VEC_ROWS, width), f32), (packed, bf16),
        ],
        [
            tile, tile, tile, ftile_ff, tile, ftile_ff, tile, tile, ftile,
            fixed(packed), fixed(packed), fixed((VEC_ROWS, width)), fixed(packed),
        ],
        [
            pltpu.VMEM((heads, LANES, LANES), bf16),
            pltpu.VMEM((CHUNK, width), f32),
            pltpu.VMEM((CHUNK, width), f32),
            pltpu.VMEM((CHUNK, ff), f32),
            pltpu.VMEM(packed, f32),
            pltpu.VMEM((CHUNK, width), f32),
            pltpu.VMEM((CHUNK, width), f32),
            pltpu.VMEM((CHUNK, LANES), f32),
            pltpu.VMEM((8 * (V_B1 + parts), width), f32),
        ],
        spot,
        (*locals_, qf, st, tokens, out_grad, w_output, w_inner, w_outer, vecs, flags, *before),
        50,
    )

    piece_o = ff // count
    piece = width // count
    per_step = width // piece_o
    sums = {}

    def run_outer(after):
        spec = block((per_step // 2, piece_o, width), lambda i: (i, 0, 0))
        send, keep = call(
            functools.partial(outer_grad_kernel, piece=piece_o),
            parts,
            [block((rows, width), lambda i: (0, i)), whole((rows, width))],
            [((half, piece_o, width), bf16)] * 2,
            [spec, spec],
            [],
            spot,
            (act, d_outer),
            9,
            after=after,
            vmem=FILL,
        )
        sums["outer"] = Halving(send, keep, count, up)
        return (keep,)

    def run_inner(after, lead, order, rides=()):
        n = parts // 2
        full = fixed((half, n * piece, width))
        send, keep = call(
            functools.partial(inner_grad_kernel, piece=piece, parts=n),
            n,
            [whole((rows, width)), block((rows, width), lambda i: (0, lead * n + i))],
            [((half, n * piece, width), bf16)] * 2,
            [full, full],
            [],
            spot,
            (first, d_inner),
            5,
            rides=rides,
            after=after,
            vmem=FILL,
        )
        sums[f"inner{lead}"] = Halving(send, keep, count, order)
        return (keep,)

    def run_query_back(after, rides=()):
        last = lambda i: jnp.minimum(i, nchunk - 1)
        ltile = block((CHUNK, width), lambda i: (last(i), 0))
        lf = block((CHUNK, feat), lambda i: (last(i), 0))
        lcol = block((CHUNK, LANES), lambda i: (last(i), 0))
        kept = block((1, gh, LANES, LANES), lambda i: (last(i), 0, 0, 0))
        depth = 2 * piece + VEC_ROWS
        full = fixed((half, depth, width))
        wide = whole((rows, width))
        dq, send, keep = call(
            functools.partial(query_back_kernel, npair=npair, nchunk=nchunk, piece=piece),
            nchunk + 1,
            [lf, lf, ltile, lf, ltile, kept, kept, kept, pspec, lcol, lcol, wide, wide, wide, whole((VEC_ROWS, width))],
            [((rows, width), bf16)] + [((half, depth, width), bf16)] * 2,
            [ltile, full, full],
            [pltpu.VMEM((rows, width), bf16), pltpu.VMEM((8, width), f32)],
            spot,
            (qf, kf, v, dn, q, *kepts, state_in, st, cs, tokens, mixed, d_branch, vgrad),
            15,
            rides=rides,
            after=after,
            vmem=FILL,
        )
        sums["query"] = Halving(send, keep, count, up)
        return dq

    after_ = []
    done = ()
    for bit in range(nbits):
        after_.append(flip(back, bit, count))
        sent = (back, *done)
        if bit == 2:
            from_next = lax.ppermute(near, AXES, [(i + 1, i) for i in range(count - 1)])
        if bit == 1:
            done = run_outer(sent)
        elif bit == 2:
            done = run_inner(sent, 0, swapped)
        elif bit == 3:
            done = (add_step(spot, [sums["outer"]], sent),)
            done = run_inner((*sent, *done), 1, up)
        elif bit == 4:
            done = (add_step(spot, [sums["inner0"]], sent),)
            dq = run_query_back((*sent, *done))
            done = (dq,)
        if bit < nbits - 1:
            back = joined(back, after_[-1], done)
    after_.append(from_next)
    (back_in,) = call(
        functools.partial(taken_kernel, lane=F_AFTER),
        1,
        [pspec] * (nbits + 1) + [fspec],
        [(packed, bf16)],
        [fixed(packed)],
        [],
        spot,
        (*after_, flags),
        1,
        after=done,
        vmem=4,
    )

    halves = 2
    hp = npair // halves
    hw = hp * LANES
    dks, dvs = [], []

    def run_value_back(n, order, rides=(), after=()):
        index = lambda i: nchunk - 1 - jnp.minimum(i, nchunk - 1)
        fcol = block((CHUNK, 2 * hw), lambda i: (index(i), n))
        vcol = block((CHUNK, hw), lambda i: (index(i), n))
        bcol = block((CHUNK, LANES), lambda i: (index(i), 0))
        grad = block((CHUNK, hw), lambda i: (index(i), 0))
        full = fixed((half, piece + 8, 2 * hw))
        dk, dv, send, keep = call(
            functools.partial(
                value_back_kernel, pair0=n * hp, npair=npair, nchunk=nchunk, piece=piece, rows=rows
            ),
            nchunk + 1,
            [fcol, fcol, vcol, fcol, vcol, pspec, bcol, bcol, bcol, whole((rows, width))],
            [((rows, hw), bf16)] * 2 + [((half, piece + 8, 2 * hw), bf16)] * 2,
            [grad, grad, full, full],
            [
                pltpu.VMEM((2 * hp, LANES, LANES), f32),
                pltpu.VMEM((rows, 2 * hw), bf16),
                pltpu.VMEM((8, 2 * hw), f32),
            ],
            spot,
            (qf, kf, v, dn, k, back_in, st, en, cs, tokens),
            10,
            rides=rides,
            after=after,
            vmem=FILL,
        )
        dks.append(dk)
        dvs.append(dv)
        sums[f"value{n}"] = Halving(send, keep, count, order)

    done = (add_step(spot, [sums["inner1"]], (back_in,)),)
    run_value_back(0, swapped, after=done)
    done = (add_step(spot, [sums["query"], sums["outer"]], (dks[0],)),)
    run_value_back(1, up, after=done)
    done = (add_step(spot, [sums["value0"], sums["inner0"], sums["inner1"]], (dks[1],)),)
    done = (add_step(spot, [sums["value1"]], done),)

    (grad_tokens,) = call(
        tokens_grad_kernel,
        nchunk,
        [tile, tile] + [block((CHUNK, hw), at)] * 4 + [square] * 3,
        [((rows, width), bf16)],
        [tile],
        [],
        spot,
        (d_r1, dq, *dks, *dvs, w_query, w_key, w_value),
        8,
        after=done,
        vmem=FILL,
    )
    done = (grad_tokens,)
    while True:
        left = [s for s in sums.values() if s.order]
        if not left:
            break
        done = (add_step(spot, left, done),)

    g_outer = sums["outer"].result()
    inner0, inner1 = sums["inner0"].result(), sums["inner1"].result()
    cuts = [inner0[i * piece : (i + 1) * piece] for i in range(parts // 2)]
    cuts += [inner1[i * piece : (i + 1) * piece] for i in range(parts // 2)]
    g_inner = jnp.concatenate(cuts, axis=1)
    query = sums["query"].result()
    g_query, g_output, vec = query[:piece], query[piece : 2 * piece], query[2 * piece :]
    kv = [sums[f"value{n}"].result() for n in range(halves)]
    g_kv = [jnp.concatenate([s[:piece, m * hw : (m + 1) * hw] for s in kv], axis=1) for m in range(2)]
    b_kv = [jnp.concatenate([s[piece, m * hw : (m + 1) * hw] for s in kv]) for m in range(2)]

    def share(line):
        size = line.shape[0] // count
        return lax.dynamic_slice(line, (place * size,), (size,))

    return (
        result,
        grad_tokens,
        g_query,
        share(vec[VEC_ROWS - 1]),
        g_kv[0],
        share(b_kv[0]),
        g_kv[1],
        share(b_kv[1]),
        g_output,
        share(vec[V_BO]),
        g_inner,
        share(vec[V_B1 : V_B1 + parts].reshape(-1)),
        g_outer,
        share(vec[V_B2]),
        share(vec[V_G1]),
        share(vec[V_E1]),
        share(vec[V_G2]),
        share(vec[V_E2]),
    )


def solution(mesh):
    split = P(AXES, None)
    line = P(AXES)
    return jax.shard_map(
        per_device,
        mesh=mesh,
        in_specs=(split, split) + (P(),) * 17,
        out_specs=(split, split) + (split, line) * 6 + (line,) * 4,
        check_vma=False,
    )
```

profile of v0, /device:TPU:0, one launch (start us, length us, event | category | flops | bytes accessed | tf_op | source)
XLA Modules:
  0.0 302.5 jit_solution(9112929983220513461)
XLA Ops:
  1.3 12.2 %shard_map.322 = (bf16[1024,768]{1,0:T(8,128)(2,1)}, bf16[1024,768]{1,0:T(8,128)(2,1)}, bf16[1024,1536]{1,0:T(8,128)(2,1)}, f32[1024,128]{1,0:T(8,128)}, s32[102...) custom-call(s32[7]{0:T(128)} %stack.31.spot_ref, ...), custom_call_target="tpu_custom_call" | custom-call | flops 120000004096 | bytes 10000 | tf_op jit(solution)/shard_map/pallas_call | solution.py:758
  21.9 4.1 %shard_map.323 = (bf16[1024,768]{1,0:T(8,128)(2,1)S(1)}, bf16[1024,1536]{1,0:T(8,128)(2,1)S(1)}) custom-call(s32[7]{0:T(128)S(1)} %copy-done.13, bf16[1024,768]{1,0:T(8,128)(2,1)S(1)} %copy-done.15, bf16[768,768]{1,0:T(8,128)(2,1)S(1)} %copy-done.17, f32[13,768]{1,0:T(8,128)S(1)} %copy-done.62, f32[1024,128]{1,0:T(8,128)S(1)} %copy-done.52, ...), custom_call_target="tpu_custom_call" | custom-call | flops 40000000000 | bytes 10000 | tf_op jit(solution)/shard_map/pallas_call | solution.py:758
  26.2 3.7 %collective-permute-start.2 = (bf16[7,128,128]{2,1,0:T(8,128)(2,1)S(1)}, bf16[7,128,128]{2,1,0:T(8,128)(2,1)S(1)}, u32[]{:S(2)}, u32[]{:S(2)}) collective-permute-start(bf16[7,128,128]{2,1,0:T(8,128)(2,1)S(1)} %add_convert_fusion.6.refs_5_), channel_id=1, source_target_pairs={{0,4},{1,5},{2,6},{3,7},{4,0},{5,1},{6,2},{7,3},{8,12},{9,13},{10,... | collective-permute-start | bytes 688136 | tf_op jit(solution)/shard_map/ppermute | solution.py:628
  30.0 4.1 %shard_map.324 = (f32[1024,512]{1,0:T(8,128)S(1)}, bf16[4,4,128,128]{3,2,1,0:T(8,128)(2,1)S(1)}) custom-call(s32[7]{0:T(128)S(1)} %copy-done.13, bf16[1024,1536]{1,0:T(8,128)(2,1)S(1)} %get-tuple-element.135.refs_0_.refs_3_, bf16[1024,1536]{1,0:T(8,128)(2,1)S(1)} %copy-done.26, bf16[1024,768]{1,0:T(8,128)(2,1)S(1)} %copy-done.32, ...), custom_call_target="tpu_custom_call" | custom-call | flops 40000000000 | bytes 10000 | tf_op jit(solution)/shard_map/pallas_call | solution.py:758
  38.7 4.1 %shard_map.325 = (f32[1024,512]{1,0:T(8,128)S(1)}, bf16[4,4,128,128]{3,2,1,0:T(8,128)(2,1)S(1)}) custom-call(s32[7]{0:T(128)S(1)} %copy-done.13, bf16[1024,1536]{1,0:T(8,128)(2,1)S(1)} %get-tuple-element.135.refs_0_.refs_3_, bf16[1024,1536]{1,0:T(8,128)(2,1)S(1)} %copy-done.26, bf16[1024,768]{1,0:T(8,128)(2,1)S(1)} %copy-done.32, ...), custom_call_target="tpu_custom_call" | custom-call | flops 40000000000 | bytes 10000 | tf_op jit(solution)/shard_map/pallas_call | solution.py:758
  46.7 4.1 %shard_map.326 = (f32[1024,512]{1,0:T(8,128)S(1)}, bf16[4,4,128,128]{3,2,1,0:T(8,128)(2,1)S(1)}) custom-call(s32[7]{0:T(128)S(1)} %copy-done.13, bf16[1024,1536]{1,0:T(8,128)(2,1)S(1)} %get-tuple-element.135.refs_0_.refs_3_, bf16[1024,1536]{1,0:T(8,128)(2,1)S(1)} %copy-done.26, bf16[1024,768]{1,0:T(8,128)(2,1)S(1)} %copy-done.32, ...), custom_call_target="tpu_custom_call" | custom-call | flops 40000000000 | bytes 10000 | tf_op jit(solution)/shard_map/pallas_call | solution.py:758
  52.1 3.8 %collective-permute-done.4.refs_16_ = bf16[7,128,128]{2,1,0:T(8,128)(2,1)S(1)} collective-permute-done((bf16[7,128,128]{2,1,0:T(8,128)(2,1)S(1)}, bf16[7,128,128]{2,1,0:T(8,128)(2,1)S(1)}, u32[]{:S(2)}, u32[]{:S(2)}) %collective-permute-start.4) | collective-permute-done | bytes 229408 | tf_op jit(solution)/shard_map/ppermute | solution.py:628
  56.6 51.9 %shard_map.327 = (bf16[1024,768]{1,0:T(8,128)(2,1)}, bf16[1024,768]{1,0:T(8,128)(2,1)}, bf16[1024,768]{1,0:T(8,128)(2,1)}, bf16[1024,3072]{1,0:T(8,128)(2,1)}, b...) custom-call(s32[7]{0:T(128)} %stack.31.spot_ref, ...), custom_call_target="tpu_custom_call" | custom-call | flops 499999997952 | bytes 10000 | tf_op jit(solution)/shard_map/pallas_call | solution.py:758
  117.9 7.5 %shard_map.328 = (bf16[16,96,768]{2,1,0:T(8,128)(2,1)S(1)}, bf16[16,96,768]{2,1,0:T(8,128)(2,1)S(1)}) custom-call(s32[7]{0:T(128)S(1)} %copy-done.14, bf16[1024,3072]{1,0:T(8,128)(2,1)S(1)} %copy-done.37, bf16[1024,768]{1,0:T(8,128)(2,1)S(1)} %copy-done.56, bf16[7,128,128]{2,1,0:T(8,128)(2,1)S(1)} %add_convert_fusion.3.refs_2_), custom_call_target="tpu_custom_call" | custom-call | flops 89999998976 | bytes 10000 | tf_op jit(solution)/shard_map/pallas_call | solution.py:758
  129.0 3.9 %shard_map.329 = (bf16[16,48,768]{2,1,0:T(8,128)(2,1)S(1)}, bf16[16,48,768]{2,1,0:T(8,128)(2,1)S(1)}) custom-call(s32[7]{0:T(128)S(1)} %copy-done.14, bf16[1024,768]{1,0:T(8,128)(2,1)S(1)} %copy-done.38, bf16[1024,3072]{1,0:T(8,128)(2,1)S(1)} %copy-done.25, bf16[7,128,128]{2,1,0:T(8,128)(2,1)S(1)} %add_convert_fusion.2.refs_2_, ...), custom_call_target="tpu_custom_call" | custom-call | flops 49999998976 | bytes 10000 | tf_op jit(solution)/shard_map/pallas_call | solution.py:758
  136.5 4.9 %shard_map.331 = (bf16[16,48,768]{2,1,0:T(8,128)(2,1)}, bf16[16,48,768]{2,1,0:T(8,128)(2,1)S(1)}) custom-call(s32[7]{0:T(128)S(1)} %copy-done.14, bf16[1024,768]{1,0:T(8,128)(2,1)S(1)} %copy-done.38, bf16[1024,3072]{1,0:T(8,128)(2,1)S(1)} %copy-done.25, bf16[7,128,128]{2,1,0:T(8,128)(2,1)S(1)} %add_convert_fusion.1.refs_2_, ...), custom_call_target="tpu_custom_call" | custom-call | flops 49999998976 | bytes 10000 | tf_op jit(solution)/shard_map/pallas_call | solution.py:758
  149.2 14.1 %shard_map.333 = (bf16[1024,768]{1,0:T(8,128)(2,1)S(1)}, bf16[16,64,768]{2,1,0:T(8,128)(2,1)S(1)}, bf16[16,64,768]{2,1,0:T(8,128)(2,1)S(1)}) custom-call(s32[7]{0:T(128)S(1)} %copy-done.14, bf16[1024,1536]{1,0:T(8,128)(2,1)} %copy-done.27, bf16[1024,1536]{1,0:T(8,128)(2,1)} %get-tuple-element.136.refs_1_, bf16[1024,768]{1,0:T(8,128)(2,1)S(1)} %copy-done.33, ...), custom_call_target="tpu_custom_call" | custom-call | flops 149999992832 | bytes 10000 | tf_op jit(solution)/shard_map/pallas_call | solution.py:758
  170.7 10.3 %shard_map.336 = (bf16[1024,384]{1,0:T(8,128)(2,1)S(1)}, bf16[1024,384]{1,0:T(8,128)(2,1)S(1)}, bf16[16,32,768]{2,1,0:T(8,128)(2,1)}, bf16[16,32,768]{2,1,0:T(8,128)(2,1)S(1)}) custom-call(s32[7]{0:T(128)S(1)} %copy-done.14, bf16[1024,1536]{1,0:T(8,128)(2,1)S(1)} %copy-done.28, bf16[1024,1536]{1,0:T(8,128)(2,1)} %get-tuple-element.136.refs_1_, ...), custom_call_target="tpu_custom_call" | custom-call | flops 99999997952 | bytes 10000 | tf_op jit(solution)/shard_map/pallas_call | solution.py:758
  181.4 10.7 %collective-permute-done.16 = bf16[8,1,96,768]{3,2,1,0:T(8,128)(2,1)S(1)} collective-permute-done((bf16[8,1,96,768]{3,2,1,0:T(8,128)(2,1)}, bf16[8,1,96,768]{3,2,1,0:T(8,128)(2,1)S(1)}, u32[]{:S(2)}, u32[]{:S(2)}) %collective-permute-start.16) | collective-permute-done | bytes 1179680 | tf_op jit(solution)/shard_map/ppermute | solution.py:628
  194.3 9.6 %shard_map.338 = (bf16[1024,384]{1,0:T(8,128)(2,1)S(1)}, bf16[1024,384]{1,0:T(8,128)(2,1)S(1)}, bf16[16,32,768]{2,1,0:T(8,128)(2,1)S(1)}, bf16[16,32,768]{2,1,0:T(8,128)(2,1)S(1)}) custom-call(s32[7]{0:T(128)S(1)} %copy-done.14, bf16[1024,1536]{1,0:T(8,128)(2,1)S(1)} %copy-done.28, bf16[1024,1536]{1,0:T(8,128)(2,1)} %get-tuple-element.136.refs_1_, ...), custom_call_target="tpu_custom_call" | custom-call | flops 99999997952 | bytes 10000 | tf_op jit(solution)/shard_map/pallas_call | solution.py:758
  206.4 13.8 %collective-permute-done.19 = bf16[4,2,48,768]{3,2,1,0:T(8,128)(2,1)S(1)} collective-permute-done((bf16[4,2,48,768]{3,2,1,0:T(8,128)(2,1)S(1)}, bf16[4,2,48,768]{3,2,1,0:T(8,128)(2,1)S(1)}, u32[]{:S(2)}, u32[]{:S(2)}) %collective-permute-start.19) | collective-permute-done | bytes 589856 | tf_op jit(solution)/shard_map/ppermute | solution.py:628
  226.1 6.7 %collective-permute-done.21 = bf16[4,1,96,768]{3,2,1,0:T(8,128)(2,1)S(1)} collective-permute-done((bf16[4,1,96,768]{3,2,1,0:T(8,128)(2,1)}, bf16[4,1,96,768]{3,2,1,0:T(8,128)(2,1)S(1)}, u32[]{:S(2)}, u32[]{:S(2)}) %collective-permute-start.21) | collective-permute-done | bytes 589856 | tf_op jit(solution)/shard_map/ppermute | solution.py:628
  235.0 5.9 %shard_map.341.refs_12_ = bf16[1024,768]{1,0:T(8,128)(2,1)} custom-call(s32[7]{0:T(128)S(1)} %copy-done.14, f32[1024,768]{1,0:T(8,128)S(1)} %copy-done.39, bf16[1024,768]{1,0:T(8,128)(2,1)S(1)} %copy-done.24, bf16[1024,384]{1,0:T(8,128)(2,1)S(1)} %get-tuple-element.187.refs_4_.refs_2_, bf16[1024,384]{1,0:T(8,128)(2,1)S(1)} %get-tuple-element.192.refs_6_.refs_3_, ...), custom_call_target="tpu_custom_call" | custom-call | flops 80000000000 | bytes 10000 | tf_op jit(solution)/shard_map/pallas_call | solution.py:758
  240.9 6.3 %collective-permute-done.22 = bf16[4,1,48,768]{3,2,1,0:T(8,128)(2,1)S(1)} collective-permute-done((bf16[4,1,48,768]{3,2,1,0:T(8,128)(2,1)S(1)}, bf16[4,1,48,768]{3,2,1,0:T(8,128)(2,1)S(1)}, u32[]{:S(2)}, u32[]{:S(2)}) %collective-permute-start.22) | collective-permute-done | bytes 294944 | tf_op jit(solution)/shard_map/ppermute | solution.py:628
  247.2 6.6 %collective-permute-done.26 = bf16[8,1,32,768]{3,2,1,0:T(8,128)(2,1)S(1)} collective-permute-done((bf16[8,1,32,768]{3,2,1,0:T(8,128)(2,1)S(1)}, bf16[8,1,32,768]{3,2,1,0:T(8,128)(2,1)S(1)}, u32[]{:S(2)}, u32[]{:S(2)}) %collective-permute-start.26) | collective-permute-done | bytes 393248 | tf_op jit(solution)/shard_map/ppermute | solution.py:628
  260.8 3.5 %collective-permute-done.28 = bf16[2,1,48,768]{3,2,0,1:T(8,128)(2,1)S(1)} collective-permute-done((bf16[2,1,48,768]{3,2,0,1:T(8,128)(2,1)S(1)}, bf16[2,1,48,768]{3,2,0,1:T(8,128)(2,1)S(1)}, u32[]{:S(2)}, u32[]{:S(2)}) %collective-permute-start.28) | collective-permute-done | bytes 147488 | tf_op jit(solution)/shard_map/ppermute | solution.py:628
  265.0 5.7 %collective-permute-done.29 = bf16[2,1,48,768]{3,2,0,1:T(8,128)(2,1)S(1)} collective-permute-done((bf16[2,1,48,768]{3,2,0,1:T(8,128)(2,1)S(1)}, bf16[2,1,48,768]{3,2,0,1:T(8,128)(2,1)S(1)}, u32[]{:S(2)}, u32[]{:S(2)}) %collective-permute-start.29) | collective-permute-done | bytes 147488 | tf_op jit(solution)/shard_map/ppermute | solution.py:628
  277.9 6.1 %collective-permute-done.40 = bf16[1,1,48,768]{3,2,1,0:T(8,128)(2,1)S(1)} collective-permute-done((bf16[1,1,48,768]{3,2,1,0:T(8,128)(2,1)S(1)}, bf16[1,1,48,768]{3,2,1,0:T(8,128)(2,1)S(1)}, u32[]{:S(2)}, u32[]{:S(2)}) %collective-permute-start.40) | collective-permute-done | bytes 73760 | tf_op jit(solution)/shard_map/ppermute | solution.py:628
  293.1 3.7 %collective-permute-done.38 = bf16[1,1,32,768]{3,2,1,0:T(8,128)(2,1)S(1)} collective-permute-done((bf16[1,1,32,768]{3,2,1,0:T(8,128)(2,1)S(1)}, bf16[1,1,32,768]{3,2,1,0:T(8,128)(2,1)S(1)}, u32[]{:S(2)}, u32[]{:S(2)}) %collective-permute-start.38) | collective-permute-done | bytes 49184 | tf_op jit(solution)/shard_map/ppermute | solution.py:628
  (258 shorter events, 93.7 us)
Async XLA Ops:
  14.0 38.1 %collective-permute-start.5 = (bf16[7,128,128]{2,1,0:T(8,128)(2,1)}, bf16[7,128,128]{2,1,0:T(8,128)(2,1)}, u32[]{:S(2)}, u32[]{:S(2)}) collective-permute-start(bf16[7,128,128]{2,1,0:T(8,128)(2,1)} %get-tuple-element.151), channel_id=1, source_target_pairs={{0,1},{1,2},{2,3},{3,4},{4,5},{5,6},{6,7},{7,8},{8,9},{9,10},{10,1... | collective-permute-start | bytes 688136 | tf_op jit(solution)/shard_map/ppermute | solution.py:880
  108.5 55.4 %collective-permute-start.13 = (bf16[7,128,128]{2,1,0:T(8,128)(2,1)}, bf16[7,128,128]{2,1,0:T(8,128)(2,1)}, u32[]{:S(2)}, u32[]{:S(2)}) collective-permute-start(bf16[7,128,128]{2,1,0:T(8,128)(2,1)} %get-tuple-element.184), channel_id=1, source_target_pairs={{1,0},{2,1},{3,2},{4,3},{5,4},{6,5},{7,6},{8,7},{9,8},{10,9},{11,1... | collective-permute-start | bytes 688136 | tf_op jit(solution)/shard_map/ppermute | solution.py:998
  111.3 14.2 %collective-permute-start.7 = (bf16[7,128,128]{2,1,0:T(8,128)(2,1)S(1)}, bf16[7,128,128]{2,1,0:T(8,128)(2,1)S(1)}, u32[]{:S(2)}, u32[]{:S(2)}) collective-permute-start(bf16[7,128,128]{2,1,0:T(8,128)(2,1)S(1)} %add_convert_fusion.3.refs_2_), channel_id=1, source_target_pairs={{0,2},{1,3},{2,0},{3,1},{4,6},{5,7},{6,4},{7,5},{8,10},{9,11},{10,... | collective-permute-start | bytes 688136 | tf_op jit(solution)/shard_map/ppermute | solution.py:628
  132.9 12.6 %collective-permute-start.11 = (bf16[16,48,768]{2,1,0:T(8,128)(2,1)S(1)}, bf16[16,48,768]{2,1,0:T(8,128)(2,1)S(1)}, u32[]{:S(2)}, u32[]{:S(2)}) collective-permute-start(bf16[16,48,768]{2,1,0:T(8,128)(2,1)S(1)} %get-tuple-element.180), channel_id=1, source_target_pairs={{0,1},{1,0},{2,3},{3,2},{4,5},{5,4},{6,7},{7,6},{8,9},{9,8},{10,11... | collective-permute-start | bytes 3538952 | tf_op jit(solution)/shard_map/ppermute | solution.py:628
  142.2 21.8 %collective-permute-start.12 = (bf16[7,128,128]{2,1,0:T(8,128)(2,1)}, bf16[7,128,128]{2,1,0:T(8,128)(2,1)}, u32[]{:S(2)}, u32[]{:S(2)}) collective-permute-start(bf16[7,128,128]{2,1,0:T(8,128)(2,1)} %add_convert_fusion.refs_2_.refs_15_), channel_id=1, source_target_pairs={{0,16},{1,17},{2,18},{3,19},{4,20},{5,21},{6,22},{7,23},{8,24},{9,... | collective-permute-start | bytes 688136 | tf_op jit(solution)/shard_map/ppermute | solution.py:628
  145.5 20.8 %collective-permute-start.14 = (bf16[16,48,768]{2,1,0:T(8,128)(2,1)}, bf16[16,48,768]{2,1,0:T(8,128)(2,1)}, u32[]{:S(2)}, u32[]{:S(2)}) collective-permute-start(bf16[16,48,768]{2,1,0:T(8,128)(2,1)} %get-tuple-element.185), channel_id=1, source_target_pairs={{0,1},{1,0},{2,3},{3,2},{4,5},{5,4},{6,7},{7,6},{8,9},{9,8},{10,11... | collective-permute-start | bytes 3538952 | tf_op jit(solution)/shard_map/ppermute | solution.py:628
  163.3 28.7 %collective-permute-start.15 = (bf16[16,64,768]{2,1,0:T(8,128)(2,1)S(1)}, bf16[16,64,768]{2,1,0:T(8,128)(2,1)S(1)}, u32[]{:S(2)}, u32[]{:S(2)}) collective-permute-start(bf16[16,64,768]{2,1,0:T(8,128)(2,1)S(1)} %get-tuple-element.189), channel_id=1, source_target_pairs={{0,1},{1,0},{2,3},{3,2},{4,5},{5,4},{6,7},{7,6},{8,9},{9,8},{10,11... | collective-permute-start | bytes 4718600 | tf_op jit(solution)/shard_map/ppermute | solution.py:628
  163.9 28.2 %collective-permute-start.16 = (bf16[8,1,96,768]{3,2,1,0:T(8,128)(2,1)}, bf16[8,1,96,768]{3,2,1,0:T(8,128)(2,1)S(1)}, u32[]{:S(2)}, u32[]{:S(2)}) collective-permute-start(bf16[8,1,96,768]{3,2,1,0:T(8,128)(2,1)} %get-tuple-element.190), channel_id=1, source_target_pairs={{0,2},{1,3},{2,0},{3,1},{4,6},{5,7},{6,4},{7,5},{8,10},{9,11},{10,... | collective-permute-start | bytes 3538952 | tf_op jit(solution)/shard_map/ppermute | solution.py:628
  181.0 39.5 %collective-permute-start.18 = (bf16[16,32,768]{2,1,0:T(8,128)(2,1)}, bf16[16,32,768]{2,1,0:T(8,128)(2,1)S(1)}, u32[]{:S(2)}, u32[]{:S(2)}) collective-permute-start(bf16[16,32,768]{2,1,0:T(8,128)(2,1)} %get-tuple-element.198), channel_id=1, source_target_pairs={{0,1},{1,0},{2,3},{3,2},{4,5},{5,4},{6,7},{7,6},{8,9},{9,8},{10,11... | collective-permute-start | bytes 2359304 | tf_op jit(solution)/shard_map/ppermute | solution.py:628
  203.9 20.5 %collective-permute-start.17 = (bf16[16,32,768]{2,1,0:T(8,128)(2,1)S(1)}, bf16[16,32,768]{2,1,0:T(8,128)(2,1)S(1)}, u32[]{:S(2)}, u32[]{:S(2)}) collective-permute-start(bf16[16,32,768]{2,1,0:T(8,128)(2,1)S(1)} %get-tuple-element.196), channel_id=1, source_target_pairs={{0,1},{1,0},{2,3},{3,2},{4,5},{5,4},{6,7},{7,6},{8,9},{9,8},{10,11... | collective-permute-start | bytes 2359304 | tf_op jit(solution)/shard_map/ppermute | solution.py:628
  204.0 16.2 %collective-permute-start.19 = (bf16[4,2,48,768]{3,2,1,0:T(8,128)(2,1)S(1)}, bf16[4,2,48,768]{3,2,1,0:T(8,128)(2,1)S(1)}, u32[]{:S(2)}, u32[]{:S(2)}) collective-permute-start(bf16[4,2,48,768]{3,2,1,0:T(8,128)(2,1)S(1)} %get-tuple-element.199), channel_id=1, source_target_pairs={{0,4},{1,5},{2,6},{3,7},{4,0},{5,1},{6,2},{7,3},{8,12},{9,13},{10,... | collective-permute-start | bytes 1769480 | tf_op jit(solution)/shard_map/ppermute | solution.py:628
  205.1 15.4 %collective-permute-start.20 = (bf16[8,1,48,768]{3,2,1,0:T(8,128)(2,1)S(1)}, bf16[8,1,48,768]{3,2,1,0:T(8,128)(2,1)S(1)}, u32[]{:S(2)}, u32[]{:S(2)}) collective-permute-start(bf16[8,1,48,768]{3,2,1,0:T(8,128)(2,1)S(1)} %copy-done.22), channel_id=1, source_target_pairs={{0,2},{1,3},{2,0},{3,1},{4,6},{5,7},{6,4},{7,5},{8,10},{9,11},{10,... | collective-permute-start | bytes 1769480 | tf_op jit(solution)/shard_map/ppermute | solution.py:628
  205.4 27.5 %collective-permute-start.21 = (bf16[4,1,96,768]{3,2,1,0:T(8,128)(2,1)}, bf16[4,1,96,768]{3,2,1,0:T(8,128)(2,1)S(1)}, u32[]{:S(2)}, u32[]{:S(2)}) collective-permute-start(bf16[4,1,96,768]{3,2,1,0:T(8,128)(2,1)} %get-tuple-element.203), channel_id=1, source_target_pairs={{0,4},{1,5},{2,6},{3,7},{4,0},{5,1},{6,2},{7,3},{8,12},{9,13},{10,... | collective-permute-start | bytes 1769480 | tf_op jit(solution)/shard_map/ppermute | solution.py:628
  220.2 27.0 %collective-permute-start.24 = (bf16[8,1,64,768]{3,2,1,0:T(8,128)(2,1)}, bf16[8,1,64,768]{3,2,1,0:T(8,128)(2,1)S(1)}, u32[]{:S(2)}, u32[]{:S(2)}) collective-permute-start(bf16[8,1,64,768]{3,2,1,0:T(8,128)(2,1)} %get-tuple-element.208), channel_id=1, source_target_pairs={{0,2},{1,3},{2,0},{3,1},{4,6},{5,7},{6,4},{7,5},{8,10},{9,11},{10,... | collective-permute-start | bytes 2359304 | tf_op jit(solution)/shard_map/ppermute | solution.py:628
  221.6 25.7 %collective-permute-start.25 = (bf16[4,2,32,768]{3,2,1,0:T(8,128)(2,1)S(1)}, bf16[4,2,32,768]{3,2,1,0:T(8,128)(2,1)S(1)}, u32[]{:S(2)}, u32[]{:S(2)}) collective-permute-start(bf16[4,2,32,768]{3,2,1,0:T(8,128)(2,1)S(1)} %get-tuple-element.210), channel_id=1, source_target_pairs={{0,4},{1,5},{2,6},{3,7},{4,0},{5,1},{6,2},{7,3},{8,12},{9,13},{10,... | collective-permute-start | bytes 1179656 | tf_op jit(solution)/shard_map/ppermute | solution.py:628
  222.6 24.6 %collective-permute-start.22 = (bf16[4,1,48,768]{3,2,1,0:T(8,128)(2,1)S(1)}, bf16[4,1,48,768]{3,2,1,0:T(8,128)(2,1)S(1)}, u32[]{:S(2)}, u32[]{:S(2)}) collective-permute-start(bf16[4,1,48,768]{3,2,1,0:T(8,128)(2,1)S(1)} %get-tuple-element.205), channel_id=1, source_target_pairs={{0,2},{1,3},{2,0},{3,1},{4,6},{5,7},{6,4},{7,5},{8,10},{9,11},{10,... | collective-permute-start | bytes 884744 | tf_op jit(solution)/shard_map/ppermute | solution.py:628
  224.4 22.8 %collective-permute-start.23 = (bf16[4,1,48,768]{3,2,1,0:T(8,128)(2,1)S(1)}, bf16[4,1,48,768]{3,2,1,0:T(8,128)(2,1)S(1)}, u32[]{:S(2)}, u32[]{:S(2)}) collective-permute-start(bf16[4,1,48,768]{3,2,1,0:T(8,128)(2,1)S(1)} %get-tuple-element.206), channel_id=1, source_target_pairs={{0,4},{1,5},{2,6},{3,7},{4,0},{5,1},{6,2},{7,3},{8,12},{9,13},{10,... | collective-permute-start | bytes 884744 | tf_op jit(solution)/shard_map/ppermute | solution.py:628
  232.8 21.0 %collective-permute-start.26 = (bf16[8,1,32,768]{3,2,1,0:T(8,128)(2,1)S(1)}, bf16[8,1,32,768]{3,2,1,0:T(8,128)(2,1)S(1)}, u32[]{:S(2)}, u32[]{:S(2)}) collective-permute-start(bf16[8,1,32,768]{3,2,1,0:T(8,128)(2,1)S(1)} %get-tuple-element.211), channel_id=1, source_target_pairs={{0,2},{1,3},{2,0},{3,1},{4,6},{5,7},{6,4},{7,5},{8,10},{9,11},{10,... | collective-permute-start | bytes 1179656 | tf_op jit(solution)/shard_map/ppermute | solution.py:628
  256.4 14.3 %collective-permute-start.30 = (bf16[4,1,64,768]{3,2,1,0:T(8,128)(2,1)S(1)}, bf16[4,1,64,768]{3,2,1,0:T(8,128)(2,1)S(1)}, u32[]{:S(2)}, u32[]{:S(2)}) collective-permute-start(bf16[4,1,64,768]{3,2,1,0:T(8,128)(2,1)S(1)} %get-tuple-element.219), channel_id=1, source_target_pairs={{0,4},{1,5},{2,6},{3,7},{4,0},{5,1},{6,2},{7,3},{8,12},{9,13},{10,... | collective-permute-start | bytes 1179656 | tf_op jit(solution)/shard_map/ppermute | solution.py:628
  258.3 12.5 %collective-permute-start.27 = (bf16[2,1,96,768]{3,2,0,1:T(8,128)(2,1)S(1)}, bf16[2,1,96,768]{3,2,0,1:T(8,128)(2,1)S(1)}, u32[]{:S(2)}, u32[]{:S(2)}) collective-permute-start(bf16[2,1,96,768]{3,2,0,1:T(8,128)(2,1)S(1)} %bitcast.140), channel_id=1, source_target_pairs={{0,8},{1,9},{2,10},{3,11},{4,12},{5,13},{6,14},{7,15},{8,0},{9,1},... | collective-permute-start | bytes 884744 | tf_op jit(solution)/shard_map/ppermute | solution.py:628
  271.7 14.5 %collective-permute-start.33 = (bf16[2,1,64,768]{3,2,0,1:T(8,128)(2,1)S(1)}, bf16[2,1,64,768]{3,2,0,1:T(8,128)(2,1)S(1)}, u32[]{:S(2)}, u32[]{:S(2)}) collective-permute-start(bf16[2,1,64,768]{3,2,0,1:T(8,128)(2,1)S(1)} %bitcast.141), channel_id=1, source_target_pairs={{0,8},{1,9},{2,10},{3,11},{4,12},{5,13},{6,14},{7,15},{8,0},{9,1},... | collective-permute-start | bytes 589832 | tf_op jit(solution)/shard_map/ppermute | solution.py:628
  272.7 12.4 %collective-permute-start.34 = (bf16[2,1,32,768]{3,2,0,1:T(8,128)(2,1)S(1)}, bf16[2,1,32,768]{3,2,0,1:T(8,128)(2,1)S(1)}, u32[]{:S(2)}, u32[]{:S(2)}) collective-permute-start(bf16[2,1,32,768]{3,2,0,1:T(8,128)(2,1)S(1)} %bitcast.145), channel_id=1, source_target_pairs={{0,8},{1,9},{2,10},{3,11},{4,12},{5,13},{6,14},{7,15},{8,0},{9,1},... | collective-permute-start | bytes 294920 | tf_op jit(solution)/shard_map/ppermute | solution.py:628
  273.8 12.4 %collective-permute-start.35 = (bf16[2,1,32,768]{3,2,0,1:T(8,128)(2,1)S(1)}, bf16[2,1,32,768]{3,2,0,1:T(8,128)(2,1)S(1)}, u32[]{:S(2)}, u32[]{:S(2)}) collective-permute-start(bf16[2,1,32,768]{3,2,0,1:T(8,128)(2,1)S(1)} %bitcast.144), channel_id=1, source_target_pairs={{0,8},{1,9},{2,10},{3,11},{4,12},{5,13},{6,14},{7,15},{8,0},{9,1},... | collective-permute-start | bytes 294920 | tf_op jit(solution)/shard_map/ppermute | solution.py:628
  274.7 14.2 %collective-permute-start.41 = (bf16[1,1,96,768]{3,2,1,0:T(8,128)(2,1)S(1)}, bf16[1,1,96,768]{3,2,1,0:T(8,128)(2,1)S(1)}, u32[]{:S(2)}, u32[]{:S(2)}) collective-permute-start(bf16[1,1,96,768]{3,2,1,0:T(8,128)(2,1)S(1)} %get-tuple-element.241), channel_id=1, source_target_pairs={{0,16},{1,17},{2,18},{3,19},{4,20},{5,21},{6,22},{7,23},{8,24},{9,... | collective-permute-start | bytes 442376 | tf_op jit(solution)/shard_map/ppermute | solution.py:628
  (88 other events, 778.4 us)
where the time goes:
time: 308 us; the launch traced here: 303 us
  Pallas kernels  150 us (49%)
  waiting for transfers between devices  72.3 us (23%)
  starting transfers between devices  47.8 us (16%)
  local copies, waits for them, and re-layouts  25.3 us (8%)
  other arithmetic  5.5 us (2%)
    pallas_call x14, Pallas kernels, call(): pl.pallas_call(body, grid_spec=pltpu.PrefetchScalarGridSpec(num_scalar_pr...  139 us
    ppermute x40, waiting for transfers between devices, exchange(): return lax.ppermute(x, AXES, [(i, i ^ mask) for i in range(count)])  72.3 us
    ppermute x40, starting transfers between devices, exchange(): return lax.ppermute(x, AXES, [(i, i ^ mask) for i in range(count)])  43.8 us
    unnamed x140, local copies, waits for them, and re-layouts  19.8 us
    pallas_call x9, Pallas kernels, add_step(): pl.pallas_call(body, in_specs=[pl.BlockSpec(memory_space=pltpu.SMEM)] + [...  11.2 us
  transfers between devices with their start and end apart: 42, of which 18 were waited for; matrix products, arithmetic and copies ran while one was open for 2% of the time, Pallas kernels for 28%

commit v1 on v0

--- a/solution.py
+++ b/solution.py
@@ -16,8 +16,8 @@
 HALF_PI = math.pi / 2.0
 MIB = 1 << 20
 VMEM = 60
-COST = 10
-FILL = 40
+COST = 0.01
+FILL = 20
 AXES = ("wide", "narrow")
 
 f32 = jnp.float32
@@ -466,22 +466,19 @@
 
 
 def query_back_kernel(
-    spot_ref, qf_ref, kf_ref, v_ref, dn_ref, q_ref, kept0, kept1, kept2, state_ref,
-    st_ref, cs_ref, x_ref, mixed_ref, dbranch_ref, vec_ref,
-    dq_ref, send_ref, keep_ref,
-    grads, lines,
-    *, npair, nchunk, piece,
+    spot_ref, qf_ref, kf_ref, v_ref, dn_ref, q_ref, kept0, kept1, kept2, state_ref, st_ref, cs_ref, *refs,
+    pair0, npair, nchunk, piece, last,
 ):
+    if last:
+        x_ref, other_ref, mixed_ref, dbranch_ref, vec_ref, dq_ref, send0, keep0, send1, keep1, grads = refs
+    else:
+        (dq_ref,) = refs
     step = pl.program_id(0)
     base = spot_ref[0]
     keepers = (kept0, kept1, kept2)
-
-    @pl.when(step == 0)
-    def _():
-        lines[...] = jnp.zeros_like(lines)
-
-    @pl.when(step < nchunk)
-    def _():
+    two = range(2)
+
+    def chunk_step():
         lo = lane_iota(CHUNK) < DH
         slots = lane_iota(LANES)
         lo_state = slots < DH
@@ -494,38 +491,46 @@
         carried = start < first
         from_far = start[0:1, :] < base
         at = pl.ds(pl.multiple_of(step * CHUNK, CHUNK), CHUNK)
-        for g in range(npair):
+        for g in range(pairs_of(v_ref.shape[1])):
             pair = slice(g * LANES, (g + 1) * LANES)
+            cols = [slice((2 * g + s) * LANES, (2 * g + s + 1) * LANES) for s in two]
+            heads = [2 * (pair0 + g) + s for s in two]
             vs = extended(v_ref[:, pair], lo)
-            far = unpack_state(state_ref, g, npair, lo_state, slots)
-            dns = [dn_ref[:, (2 * g + s) * LANES : (2 * g + s + 1) * LANES] for s in range(2)]
-            d_probs = [nt(dns[s], vs[s]) for s in range(2)]
+            far = unpack_state(state_ref, pair0 + g, npair, lo_state, slots)
+            dns = [dn_ref[:, c] for c in cols]
+            d_probs = [nt(dns[s], vs[s]) for s in two]
             d_probs = [jnp.where(mask, d, 0.0).astype(bf16) for d in d_probs]
             held = [
-                (keepers[h // 4][0, h % 4].astype(f32) + jnp.where(from_far, far[h - 2 * g], 0.0)).astype(bf16)
-                for h in (2 * g, 2 * g + 1)
+                (keepers[heads[s] // 4][0, heads[s] % 4].astype(f32) + jnp.where(from_far, far[s], 0.0)).astype(bf16)
+                for s in two
             ]
             d_qf = [
-                nn(d_probs[s], kf_ref[:, (2 * g + s) * LANES : (2 * g + s + 1) * LANES])
-                + jnp.where(carried, nt(dns[s], held[s]), 0.0)
-                for s in range(2)
+                nn(d_probs[s], kf_ref[:, cols[s]]) + jnp.where(carried, nt(dns[s], held[s]), 0.0) for s in two
             ]
             turned = [d * cs for d in d_qf]
             turned = [t + swap_halves(t) for t in turned]
             value = jnp.where(lo, turned[0], turned[1]) * sigmoid(q_ref[:, pair].astype(f32))
-            lines[0:8, pair] += fold_rows(value)
             value = value.astype(bf16)
             dq_ref[:, pair] = value
-            grads[at, pair] = value
+            if last:
+                grads[at, pair] = value
+
+    if not last:
+        chunk_step()
+        return
+
+    pl.when(step < nchunk)(chunk_step)
 
     @pl.when(step == nchunk)
     def _():
         own = spot_ref[2]
-        store_pieces(own, tn(x_ref[...], grads[...]), piece, send_ref, keep_ref, 0)
-        store_pieces(own, tn(mixed_ref[...], dbranch_ref[...]), piece, send_ref, keep_ref, piece)
-        total = jnp.sum(lines[...], axis=0, keepdims=True)
+        whole_q = jnp.concatenate([other_ref[...], grads[...]], axis=1)
+        store_pieces(own, tn(x_ref[...], whole_q), piece, send0, keep0, 0)
+        store_pieces(own, tn(mixed_ref[...], dbranch_ref[...]), piece, send1, keep1, 0)
+        total = jnp.sum(fold_rows(whole_q.astype(f32)), axis=0, keepdims=True)
         vec = jnp.where(row_iota(VEC_ROWS, total.shape[1]) == VEC_ROWS - 1, total, vec_ref[...])
-        store_lines(vec, send_ref, keep_ref, 2 * piece)
+        store_lines(vec[:8], send0, keep0, piece)
+        store_lines(vec[8:], send1, keep1, piece)
 
 
 def value_back_kernel(
@@ -599,8 +604,17 @@
         store_lines(jnp.broadcast_to(total, lines.shape), send_ref, keep_ref, piece)
 
 
-def outer_grad_kernel(spot_ref, act_ref, d_ref, send_ref, keep_ref, *, piece):
-    store_pieces(spot_ref[2], tn(act_ref[...], d_ref[...]), piece, send_ref, keep_ref, 0)
+def outer_grad_kernel(spot_ref, act_ref, d_ref, send0, keep0, send1, keep1, *, piece):
+    value = tn(act_ref[...], d_ref[...]).astype(bf16)
+    cut = piece // 2
+    for bit in range(2):
+
+        @pl.when(spot_ref[2] == bit)
+        def _():
+            for d in range(value.shape[0] // piece):
+                first, second = (keep0, keep1) if d % 2 == bit else (send0, send1)
+                first[d // 2] = value[d * piece : d * piece + cut, :]
+                second[d // 2] = value[d * piece + cut : (d + 1) * piece, :]
 
 
 def inner_grad_kernel(spot_ref, first_ref, dinner_ref, send_ref, keep_ref, *, piece, parts):
@@ -612,9 +626,9 @@
             store_pieces(spot_ref[2], value, piece, send_ref, keep_ref, i * piece)
 
 
-def tokens_grad_kernel(spot_ref, dr1_ref, q_ref, k0, k1, v0, v1, wq_ref, wk_ref, wv_ref, out_ref):
-    total = dr1_ref[...] + nt(q_ref[...], wq_ref[...])
-    for refs, w in (((k0, k1), wk_ref), ((v0, v1), wv_ref)):
+def tokens_grad_kernel(spot_ref, dr1_ref, q0, q1, k0, k1, v0, v1, wq_ref, wk_ref, wv_ref, out_ref):
+    total = dr1_ref[...]
+    for refs, w in (((q0, q1), wq_ref), ((k0, k1), wk_ref), ((v0, v1), wv_ref)):
         total = total + nt(jnp.concatenate([r[...] for r in refs], axis=1), w[...])
     out_ref[...] = total.astype(bf16)
 
@@ -634,81 +648,78 @@
 
 class Halving:
 
-    def __init__(self, send, keep, count, order):
+    def __init__(self, name, send, keep, count):
         self.count = count
         self.left = list(range(count.bit_length() - 2, 0, -1))
-        self.order = list(order)
         self.tail = send.shape[1:]
+        self.parts = [(name, self.tail[0])]
         self.keep = keep
-        self.recv = flip(send, 0, count)
-
-    def advance(self):
-        self.bit = self.order.pop(0)
-        axis = self.left.index(self.bit)
-        self.a, self.b = 1 << axis, 1 << (len(self.left) - 1 - axis)
-        self.left.remove(self.bit)
-        view = (self.a, 2, self.b, *self.tail)
-        full = jax.ShapeDtypeStruct((self.a, self.b, *self.tail), bf16)
-        return self.keep.reshape(view), self.recv.reshape(view), full
-
-    def specs(self, steps):
-        keep, recv, full = self.advance()
-        bit, rank = self.bit, len(self.tail)
-        used = min(self.a * self.b, 4, steps)
-        while used & (used - 1):
-            used -= 1
-        ca = min(self.a, used)
-        cb = used // ca
-        shape = (self.a // ca, None, self.b // cb, *self.tail)
-
-        def index(i, spot, other):
-            i = jnp.minimum(i, used - 1)
-            own = spot[2 + bit]
-            return (i // cb, 1 - own if other else own, i % cb) + (0,) * rank
-
-        def out_index(i, spot):
-            i = jnp.minimum(i, used - 1)
-            return (i // cb, i % cb) + (0,) * rank
-
-        ins = [pl.BlockSpec(shape, functools.partial(index, other=o)) for o in (True, True, False, False)]
-        out = pl.BlockSpec((shape[0], shape[2], *self.tail), out_index)
-        return ins, [keep, recv, keep, recv], [out, out], [full, full]
-
-    def take(self, send, keep):
-        self.keep = keep
-        self.recv = flip(send, self.bit, self.count)
+        self.send = send
+        self.bit = 0
+
+    def launch(self, *after):
+        send, *_ = lax.optimization_barrier((self.send, *after))
+        self.recv = exchange(send, 1 << self.bit, self.count)
+
+    def view(self, bit):
+        axis = self.left.index(bit)
+        a, b = 1 << axis, 1 << (len(self.left) - 1 - axis)
+        shape = (a, 2, b, *self.tail)
+        return self.keep.reshape(shape), self.recv.reshape(shape)
 
     def result(self):
-        return self.keep.reshape(self.tail).astype(f32) + self.recv.reshape(self.tail).astype(f32)
-
-
-def add_step(spot, sums, after=()):
-    for one in sums:
-        assert one.order
-    views = [one.advance() for one in sums]
+        total = self.keep.reshape(self.tail).astype(f32) + self.recv.reshape(self.tail).astype(f32)
+        out, at = {}, 0
+        for name, n in self.parts:
+            out[name] = total[at : at + n]
+            at += n
+        return out
+
+
+def add_step(spot, groups, after=()):
+    args, shapes, spans = [], [], []
+    for sums, bit in groups:
+        views = [one.view(bit) for one in sums]
+        args += [x for v in views for x in v]
+        a, _, b = views[0][0].shape[:3]
+        rows = sum(one.tail[0] for one in sums)
+        shapes += [jax.ShapeDtypeStruct((a, b, rows, sums[0].tail[1]), bf16)] * 2
+    nargs = len(args)
 
     def body(spot_ref, *refs):
-        ins, outs = refs[: 2 * len(sums)], refs[2 * len(sums) + len(after) :]
-        for n, one in enumerate(sums):
-            keep, recv = ins[2 * n : 2 * n + 2]
-            own = spot_ref[2 + one.bit]
-            for half, ref in ((1 - own, outs[2 * n]), (own, outs[2 * n + 1])):
-                ref[...] = (keep[:, half].astype(f32) + recv[:, half].astype(f32)).astype(bf16)
+        ins, outs = iter(refs[:nargs]), iter(refs[nargs + len(after) :])
+        for sums, bit in groups:
+            send, left = next(outs), next(outs)
+            own = spot_ref[2 + bit]
+            at = 0
+            for one in sums:
+                keep, recv = next(ins), next(ins)
+                n = one.tail[0]
+                for half, ref in ((1 - own, send), (own, left)):
+                    ref[:, :, at : at + n, :] = (keep[:, half].astype(f32) + recv[:, half].astype(f32)).astype(bf16)
+                at += n
 
     vmem = pl.BlockSpec(memory_space=pltpu.VMEM)
     out = pl.pallas_call(
         body,
         in_specs=[pl.BlockSpec(memory_space=pltpu.SMEM)]
-        + [vmem] * (2 * len(sums))
+        + [vmem] * nargs
         + [pl.BlockSpec(memory_space=pl.ANY)] * len(after),
-        out_specs=[vmem] * (2 * len(sums)),
-        out_shape=[v[2] for v in views for _ in range(2)],
-        compiler_params=pltpu.CompilerParams(vmem_limit_bytes=8 * MIB),
+        out_specs=[vmem] * len(shapes),
+        out_shape=shapes,
+        compiler_params=pltpu.CompilerParams(vmem_limit_bytes=16 * MIB),
         cost_estimate=pl.CostEstimate(flops=int(1e5), bytes_accessed=int(1e5), transcendentals=0),
-    )(spot, *[x for v in views for x in v[:2]], *after)
-    for n, one in enumerate(sums):
-        one.take(*out[2 * n : 2 * n + 2])
-    return out[-1]
+    )(spot, *args, *after)
+    got = []
+    for n, (sums, bit) in enumerate(groups):
+        one = sums[0]
+        one.parts = [p for s in sums for p in s.parts]
+        one.left = [x for x in one.left if x != bit]
+        one.tail = out[2 * n].shape[2:]
+        one.send, one.keep, one.bit = out[2 * n], out[2 * n + 1], bit
+        one.launch()
+        got.append(one)
+    return got, (out[-1],)
 
 
 def block(shape, index):
@@ -722,60 +733,27 @@
 SMEM = pl.BlockSpec(memory_space=pltpu.SMEM)
 
 
-def call(kernel, grid, in_specs, outs, out_specs, scratch, spot, args, micros, rides=(), after=(), thread=(), vmem=VMEM):
-    nin, nout, nafter, nthread = len(in_specs), len(outs), len(after), len(thread)
-    in_specs, out_specs = list(in_specs), list(out_specs)
-    out_shape = [jax.ShapeDtypeStruct(s, d) for s, d in outs]
-    args = list(args)
-    counts = []
-    for ride in rides:
-        i_specs, i_args, o_specs, o_shape = ride.specs(grid)
-        in_specs += i_specs
-        args += i_args
-        out_specs += o_specs
-        out_shape += o_shape
-        counts.append(len(o_specs))
-    nride = sum(counts)
-    hbm = pl.BlockSpec(memory_space=pl.ANY)
-    in_specs += [hbm] * (nafter + nthread)
-    out_specs += [hbm] * nthread
-    out_shape += [jax.ShapeDtypeStruct(t.shape, t.dtype) for t in thread]
-    first_thread = 1 + nin + 2 * nride + nafter
-    args += list(after) + list(thread)
+def call(kernel, grid, in_specs, outs, out_specs, scratch, spot, args, micros, after=(), vmem=VMEM):
+    nin, nafter = len(in_specs), len(after)
 
     def body(spot_ref, *refs):
-        ins = refs[:nin]
-        ride_ins = refs[nin : nin + 2 * nride]
-        rest = refs[nin + 2 * nride + nafter + nthread :]
-        host_outs = rest[:nout]
-        ride_outs = rest[nout : nout + nride]
-        held = rest[nout + nride + nthread :]
-        for n in range(nride):
-            a, b = ride_ins[2 * n : 2 * n + 2]
-            ride_outs[n][...] = (a[...].astype(f32) + b[...].astype(f32)).astype(bf16)
-        kernel(spot_ref, *ins, *host_outs, *held)
-
-    out = pl.pallas_call(
+        kernel(spot_ref, *refs[:nin], *refs[nin + nafter :])
+
+    return pl.pallas_call(
         body,
         grid_spec=pltpu.PrefetchScalarGridSpec(
             num_scalar_prefetch=1,
             grid=(grid,),
-            in_specs=in_specs,
-            out_specs=out_specs,
+            in_specs=[*in_specs, *[pl.BlockSpec(memory_space=pl.ANY)] * nafter],
+            out_specs=list(out_specs),
             scratch_shapes=scratch,
         ),
-        out_shape=out_shape,
-        input_output_aliases={first_thread + n: nout + nride + n for n in range(nthread)},
+        out_shape=[jax.ShapeDtypeStruct(s, d) for s, d in outs],
         compiler_params=pltpu.CompilerParams(
             dimension_semantics=("arbitrary",), vmem_limit_bytes=vmem * MIB
         ),
         cost_estimate=pl.CostEstimate(flops=int(COST * 1e9 * micros), bytes_accessed=int(1e4), transcendentals=0),
-    )(spot, *args)
-    at = nout
-    for ride, n in zip(rides, counts):
-        ride.take(*out[at : at + n])
-        at += n
-    return out[:nout] + out[at:]
+    )(spot, *args, *after)
 
 
 def per_device(
@@ -806,8 +784,6 @@
     pspec = whole(packed)
     fspec = whole((8, LANES))
     fixed = lambda shape: pl.BlockSpec(shape, lambda i, spot: (0,) * len(shape))
-    up = list(range(1, nbits))
-    swapped = up[:2][::-1] + up[2:]
 
     lines = (b_query, b_key, b_value, b_output, gain_first, shift_first, b_outer, gain_second, shift_second)
     k, v, kf, cs, st, en, total, near, flags, vecs = call(
@@ -926,13 +902,14 @@
     sums = {}
 
     def run_outer(after):
-        spec = block((per_step // 2, piece_o, width), lambda i: (i, 0, 0))
-        send, keep = call(
+        cut = piece_o // 2
+        spec = block((per_step // 2, cut, width), lambda i: (i, 0, 0))
+        out = call(
             functools.partial(outer_grad_kernel, piece=piece_o),
             parts,
             [block((rows, width), lambda i: (0, i)), whole((rows, width))],
-            [((half, piece_o, width), bf16)] * 2,
-            [spec, spec],
+            [((half, cut, width), bf16)] * 4,
+            [spec] * 4,
             [],
             spot,
             (act, d_outer),
@@ -940,10 +917,11 @@
             after=after,
             vmem=FILL,
         )
-        sums["outer"] = Halving(send, keep, count, up)
-        return (keep,)
-
-    def run_inner(after, lead, order, rides=()):
+        sums["outer0"] = Halving("outer0", out[0], out[1], count)
+        sums["outer1"] = Halving("outer1", out[2], out[3], count)
+        return (out[1],)
+
+    def run_inner(after, lead):
         n = parts // 2
         full = fixed((half, n * piece, width))
         send, keep = call(
@@ -956,60 +934,89 @@
             spot,
             (first, d_inner),
             5,
-            rides=rides,
             after=after,
             vmem=FILL,
         )
-        sums[f"inner{lead}"] = Halving(send, keep, count, order)
+        sums[f"inner{lead}"] = Halving(f"inner{lead}", send, keep, count)
         return (keep,)
 
-    def run_query_back(after, rides=()):
-        last = lambda i: jnp.minimum(i, nchunk - 1)
-        ltile = block((CHUNK, width), lambda i: (last(i), 0))
-        lf = block((CHUNK, feat), lambda i: (last(i), 0))
-        lcol = block((CHUNK, LANES), lambda i: (last(i), 0))
-        kept = block((1, gh, LANES, LANES), lambda i: (last(i), 0, 0, 0))
-        depth = 2 * piece + VEC_ROWS
+    halves = 2
+    hp = npair // halves
+    hw = hp * LANES
+    dqs = []
+
+    def run_query_back(n, after):
+        last = n == halves - 1
+        at_ = (lambda i: jnp.minimum(i, nchunk - 1)) if last else (lambda i: i)
+        fcol = block((CHUNK, 2 * hw), lambda i: (at_(i), n))
+        vcol = block((CHUNK, hw), lambda i: (at_(i), n))
+        lcol = block((CHUNK, LANES), lambda i: (at_(i), 0))
+        out = block((CHUNK, hw), lambda i: (at_(i), 0))
+        kept = block((1, gh, LANES, LANES), lambda i: (at_(i), 0, 0, 0))
+        depth = piece + 8
         full = fixed((half, depth, width))
         wide = whole((rows, width))
-        dq, send, keep = call(
-            functools.partial(query_back_kernel, npair=npair, nchunk=nchunk, piece=piece),
-            nchunk + 1,
-            [lf, lf, ltile, lf, ltile, kept, kept, kept, pspec, lcol, lcol, wide, wide, wide, whole((VEC_ROWS, width))],
-            [((rows, width), bf16)] + [((half, depth, width), bf16)] * 2,
-            [ltile, full, full],
-            [pltpu.VMEM((rows, width), bf16), pltpu.VMEM((8, width), f32)],
+        got = call(
+            functools.partial(
+                query_back_kernel, pair0=n * hp, npair=npair, nchunk=nchunk, piece=piece, last=last
+            ),
+            nchunk + last,
+            [fcol, fcol, vcol, fcol, vcol, kept, kept, kept, pspec, lcol, lcol]
+            + [wide, whole((rows, hw)), wide, wide, whole((VEC_ROWS, width))] * last,
+            [((rows, hw), bf16)] + [((half, depth, width), bf16)] * (4 * last),
+            [out] + [full] * (4 * last),
+            [pltpu.VMEM((rows, hw), bf16)] * last,
             spot,
-            (qf, kf, v, dn, q, *kepts, state_in, st, cs, tokens, mixed, d_branch, vgrad),
-            15,
-            rides=rides,
+            (qf, kf, v, dn, q, *kepts, state_in, st, cs)
+            + ((tokens, dqs[0], mixed, d_branch, vgrad) if last else ()),
+            9 if last else 7,
             after=after,
             vmem=FILL,
         )
-        sums["query"] = Halving(send, keep, count, up)
-        return dq
-
-    after_ = []
-    done = ()
-    for bit in range(nbits):
-        after_.append(flip(back, bit, count))
-        sent = (back, *done)
-        if bit == 2:
-            from_next = lax.ppermute(near, AXES, [(i + 1, i) for i in range(count - 1)])
-        if bit == 1:
-            done = run_outer(sent)
-        elif bit == 2:
-            done = run_inner(sent, 0, swapped)
-        elif bit == 3:
-            done = (add_step(spot, [sums["outer"]], sent),)
-            done = run_inner((*sent, *done), 1, up)
-        elif bit == 4:
-            done = (add_step(spot, [sums["inner0"]], sent),)
-            dq = run_query_back((*sent, *done))
-            done = (dq,)
-        if bit < nbits - 1:
-            back = joined(back, after_[-1], done)
-    after_.append(from_next)
+        dqs.append(got[0])
+        if last:
+            sums["query"] = Halving("query", got[1], got[2], count)
+            sums["output"] = Halving("output", got[3], got[4], count)
+        return (got[0],)
+
+    theirs = []
+    b1, b2 = 1, 2
+
+    def round_of(bit):
+        theirs.append(flip(back, bit, count))
+
+    def recvs(*names):
+        return tuple(sums[n].recv for n in names)
+
+    round_of(0)
+    back = joined(back, theirs[0])
+    round_of(1)
+    done = run_outer((back,))
+    back = joined(back, theirs[1], done)
+
+    round_of(2)
+    sums["outer0"].launch(back)
+    sums["outer1"].launch(back)
+    done = run_inner((back,), 0)
+    done = run_inner(done, 1)
+    back = joined(back, theirs[2], done + recvs("outer0", "outer1"))
+
+    round_of(3)
+    _, done = add_step(spot, [([sums["outer0"]], b1), ([sums["outer1"]], b2)], (back,))
+    sums["inner0"].launch(*done)
+    sums["inner1"].launch(*done)
+    done = run_query_back(0, done)
+    back = joined(back, theirs[3], done + recvs("outer0", "outer1", "inner0", "inner1"))
+
+    round_of(4)
+    near, *_ = lax.optimization_barrier((near, back))
+    from_next = lax.ppermute(near, AXES, [(i + 1, i) for i in range(count - 1)])
+    _, done = add_step(spot, [([sums["inner0"]], b1), ([sums["inner1"]], b2)], (back,))
+    done = run_query_back(1, done)
+    for bit in range(5, nbits):
+        back = joined(back, theirs[-1], done)
+        round_of(bit)
+    done += recvs("inner0", "inner1")
     (back_in,) = call(
         functools.partial(taken_kernel, lane=F_AFTER),
         1,
@@ -1018,18 +1025,15 @@
         [fixed(packed)],
         [],
         spot,
-        (*after_, flags),
+        (*theirs, from_next, flags),
         1,
         after=done,
         vmem=4,
     )
 
-    halves = 2
-    hp = npair // halves
-    hw = hp * LANES
     dks, dvs = [], []
 
-    def run_value_back(n, order, rides=(), after=()):
+    def run_value_back(n, after):
         index = lambda i: nchunk - 1 - jnp.minimum(i, nchunk - 1)
         fcol = block((CHUNK, 2 * hw), lambda i: (index(i), n))
         vcol = block((CHUNK, hw), lambda i: (index(i), n))
@@ -1052,49 +1056,66 @@
             spot,
             (qf, kf, v, dn, k, back_in, st, en, cs, tokens),
             10,
-            rides=rides,
             after=after,
             vmem=FILL,
         )
         dks.append(dk)
         dvs.append(dv)
-        sums[f"value{n}"] = Halving(send, keep, count, order)
-
-    done = (add_step(spot, [sums["inner1"]], (back_in,)),)
-    run_value_back(0, swapped, after=done)
-    done = (add_step(spot, [sums["query"], sums["outer"]], (dks[0],)),)
-    run_value_back(1, up, after=done)
-    done = (add_step(spot, [sums["value0"], sums["inner0"], sums["inner1"]], (dks[1],)),)
-    done = (add_step(spot, [sums["value1"]], done),)
+        sums[f"value{n}"] = Halving(f"value{n}", send, keep, count)
+
+    g0, g1 = [sums["outer0"], sums["inner0"]], [sums["outer1"], sums["inner1"]]
+    (f0, f1), done = add_step(spot, [(g0, b2), (g1, b1)], (back_in,))
+    sums["query"].launch(*done)
+    sums["output"].launch(*done)
+    run_value_back(0, done)
+
+    rest = list(range(3, nbits))
+    q, o, kv0 = sums["query"], sums["output"], sums["value0"]
+    done = (dks[0], f0.recv, f1.recv, q.recv, o.recv)
+    (ffn, q, o), done = add_step(spot, [([f0, f1], rest[0]), ([q], b1), ([o], b2)], done)
+    kv0.launch(*done)
+    run_value_back(1, done)
+
+    kv1 = sums["value1"]
+    kv1.launch(dks[1], ffn.recv, q.recv, o.recv)
+    groups = [([kv1], b1), ([kv0], b2), ([q], b2), ([o], b1), ([ffn], rest[1])]
+    (kv1, kv0, q, o, ffn), done = add_step(spot, groups, (dks[1], ffn.recv, q.recv, o.recv))
 
     (grad_tokens,) = call(
         tokens_grad_kernel,
         nchunk,
-        [tile, tile] + [block((CHUNK, hw), at)] * 4 + [square] * 3,
+        [tile] + [block((CHUNK, hw), at)] * 6 + [square] * 3,
         [((rows, width), bf16)],
         [tile],
         [],
         spot,
-        (d_r1, dq, *dks, *dvs, w_query, w_key, w_value),
+        (d_r1, *dqs, *dks, *dvs, w_query, w_key, w_value),
         8,
         after=done,
         vmem=FILL,
     )
-    done = (grad_tokens,)
-    while True:
-        left = [s for s in sums.values() if s.order]
-        if not left:
-            break
-        done = (add_step(spot, left, done),)
-
-    g_outer = sums["outer"].result()
-    inner0, inner1 = sums["inner0"].result(), sums["inner1"].result()
-    cuts = [inner0[i * piece : (i + 1) * piece] for i in range(parts // 2)]
-    cuts += [inner1[i * piece : (i + 1) * piece] for i in range(parts // 2)]
+    done = (grad_tokens, ffn.recv, q.recv, o.recv, kv0.recv, kv1.recv)
+    groups = [([kv1], b2), ([kv0], b1), ([q, o], rest[0])]
+    more = [([ffn], rest[2])] if len(rest) > 2 else []
+    (kv1, kv0, qo, *_), done = add_step(spot, groups + more, done)
+    done = (kv0.recv, kv1.recv, qo.recv)
+    (kv, qo), done = add_step(spot, [([kv0, kv1], rest[0]), ([qo], rest[1])], done)
+    while kv.left:
+        open_ = [one for one in (kv, qo, ffn) if one.left]
+        add_step(spot, [([one], one.left[-1]) for one in open_])
+
+    found = {}
+    for one in (ffn, qo, kv):
+        found.update(one.result())
+    g_outer = jnp.concatenate([found["outer0"], found["outer1"]])
+    cuts = []
+    for lead in range(2):
+        block_sum = found[f"inner{lead}"]
+        cuts += [block_sum[i * piece : (i + 1) * piece] for i in range(parts // 2)]
     g_inner = jnp.concatenate(cuts, axis=1)
-    query = sums["query"].result()
-    g_query, g_output, vec = query[:piece], query[piece : 2 * piece], query[2 * piece :]
-    kv = [sums[f"value{n}"].result() for n in range(halves)]
+    g_query, g_output = found["query"][:piece], found["output"][:piece]
+    vec = jnp.concatenate([found["query"][piece:], found["output"][piece:]])
+    kv = [found[f"value{n}"] for n in range(halves)]
     g_kv = [jnp.concatenate([s[:piece, m * hw : (m + 1) * hw] for s in kv], axis=1) for m in range(2)]
     b_kv = [jnp.concatenate([s[piece, m * hw : (m + 1) * hw] for s in kv]) for m in range(2)]
 

time: 308 us -> 273 us (0.89)
  waiting for transfers between devices: 72.3 us -> 42.6 us
  local copies, waits for them, and re-layouts: 25.3 us -> 38.3 us
  starting transfers between devices: 47.8 us -> 39.1 us
  Pallas kernels: 150 us -> 142 us
    ppermute x40 -> x38, waiting for transfers between devices: 72.3 us -> 42.6 us  [exchange(): return lax.ppermute(x, AXES, [(i, i ^ mask) for i in range(count)])]
    unnamed x140 -> x150, local copies, waits for them, and re-layouts: 19.8 us -> 32.9 us
    ppermute x40 -> x38, starting transfers between devices: 43.8 us -> 36.2 us  [exchange(): return lax.ppermute(x, AXES, [(i, i ^ mask) for i in range(count)])]
    pallas_call x14 -> x15, Pallas kernels: 139 us -> 133 us  [call(): pl.pallas_call(body, grid_spec=pltpu.PrefetchScalarGridSpec(num_scalar_pr...]
    pallas_call x9 -> x8, Pallas kernels: 11.2 us -> 8.37 us  [add_step(): pl.pallas_call(body, in_specs=[pl.BlockSpec(memory_space=pltpu.SMEM)] + [...]
  transfers between devices with their start and end apart: 42 -> 40, of which waited for: 18 -> 16; matrix products, arithmetic and copies ran while one was open for 2% -> 2% of each run, Pallas kernels for 28% -> 25%
where the time goes in v1:
time: 273 us; the launch traced here: 268 us
  Pallas kernels  142 us (52%)
  waiting for transfers between devices  42.6 us (16%)
  starting transfers between devices  39.1 us (14%)
  local copies, waits for them, and re-layouts  38.3 us (14%)
  other arithmetic  4.79 us (2%)
    pallas_call x15, Pallas kernels, call(): pl.pallas_call(body, grid_spec=pltpu.PrefetchScalarGridSpec(num_scalar_pr...  133 us
    ppermute x38, waiting for transfers between devices, exchange(): return lax.ppermute(x, AXES, [(i, i ^ mask) for i in range(count)])  42.6 us
    ppermute x38, starting transfers between devices, exchange(): return lax.ppermute(x, AXES, [(i, i ^ mask) for i in range(count)])  36.2 us
    unnamed x150, local copies, waits for them, and re-layouts  32.9 us
    pallas_call x8, Pallas kernels, add_step(): pl.pallas_call(body, in_specs=[pl.BlockSpec(memory_space=pltpu.SMEM)] + [...  8.37 us
  transfers between devices with their start and end apart: 40, of which 16 were waited for; matrix products, arithmetic and copies ran while one was open for 2% of the time, Pallas kernels for 25%

profile of v1, /device:TPU:0, one launch (start us, length us, event | category | flops | bytes accessed | tf_op | source)
XLA Modules:
  0.0 268.1 jit_solution(2946297304049945192)
XLA Ops:
  1.3 12.2 %shard_map.322 = (bf16[1024,768]{1,0:T(8,128)(2,1)}, bf16[1024,768]{1,0:T(8,128)(2,1)}, bf16[1024,1536]{1,0:T(8,128)(2,1)}, f32[1024,128]{1,0:T(8,128)}, s32[102...) custom-call(s32[7]{0:T(128)} %stack.31.spot_ref, ...), custom_call_target="tpu_custom_call" | custom-call | flops 120000000 | bytes 10000 | tf_op jit(solution)/shard_map/pallas_call | solution.py:742
  16.4 3.0 %collective-permute-start.1 = (bf16[7,128,128]{2,1,0:T(8,128)(2,1)S(1)}, bf16[7,128,128]{2,1,0:T(8,128)(2,1)S(1)}, u32[]{:S(2)}, u32[]{:S(2)}) collective-permute-start(bf16[7,128,128]{2,1,0:T(8,128)(2,1)S(1)} %add_convert_fusion.7.refs_4_), channel_id=1, source_target_pairs={{0,2},{1,3},{2,0},{3,1},{4,6},{5,7},{6,4},{7,5},{8,10},{9,11},{10,... | collective-permute-start | bytes 688136 | tf_op jit(solution)/shard_map/ppermute | solution.py:642
  23.9 4.1 %shard_map.323 = (bf16[1024,768]{1,0:T(8,128)(2,1)S(1)}, bf16[1024,1536]{1,0:T(8,128)(2,1)S(1)}) custom-call(s32[7]{0:T(128)S(1)} %copy-done.54, bf16[1024,768]{1,0:T(8,128)(2,1)S(1)} %copy-done.6, bf16[768,768]{1,0:T(8,128)(2,1)S(1)} %copy-done.22, f32[13,768]{1,0:T(8,128)S(1)} %copy-done.60, f32[1024,128]{1,0:T(8,128)S(1)} %copy-done.14, ...), custom_call_target="tpu_custom_call" | custom-call | flops 40000000 | bytes 10000 | tf_op jit(solution)/shard_map/pallas_call | solution.py:742
  31.8 4.1 %shard_map.324 = (f32[1024,512]{1,0:T(8,128)S(1)}, bf16[4,4,128,128]{3,2,1,0:T(8,128)(2,1)S(1)}) custom-call(s32[7]{0:T(128)S(1)} %copy-done.54, bf16[1024,1536]{1,0:T(8,128)(2,1)S(1)} %get-tuple-element.140.refs_0_.refs_3_, bf16[1024,1536]{1,0:T(8,128)(2,1)S(1)} %copy-done.2, bf16[1024,768]{1,0:T(8,128)(2,1)S(1)} %copy-done.4, s32[1024,128]{1,0:T(8,128)S(1)} %copy-done.9, ...), custom_call_target="tpu_custom_call" | custom-call | flops 40000000 | bytes 10000 | tf_op jit(solution)/shard_map/pallas_call | solution.py:742
  39.3 4.1 %shard_map.325 = (f32[1024,512]{1,0:T(8,128)S(1)}, bf16[4,4,128,128]{3,2,1,0:T(8,128)(2,1)S(1)}) custom-call(s32[7]{0:T(128)S(1)} %copy-done.54, bf16[1024,1536]{1,0:T(8,128)(2,1)S(1)} %get-tuple-element.140.refs_0_.refs_3_, bf16[1024,1536]{1,0:T(8,128)(2,1)S(1)} %copy-done.2, bf16[1024,768]{1,0:T(8,128)(2,1)S(1)} %copy-done.4, s32[1024,128]{1,0:T(8,128)S(1)} %copy-done.9, ...), custom_call_target="tpu_custom_call" | custom-call | flops 40000000 | bytes 10000 | tf_op jit(solution)/shard_map/pallas_call | solution.py:742
  45.6 3.1 %collective-permute-start.4 = (bf16[7,128,128]{2,1,0:T(8,128)(2,1)S(1)}, bf16[7,128,128]{2,1,0:T(8,128)(2,1)S(1)}, u32[]{:S(2)}, u32[]{:S(2)}) collective-permute-start(bf16[7,128,128]{2,1,0:T(8,128)(2,1)S(1)} %add_convert_fusion.4.refs_5_), channel_id=1, source_target_pairs={{0,16},{1,17},{2,18},{3,19},{4,20},{5,21},{6,22},{7,23},{8,24},{9,... | collective-permute-start | bytes 688136 | tf_op jit(solution)/shard_map/ppermute | solution.py:642
  48.7 4.1 %shard_map.326 = (f32[1024,512]{1,0:T(8,128)S(1)}, bf16[4,4,128,128]{3,2,1,0:T(8,128)(2,1)S(1)}) custom-call(s32[7]{0:T(128)S(1)} %copy-done.54, bf16[1024,1536]{1,0:T(8,128)(2,1)S(1)} %get-tuple-element.140.refs_0_.refs_3_, bf16[1024,1536]{1,0:T(8,128)(2,1)S(1)} %copy-done.2, bf16[1024,768]{1,0:T(8,128)(2,1)S(1)} %copy-done.4, s32[1024,128]{1,0:T(8,128)S(1)} %copy-done.9, ...), custom_call_target="tpu_custom_call" | custom-call | flops 40000000 | bytes 10000 | tf_op jit(solution)/shard_map/pallas_call | solution.py:742
  54.8 5.1 %collective-permute-done.4.refs_16_ = bf16[7,128,128]{2,1,0:T(8,128)(2,1)S(1)} collective-permute-done((bf16[7,128,128]{2,1,0:T(8,128)(2,1)S(1)}, bf16[7,128,128]{2,1,0:T(8,128)(2,1)S(1)}, u32[]{:S(2)}, u32[]{:S(2)}) %collective-permute-start.4) | collective-permute-done | bytes 229408 | tf_op jit(solution)/shard_map/ppermute | solution.py:642
  60.6 51.9 %shard_map.327 = (bf16[1024,768]{1,0:T(8,128)(2,1)}, bf16[1024,768]{1,0:T(8,128)(2,1)}, bf16[1024,768]{1,0:T(8,128)(2,1)}, bf16[1024,3072]{1,0:T(8,128)(2,1)}, b...) custom-call(s32[7]{0:T(128)} %stack.31.spot_ref, ...), custom_call_target="tpu_custom_call" | custom-call | flops 500000000 | bytes 10000 | tf_op jit(solution)/shard_map/pallas_call | solution.py:742
  116.1 2.8 %copy-done.18 = bf16[1024,3072]{1,0:T(8,128)(2,1)S(1)} copy-done((bf16[1024,3072]{1,0:T(8,128)(2,1)S(1)}, bf16[1024,3072]{1,0:T(8,128)(2,1)}, u32[]{:S(2)}) %copy-start.18) | copy-done | bytes 6291480
  120.3 7.2 %shard_map.328 = (bf16[16,48,768]{2,1,0:T(8,128)(2,1)S(1)}, bf16[16,48,768]{2,1,0:T(8,128)(2,1)S(1)}, bf16[16,48,768]{2,1,0:T(8,128)(2,1)S(1)}, bf16[16,48,768]{2,1,0:T(8,128)(2,1)S(1)}) custom-call(s32[7]{0:T(128)S(1)} %copy-done.55, bf16[1024,3072]{1,0:T(8,128)(2,1)S(1)} %copy-done.18, bf16[1024,768]{1,0:T(8,128)(2,1)S(1)} %copy-done.40, ...), custom_call_target="tpu_custom_call" | custom-call | flops 90000000 | bytes 10000 | tf_op jit(solution)/shard_map/pallas_call | solution.py:742
  129.3 3.9 %shard_map.329 = (bf16[16,48,768]{2,1,0:T(8,128)(2,1)S(1)}, bf16[16,48,768]{2,1,0:T(8,128)(2,1)S(1)}) custom-call(s32[7]{0:T(128)S(1)} %copy-done.55, bf16[1024,768]{1,0:T(8,128)(2,1)S(1)} %copy-done.19, bf16[1024,3072]{1,0:T(8,128)(2,1)S(1)} %copy-done.11, bf16[7,128,128]{2,1,0:T(8,128)(2,1)S(1)} %add_convert_fusion.2.refs_2_), custom_call_target="tpu_custom_call" | custom-call | flops 50000000 | bytes 10000 | tf_op jit(solution)/shard_map/pallas_call | solution.py:742
  133.3 3.9 %shard_map.330 = (bf16[16,48,768]{2,1,0:T(8,128)(2,1)S(1)}, bf16[16,48,768]{2,1,0:T(8,128)(2,1)S(1)}) custom-call(s32[7]{0:T(128)S(1)} %copy-done.55, bf16[1024,768]{1,0:T(8,128)(2,1)S(1)} %copy-done.19, bf16[1024,3072]{1,0:T(8,128)(2,1)S(1)} %copy-done.11, bf16[16,48,768]{2,1,0:T(8,128)(2,1)S(1)} %get-tuple-element.179.refs_2_), custom_call_target="tpu_custom_call" | custom-call | flops 50000000 | bytes 10000 | tf_op jit(solution)/shard_map/pallas_call | solution.py:742
  141.2 4.4 %shard_map.332.refs_12_.refs_1_ = bf16[1024,384]{1,0:T(8,128)(2,1)S(1)} custom-call(s32[7]{0:T(128)S(1)} %copy-done.55, bf16[1024,1536]{1,0:T(8,128)(2,1)S(1)} %copy-done.1, bf16[1024,1536]{1,0:T(8,128)(2,1)S(1)} %copy-done.3, bf16[1024,768]{1,0:T(8,128)(2,1)S(1)} %copy-done.5, bf16[1024,1536]{1,0:T(8,128)(2,1)S(1)} %copy-done.8, ...), custom_call_target="tpu_custom_call" | custom-call | flops 70000000 | bytes 10000 | tf_op jit(solution)/shard_map/pallas_call | solution.py:742
  148.2 6.2 %collective-permute-done.14 = bf16[8,1,48,768]{3,2,1,0:T(8,128)(2,1)S(1)} collective-permute-done((bf16[8,1,48,768]{3,2,1,0:T(8,128)(2,1)S(1)}, bf16[8,1,48,768]{3,2,1,0:T(8,128)(2,1)S(1)}, u32[]{:S(2)}, u32[]{:S(2)}) %collective-permute-start.14) | collective-permute-done | bytes 589856 | tf_op jit(solution)/shard_map/ppermute | solution.py:642
  160.7 9.2 %shard_map.334 = (bf16[1024,384]{1,0:T(8,128)(2,1)S(1)}, bf16[16,32,768]{2,1,0:T(8,128)(2,1)S(1)}, bf16[16,32,768]{2,1,0:T(8,128)(2,1)S(1)}, bf16[16,32,768]{2,1,0:T(8,128)(2,1)S(1)}, bf16[16,32,768]{2,1,0:T(8,128)(2,1)S(1)}) custom-call(s32[7]{0:T(128)S(1)} %copy-done.55, bf16[1024,1536]{1,0:T(8,128)(2,1)S(1)} %copy-done.1, ...), custom_call_target="tpu_custom_call" | custom-call | flops 90000000 | bytes 10000 | tf_op jit(solution)/shard_map/pallas_call | solution.py:742
  170.0 4.5 %collective-permute-done.16.refs_4_ = bf16[7,128,128]{2,1,0:T(8,128)(2,1)S(1)} collective-permute-done((bf16[7,128,128]{2,1,0:T(8,128)(2,1)S(1)}, bf16[7,128,128]{2,1,0:T(8,128)(2,1)S(1)}, u32[]{:S(2)}, u32[]{:S(2)}) %collective-permute-start.16) | collective-permute-done | bytes 229408 | tf_op jit(solution)/shard_map/ppermute | solution.py:642
  179.2 8.5 %shard_map.337 = (bf16[1024,384]{1,0:T(8,128)(2,1)S(1)}, bf16[1024,384]{1,0:T(8,128)(2,1)S(1)}, bf16[16,32,768]{2,1,0:T(8,128)(2,1)S(1)}, bf16[16,32,768]{2,1,0:T(8,128)(2,1)S(1)}) custom-call(s32[7]{0:T(128)S(1)} %copy-done.55, bf16[1024,1536]{1,0:T(8,128)(2,1)S(1)} %copy-done.1, bf16[1024,1536]{1,0:T(8,128)(2,1)S(1)} %copy-done.3, ...), custom_call_target="tpu_custom_call" | custom-call | flops 100000000 | bytes 10000 | tf_op jit(solution)/shard_map/pallas_call | solution.py:742
  187.7 4.8 %collective-permute-done.20.refs_9_ = bf16[4,1,96,768]{3,2,1,0:T(8,128)(2,1)S(1)} collective-permute-done((bf16[4,1,96,768]{3,2,1,0:T(8,128)(2,1)S(1)}, bf16[4,1,96,768]{3,2,1,0:T(8,128)(2,1)S(1)}, u32[]{:S(2)}, u32[]{:S(2)}) %collective-permute-start.20) | collective-permute-done | bytes 589856 | tf_op jit(solution)/shard_map/ppermute | solution.py:642
  196.5 8.7 %shard_map.339 = (bf16[1024,384]{1,0:T(8,128)(2,1)S(1)}, bf16[1024,384]{1,0:T(8,128)(2,1)S(1)}, bf16[16,32,768]{2,1,0:T(8,128)(2,1)S(1)}, bf16[16,32,768]{2,1,0:T(8,128)(2,1)S(1)}) custom-call(s32[7]{0:T(128)S(1)} %copy-done.55, bf16[1024,1536]{1,0:T(8,128)(2,1)S(1)} %copy-done.1, bf16[1024,1536]{1,0:T(8,128)(2,1)S(1)} %copy-done.3, ...), custom_call_target="tpu_custom_call" | custom-call | flops 100000000 | bytes 10000 | tf_op jit(solution)/shard_map/pallas_call | solution.py:742
  205.2 3.1 %collective-permute-done.24.refs_11_ = bf16[2,1,192,768]{3,2,1,0:T(8,128)(2,1)S(1)} collective-permute-done((bf16[2,1,192,768]{3,2,1,0:T(8,128)(2,1)S(1)}, bf16[2,1,192,768]{3,2,1,0:T(8,128)(2,1)S(1)}, u32[]{:S(2)}, u32[]{:S(2)}) %collective-permute-start.24) | collective-permute-done | bytes 589856 | tf_op jit(solution)/shard_map/ppermute | solution.py:642
  233.1 5.8 %shard_map.341.refs_8_ = bf16[1024,768]{1,0:T(8,128)(2,1)} custom-call(s32[7]{0:T(128)S(1)} %copy-done.55, f32[1024,768]{1,0:T(8,128)S(1)} %copy-done.30, bf16[1024,384]{1,0:T(8,128)(2,1)S(1)} %shard_map.332.refs_12_.refs_1_, bf16[1024,384]{1,0:T(8,128)(2,1)S(1)} %copy-done.29, bf16[1024,384]{1,0:T(8,128)(2,1)S(1)} %copy-done.27, ...), custom_call_target="tpu_custom_call" | custom-call | flops 80000000 | bytes 10000 | tf_op jit(solution)/shard_map/pallas_call | solution.py:742
  253.8 2.9 %collective-permute-done.37 = bf16[1,1,64,768]{3,2,1,0:T(8,128)(2,1)S(1)} collective-permute-done((bf16[1,1,64,768]{3,2,1,0:T(8,128)(2,1)S(1)}, bf16[1,1,64,768]{3,2,1,0:T(8,128)(2,1)S(1)}, u32[]{:S(2)}, u32[]{:S(2)}) %collective-permute-start.37) | collective-permute-done | bytes 98336 | tf_op jit(solution)/shard_map/ppermute | solution.py:642
  262.6 3.3 %collective-permute-done.39 = bf16[1,1,64,768]{3,2,1,0:T(8,128)(2,1)S(1)} collective-permute-done((bf16[1,1,64,768]{3,2,1,0:T(8,128)(2,1)S(1)}, bf16[1,1,64,768]{3,2,1,0:T(8,128)(2,1)S(1)}, u32[]{:S(2)}, u32[]{:S(2)}) %collective-permute-start.39) | collective-permute-done | bytes 98336 | tf_op jit(solution)/shard_map/ppermute | solution.py:642
  (261 shorter events, 95.5 us)
Async XLA Ops:
  16.4 11.6 %collective-permute-start.1 = (bf16[7,128,128]{2,1,0:T(8,128)(2,1)S(1)}, bf16[7,128,128]{2,1,0:T(8,128)(2,1)S(1)}, u32[]{:S(2)}, u32[]{:S(2)}) collective-permute-start(bf16[7,128,128]{2,1,0:T(8,128)(2,1)S(1)} %add_convert_fusion.7.refs_4_), channel_id=1, source_target_pairs={{0,2},{1,3},{2,0},{3,1},{4,6},{5,7},{6,4},{7,5},{8,10},{9,11},{10,... | collective-permute-start | bytes 688136 | tf_op jit(solution)/shard_map/ppermute | solution.py:642
  37.6 17.2 %collective-permute-start.5 = (bf16[7,128,128]{2,1,0:T(8,128)(2,1)S(1)}, bf16[7,128,128]{2,1,0:T(8,128)(2,1)S(1)}, u32[]{:S(2)}, u32[]{:S(2)}) collective-permute-start(bf16[7,128,128]{2,1,0:T(8,128)(2,1)S(1)} %copy-done.74), channel_id=1, source_target_pairs={{0,1},{1,2},{2,3},{3,4},{4,5},{5,6},{6,7},{7,8},{8,9},{9,10},{10,1... | collective-permute-start | bytes 688136 | tf_op jit(solution)/shard_map/ppermute | solution.py:856
  45.6 14.3 %collective-permute-start.4 = (bf16[7,128,128]{2,1,0:T(8,128)(2,1)S(1)}, bf16[7,128,128]{2,1,0:T(8,128)(2,1)S(1)}, u32[]{:S(2)}, u32[]{:S(2)}) collective-permute-start(bf16[7,128,128]{2,1,0:T(8,128)(2,1)S(1)} %add_convert_fusion.4.refs_5_), channel_id=1, source_target_pairs={{0,16},{1,17},{2,18},{3,19},{4,20},{5,21},{6,22},{7,23},{8,24},{9,... | collective-permute-start | bytes 688136 | tf_op jit(solution)/shard_map/ppermute | solution.py:642
  115.2 12.3 %collective-permute-start.7 = (bf16[7,128,128]{2,1,0:T(8,128)(2,1)S(1)}, bf16[7,128,128]{2,1,0:T(8,128)(2,1)S(1)}, u32[]{:S(2)}, u32[]{:S(2)}) collective-permute-start(bf16[7,128,128]{2,1,0:T(8,128)(2,1)S(1)} %add_convert_fusion.3.refs_2_), channel_id=1, source_target_pairs={{0,2},{1,3},{2,0},{3,1},{4,6},{5,7},{6,4},{7,5},{8,10},{9,11},{10,... | collective-permute-start | bytes 688136 | tf_op jit(solution)/shard_map/ppermute | solution.py:642
  138.5 16.9 %collective-permute-start.12 = (bf16[16,48,768]{2,1,0:T(8,128)(2,1)S(1)}, bf16[16,48,768]{2,1,0:T(8,128)(2,1)S(1)}, u32[]{:S(2)}, u32[]{:S(2)}) collective-permute-start(bf16[16,48,768]{2,1,0:T(8,128)(2,1)S(1)} %get-tuple-element.190), channel_id=1, source_target_pairs={{0,1},{1,0},{2,3},{3,2},{4,5},{5,4},{6,7},{7,6},{8,9},{9,8},{10,11... | collective-permute-start | bytes 3538952 | tf_op jit(solution)/shard_map/ppermute | solution.py:642
  138.5 16.8 %collective-permute-start.11 = (bf16[16,48,768]{2,1,0:T(8,128)(2,1)S(1)}, bf16[16,48,768]{2,1,0:T(8,128)(2,1)S(1)}, u32[]{:S(2)}, u32[]{:S(2)}) collective-permute-start(bf16[16,48,768]{2,1,0:T(8,128)(2,1)S(1)} %get-tuple-element.188), channel_id=1, source_target_pairs={{0,1},{1,0},{2,3},{3,2},{4,5},{5,4},{6,7},{7,6},{8,9},{9,8},{10,11... | collective-permute-start | bytes 3538952 | tf_op jit(solution)/shard_map/ppermute | solution.py:642
  139.0 15.3 %collective-permute-start.14 = (bf16[8,1,48,768]{3,2,1,0:T(8,128)(2,1)S(1)}, bf16[8,1,48,768]{3,2,1,0:T(8,128)(2,1)S(1)}, u32[]{:S(2)}, u32[]{:S(2)}) collective-permute-start(bf16[8,1,48,768]{3,2,1,0:T(8,128)(2,1)S(1)} %get-tuple-element.191), channel_id=1, source_target_pairs={{0,2},{1,3},{2,0},{3,1},{4,6},{5,7},{6,4},{7,5},{8,10},{9,11},{10,... | collective-permute-start | bytes 1769480 | tf_op jit(solution)/shard_map/ppermute | solution.py:642
  140.3 15.0 %collective-permute-start.15 = (bf16[4,2,48,768]{3,2,1,0:T(8,128)(2,1)S(1)}, bf16[4,2,48,768]{3,2,1,0:T(8,128)(2,1)S(1)}, u32[]{:S(2)}, u32[]{:S(2)}) collective-permute-start(bf16[4,2,48,768]{3,2,1,0:T(8,128)(2,1)S(1)} %get-tuple-element.192), channel_id=1, source_target_pairs={{0,4},{1,5},{2,6},{3,7},{4,0},{5,1},{6,2},{7,3},{8,12},{9,13},{10,... | collective-permute-start | bytes 1769480 | tf_op jit(solution)/shard_map/ppermute | solution.py:642
  156.5 18.0 %collective-permute-start.18 = (bf16[8,1,48,768]{3,2,1,0:T(8,128)(2,1)S(1)}, bf16[8,1,48,768]{3,2,1,0:T(8,128)(2,1)S(1)}, u32[]{:S(2)}, u32[]{:S(2)}) collective-permute-start(bf16[8,1,48,768]{3,2,1,0:T(8,128)(2,1)S(1)} %get-tuple-element.200), channel_id=1, source_target_pairs={{0,2},{1,3},{2,0},{3,1},{4,6},{5,7},{6,4},{7,5},{8,10},{9,11},{10,... | collective-permute-start | bytes 1769480 | tf_op jit(solution)/shard_map/ppermute | solution.py:642
  157.4 17.1 %collective-permute-start.19 = (bf16[4,2,48,768]{3,2,1,0:T(8,128)(2,1)S(1)}, bf16[4,2,48,768]{3,2,1,0:T(8,128)(2,1)S(1)}, u32[]{:S(2)}, u32[]{:S(2)}) collective-permute-start(bf16[4,2,48,768]{3,2,1,0:T(8,128)(2,1)S(1)} %get-tuple-element.201), channel_id=1, source_target_pairs={{0,4},{1,5},{2,6},{3,7},{4,0},{5,1},{6,2},{7,3},{8,12},{9,13},{10,... | collective-permute-start | bytes 1769480 | tf_op jit(solution)/shard_map/ppermute | solution.py:642
  158.2 11.7 %collective-permute-start.17 = (bf16[7,128,128]{2,1,0:T(8,128)(2,1)S(1)}, bf16[7,128,128]{2,1,0:T(8,128)(2,1)S(1)}, u32[]{:S(2)}, u32[]{:S(2)}) collective-permute-start(bf16[7,128,128]{2,1,0:T(8,128)(2,1)S(1)} %copy-done.73), channel_id=1, source_target_pairs={{1,0},{2,1},{3,2},{4,3},{5,4},{6,5},{7,6},{8,7},{9,8},{10,9},{11,1... | collective-permute-start | bytes 688136 | tf_op jit(solution)/shard_map/ppermute | solution.py:1013
  159.5 14.9 %collective-permute-start.16 = (bf16[7,128,128]{2,1,0:T(8,128)(2,1)S(1)}, bf16[7,128,128]{2,1,0:T(8,128)(2,1)S(1)}, u32[]{:S(2)}, u32[]{:S(2)}) collective-permute-start(bf16[7,128,128]{2,1,0:T(8,128)(2,1)S(1)} %add_convert_fusion.refs_4_), channel_id=1, source_target_pairs={{0,16},{1,17},{2,18},{3,19},{4,20},{5,21},{6,22},{7,23},{8,24},{9,... | collective-permute-start | bytes 688136 | tf_op jit(solution)/shard_map/ppermute | solution.py:642
  176.7 15.9 %collective-permute-start.23 = (bf16[16,32,768]{2,1,0:T(8,128)(2,1)S(1)}, bf16[16,32,768]{2,1,0:T(8,128)(2,1)S(1)}, u32[]{:S(2)}, u32[]{:S(2)}) collective-permute-start(bf16[16,32,768]{2,1,0:T(8,128)(2,1)S(1)} %get-tuple-element.214), channel_id=1, source_target_pairs={{0,1},{1,0},{2,3},{3,2},{4,5},{5,4},{6,7},{7,6},{8,9},{9,8},{10,11... | collective-permute-start | bytes 2359304 | tf_op jit(solution)/shard_map/ppermute | solution.py:642
  176.8 15.8 %collective-permute-start.22 = (bf16[16,32,768]{2,1,0:T(8,128)(2,1)S(1)}, bf16[16,32,768]{2,1,0:T(8,128)(2,1)S(1)}, u32[]{:S(2)}, u32[]{:S(2)}) collective-permute-start(bf16[16,32,768]{2,1,0:T(8,128)(2,1)S(1)} %get-tuple-element.211), channel_id=1, source_target_pairs={{0,1},{1,0},{2,3},{3,2},{4,5},{5,4},{6,7},{7,6},{8,9},{9,8},{10,11... | collective-permute-start | bytes 2359304 | tf_op jit(solution)/shard_map/ppermute | solution.py:642
  177.3 15.3 %collective-permute-start.20 = (bf16[4,1,96,768]{3,2,1,0:T(8,128)(2,1)S(1)}, bf16[4,1,96,768]{3,2,1,0:T(8,128)(2,1)S(1)}, u32[]{:S(2)}, u32[]{:S(2)}) collective-permute-start(bf16[4,1,96,768]{3,2,1,0:T(8,128)(2,1)S(1)} %get-tuple-element.207), channel_id=1, source_target_pairs={{0,4},{1,5},{2,6},{3,7},{4,0},{5,1},{6,2},{7,3},{8,12},{9,13},{10,... | collective-permute-start | bytes 1769480 | tf_op jit(solution)/shard_map/ppermute | solution.py:642
  177.5 15.1 %collective-permute-start.21 = (bf16[4,1,96,768]{3,2,1,0:T(8,128)(2,1)S(1)}, bf16[4,1,96,768]{3,2,1,0:T(8,128)(2,1)S(1)}, u32[]{:S(2)}, u32[]{:S(2)}) collective-permute-start(bf16[4,1,96,768]{3,2,1,0:T(8,128)(2,1)S(1)} %get-tuple-element.208), channel_id=1, source_target_pairs={{0,2},{1,3},{2,0},{3,1},{4,6},{5,7},{6,4},{7,5},{8,10},{9,11},{10,... | collective-permute-start | bytes 1769480 | tf_op jit(solution)/shard_map/ppermute | solution.py:642
  193.8 14.5 %collective-permute-start.24 = (bf16[2,1,192,768]{3,2,1,0:T(8,128)(2,1)S(1)}, bf16[2,1,192,768]{3,2,1,0:T(8,128)(2,1)S(1)}, u32[]{:S(2)}, u32[]{:S(2)}) collective-permute-start(bf16[2,1,192,768]{3,2,1,0:T(8,128)(2,1)S(1)} %get-tuple-element.221), channel_id=1, source_target_pairs={{0,8},{1,9},{2,10},{3,11},{4,12},{5,13},{6,14},{7,15},{8,0},{9,1},... | collective-permute-start | bytes 1769480 | tf_op jit(solution)/shard_map/ppermute | solution.py:642
  193.9 11.3 %collective-permute-start.25 = (bf16[8,1,32,768]{3,2,1,0:T(8,128)(2,1)S(1)}, bf16[8,1,32,768]{3,2,1,0:T(8,128)(2,1)S(1)}, u32[]{:S(2)}, u32[]{:S(2)}) collective-permute-start(bf16[8,1,32,768]{3,2,1,0:T(8,128)(2,1)S(1)} %get-tuple-element.222), channel_id=1, source_target_pairs={{0,2},{1,3},{2,0},{3,1},{4,6},{5,7},{6,4},{7,5},{8,10},{9,11},{10,... | collective-permute-start | bytes 1179656 | tf_op jit(solution)/shard_map/ppermute | solution.py:642
  196.5 11.9 %collective-permute-start.28 = (bf16[16,32,768]{2,1,0:T(8,128)(2,1)S(1)}, bf16[16,32,768]{2,1,0:T(8,128)(2,1)S(1)}, u32[]{:S(2)}, u32[]{:S(2)}) collective-permute-start(bf16[16,32,768]{2,1,0:T(8,128)(2,1)S(1)} %get-tuple-element.227), channel_id=1, source_target_pairs={{0,1},{1,0},{2,3},{3,2},{4,5},{5,4},{6,7},{7,6},{8,9},{9,8},{10,11... | collective-permute-start | bytes 2359304 | tf_op jit(solution)/shard_map/ppermute | solution.py:642
  218.9 20.0 %collective-permute-start.33 = (bf16[1,1,192,768]{3,2,1,0:T(8,128)(2,1)}, bf16[1,1,192,768]{3,2,1,0:T(8,128)(2,1)S(1)}, u32[]{:S(2)}, u32[]{:S(2)}) collective-permute-start(bf16[1,1,192,768]{3,2,1,0:T(8,128)(2,1)} %get-tuple-element.239), channel_id=1, source_target_pairs={{0,16},{1,17},{2,18},{3,19},{4,20},{5,21},{6,22},{7,23},{8,24},{9,... | collective-permute-start | bytes 884744 | tf_op jit(solution)/shard_map/ppermute | solution.py:642
  219.3 20.6 %collective-permute-start.29 = (bf16[8,1,32,768]{3,2,1,0:T(8,128)(2,1)}, bf16[8,1,32,768]{3,2,1,0:T(8,128)(2,1)S(1)}, u32[]{:S(2)}, u32[]{:S(2)}) collective-permute-start(bf16[8,1,32,768]{3,2,1,0:T(8,128)(2,1)} %copy-done.64), channel_id=1, source_target_pairs={{0,2},{1,3},{2,0},{3,1},{4,6},{5,7},{6,4},{7,5},{8,10},{9,11},{10,... | collective-permute-start | bytes 1179656 | tf_op jit(solution)/shard_map/ppermute | solution.py:642
  221.1 18.8 %collective-permute-start.30 = (bf16[4,2,32,768]{3,2,1,0:T(8,128)(2,1)}, bf16[4,2,32,768]{3,2,1,0:T(8,128)(2,1)S(1)}, u32[]{:S(2)}, u32[]{:S(2)}) collective-permute-start(bf16[4,2,32,768]{3,2,1,0:T(8,128)(2,1)} %copy-done.63), channel_id=1, source_target_pairs={{0,4},{1,5},{2,6},{3,7},{4,0},{5,1},{6,2},{7,3},{8,12},{9,13},{10,... | collective-permute-start | bytes 1179656 | tf_op jit(solution)/shard_map/ppermute | solution.py:642
  222.5 17.3 %collective-permute-start.31 = (bf16[4,1,32,768]{3,2,1,0:T(8,128)(2,1)}, bf16[4,1,32,768]{3,2,1,0:T(8,128)(2,1)S(1)}, u32[]{:S(2)}, u32[]{:S(2)}) collective-permute-start(bf16[4,1,32,768]{3,2,1,0:T(8,128)(2,1)} %copy-done.66), channel_id=1, source_target_pairs={{0,4},{1,5},{2,6},{3,7},{4,0},{5,1},{6,2},{7,3},{8,12},{9,13},{10,... | collective-permute-start | bytes 589832 | tf_op jit(solution)/shard_map/ppermute | solution.py:642
  223.1 16.7 %collective-permute-start.32 = (bf16[4,1,32,768]{3,2,1,0:T(8,128)(2,1)}, bf16[4,1,32,768]{3,2,1,0:T(8,128)(2,1)S(1)}, u32[]{:S(2)}, u32[]{:S(2)}) collective-permute-start(bf16[4,1,32,768]{3,2,1,0:T(8,128)(2,1)} %copy-done.65), channel_id=1, source_target_pairs={{0,2},{1,3},{2,0},{3,1},{4,6},{5,7},{6,4},{7,5},{8,10},{9,11},{10,... | collective-permute-start | bytes 589832 | tf_op jit(solution)/shard_map/ppermute | solution.py:642
  (91 other events, 520.7 us)

commit v2 on v1

--- a/solution.py
+++ b/solution.py
@@ -17,7 +17,7 @@
 MIB = 1 << 20
 VMEM = 60
 COST = 0.01
-FILL = 20
+FILL = 30
 AXES = ("wide", "narrow")
 
 f32 = jnp.float32
@@ -733,8 +733,11 @@
 SMEM = pl.BlockSpec(memory_space=pltpu.SMEM)
 
 
-def call(kernel, grid, in_specs, outs, out_specs, scratch, spot, args, micros, after=(), vmem=VMEM):
+def call(kernel, grid, in_specs, outs, out_specs, scratch, spot, args, micros, after=(), vmem=VMEM, hbm=()):
     nin, nafter = len(in_specs), len(after)
+    args = [
+        pltpu.with_memory_space_constraint(x, pltpu.HBM) if n in hbm else x for n, x in enumerate(args)
+    ]
 
     def body(spot_ref, *refs):
         kernel(spot_ref, *refs[:nin], *refs[nin + nafter :])
@@ -914,6 +917,7 @@
             spot,
             (act, d_outer),
             9,
+            hbm=(0,),
             after=after,
             vmem=FILL,
         )
@@ -934,6 +938,7 @@
             spot,
             (first, d_inner),
             5,
+            hbm=(1,),
             after=after,
             vmem=FILL,
         )
@@ -1091,6 +1096,7 @@
         spot,
         (d_r1, *dqs, *dks, *dvs, w_query, w_key, w_value),
         8,
+        hbm=(0, 1, 2, 3, 4, 5, 6, 7, 8, 9),
         after=done,
         vmem=FILL,
     )

time: 273 us -> 265 us (0.971)
  local copies, waits for them, and re-layouts: 38.3 us -> 19.5 us
  Pallas kernels: 142 us -> 151 us
    unnamed x150 -> x112, local copies, waits for them, and re-layouts: 32.9 us -> 14 us
    pallas_call x15, Pallas kernels: 133 us -> 142 us  [call(): pl.pallas_call(body, grid_spec=pltpu.PrefetchScalarGridSpec(num_scalar_pr...]
  transfers between devices with their start and end apart: 40 -> 40, of which waited for: 16 -> 16; matrix products, arithmetic and copies ran while one was open for 2% -> 2% of each run, Pallas kernels for 25% -> 30%
where the time goes in v2:
time: 265 us; the launch traced here: 260 us
  Pallas kernels  151 us (57%)
  waiting for transfers between devices  43.5 us (16%)
  starting transfers between devices  39.9 us (15%)
  local copies, waits for them, and re-layouts  19.5 us (7%)
  other arithmetic  4.78 us (2%)
    pallas_call x15, Pallas kernels, call(): pl.pallas_call(body, grid_spec=pltpu.PrefetchScalarGridSpec(num_scalar_pr...  142 us
    ppermute x38, waiting for transfers between devices, exchange(): return lax.ppermute(x, AXES, [(i, i ^ mask) for i in range(count)])  43.5 us
    ppermute x38, starting transfers between devices, exchange(): return lax.ppermute(x, AXES, [(i, i ^ mask) for i in range(count)])  37 us
    unnamed x112, local copies, waits for them, and re-layouts  14 us
    pallas_call x8, Pallas kernels, add_step(): pl.pallas_call(body, in_specs=[pl.BlockSpec(memory_space=pltpu.SMEM)] + [...  8.63 us
  transfers between devices with their start and end apart: 40, of which 16 were waited for; matrix products, arithmetic and copies ran while one was open for 2% of the time, Pallas kernels for 30%

profile of v2, /device:TPU:0, one launch (start us, length us, event | category | flops | bytes accessed | tf_op | source)
XLA Modules:
  0.0 260.5 jit_solution(6315812455899977688)
XLA Ops:
  1.3 12.2 %shard_map.322 = (bf16[1024,768]{1,0:T(8,128)(2,1)}, bf16[1024,768]{1,0:T(8,128)(2,1)}, bf16[1024,1536]{1,0:T(8,128)(2,1)}, f32[1024,128]{1,0:T(8,128)}, s32[102...) custom-call(s32[7]{0:T(128)} %stack.31.spot_ref, ...), custom_call_target="tpu_custom_call" | custom-call | flops 120000000 | bytes 10000 | tf_op jit(solution)/shard_map/pallas_call | solution.py:745
  16.4 3.0 %collective-permute-start.1 = (bf16[7,128,128]{2,1,0:T(8,128)(2,1)S(1)}, bf16[7,128,128]{2,1,0:T(8,128)(2,1)S(1)}, u32[]{:S(2)}, u32[]{:S(2)}) collective-permute-start(bf16[7,128,128]{2,1,0:T(8,128)(2,1)S(1)} %add_convert_fusion.7.refs_4_), channel_id=1, source_target_pairs={{0,2},{1,3},{2,0},{3,1},{4,6},{5,7},{6,4},{7,5},{8,10},{9,11},{10,... | collective-permute-start | bytes 688136 | tf_op jit(solution)/shard_map/ppermute | solution.py:642
  23.9 4.1 %shard_map.323 = (bf16[1024,768]{1,0:T(8,128)(2,1)S(1)}, bf16[1024,1536]{1,0:T(8,128)(2,1)S(1)}) custom-call(s32[7]{0:T(128)S(1)} %copy-done.43, bf16[1024,768]{1,0:T(8,128)(2,1)S(1)} %copy-done.6, bf16[768,768]{1,0:T(8,128)(2,1)S(1)} %copy-done.22, f32[13,768]{1,0:T(8,128)S(1)} %copy-done.45, f32[1024,128]{1,0:T(8,128)S(1)} %copy-done.14, ...), custom_call_target="tpu_custom_call" | custom-call | flops 40000000 | bytes 10000 | tf_op jit(solution)/shard_map/pallas_call | solution.py:745
  31.8 4.1 %shard_map.324 = (f32[1024,512]{1,0:T(8,128)S(1)}, bf16[4,4,128,128]{3,2,1,0:T(8,128)(2,1)S(1)}) custom-call(s32[7]{0:T(128)S(1)} %copy-done.43, bf16[1024,1536]{1,0:T(8,128)(2,1)S(1)} %get-tuple-element.140.refs_0_.refs_3_, bf16[1024,1536]{1,0:T(8,128)(2,1)S(1)} %copy-done.2, bf16[1024,768]{1,0:T(8,128)(2,1)S(1)} %copy-done.4, s32[1024,128]{1,0:T(8,128)S(1)} %copy-done.10, ...), custom_call_target="tpu_custom_call" | custom-call | flops 40000000 | bytes 10000 | tf_op jit(solution)/shard_map/pallas_call | solution.py:745
  39.3 4.1 %shard_map.325 = (f32[1024,512]{1,0:T(8,128)S(1)}, bf16[4,4,128,128]{3,2,1,0:T(8,128)(2,1)S(1)}) custom-call(s32[7]{0:T(128)S(1)} %copy-done.43, bf16[1024,1536]{1,0:T(8,128)(2,1)S(1)} %get-tuple-element.140.refs_0_.refs_3_, bf16[1024,1536]{1,0:T(8,128)(2,1)S(1)} %copy-done.2, bf16[1024,768]{1,0:T(8,128)(2,1)S(1)} %copy-done.4, s32[1024,128]{1,0:T(8,128)S(1)} %copy-done.10, ...), custom_call_target="tpu_custom_call" | custom-call | flops 40000000 | bytes 10000 | tf_op jit(solution)/shard_map/pallas_call | solution.py:745
  45.6 3.1 %collective-permute-start.4 = (bf16[7,128,128]{2,1,0:T(8,128)(2,1)S(1)}, bf16[7,128,128]{2,1,0:T(8,128)(2,1)S(1)}, u32[]{:S(2)}, u32[]{:S(2)}) collective-permute-start(bf16[7,128,128]{2,1,0:T(8,128)(2,1)S(1)} %add_convert_fusion.4.refs_5_), channel_id=1, source_target_pairs={{0,16},{1,17},{2,18},{3,19},{4,20},{5,21},{6,22},{7,23},{8,24},{9,... | collective-permute-start | bytes 688136 | tf_op jit(solution)/shard_map/ppermute | solution.py:642
  48.7 4.1 %shard_map.326 = (f32[1024,512]{1,0:T(8,128)S(1)}, bf16[4,4,128,128]{3,2,1,0:T(8,128)(2,1)S(1)}) custom-call(s32[7]{0:T(128)S(1)} %copy-done.43, bf16[1024,1536]{1,0:T(8,128)(2,1)S(1)} %get-tuple-element.140.refs_0_.refs_3_, bf16[1024,1536]{1,0:T(8,128)(2,1)S(1)} %copy-done.2, bf16[1024,768]{1,0:T(8,128)(2,1)S(1)} %copy-done.4, s32[1024,128]{1,0:T(8,128)S(1)} %copy-done.10, ...), custom_call_target="tpu_custom_call" | custom-call | flops 40000000 | bytes 10000 | tf_op jit(solution)/shard_map/pallas_call | solution.py:745
  54.9 5.0 %collective-permute-done.4.refs_16_ = bf16[7,128,128]{2,1,0:T(8,128)(2,1)S(1)} collective-permute-done((bf16[7,128,128]{2,1,0:T(8,128)(2,1)S(1)}, bf16[7,128,128]{2,1,0:T(8,128)(2,1)S(1)}, u32[]{:S(2)}, u32[]{:S(2)}) %collective-permute-start.4) | collective-permute-done | bytes 229408 | tf_op jit(solution)/shard_map/ppermute | solution.py:642
  60.6 51.9 %shard_map.327 = (bf16[1024,768]{1,0:T(8,128)(2,1)}, bf16[1024,768]{1,0:T(8,128)(2,1)}, bf16[1024,768]{1,0:T(8,128)(2,1)}, bf16[1024,3072]{1,0:T(8,128)(2,1)}, b...) custom-call(s32[7]{0:T(128)} %stack.31.spot_ref, ...), custom_call_target="tpu_custom_call" | custom-call | flops 500000000 | bytes 10000 | tf_op jit(solution)/shard_map/pallas_call | solution.py:745
  117.5 8.3 %shard_map.328 = (bf16[16,48,768]{2,1,0:T(8,128)(2,1)S(1)}, bf16[16,48,768]{2,1,0:T(8,128)(2,1)S(1)}, bf16[16,48,768]{2,1,0:T(8,128)(2,1)S(1)}, bf16[16,48,768]{2,1,0:T(8,128)(2,1)S(1)}) custom-call(s32[7]{0:T(128)S(1)} %copy-done.44, bf16[1024,3072]{1,0:T(8,128)(2,1)} %get-tuple-element.164.refs_0_, bf16[1024,768]{1,0:T(8,128)(2,1)S(1)} %copy-done.35, ...), custom_call_target="tpu_custom_call" | custom-call | flops 90000000 | bytes 10000 | tf_op jit(solution)/shard_map/pallas_call | solution.py:745
  127.6 5.1 %shard_map.329 = (bf16[16,48,768]{2,1,0:T(8,128)(2,1)S(1)}, bf16[16,48,768]{2,1,0:T(8,128)(2,1)S(1)}) custom-call(s32[7]{0:T(128)S(1)} %copy-done.44, bf16[1024,768]{1,0:T(8,128)(2,1)S(1)} %copy-done.19, bf16[1024,3072]{1,0:T(8,128)(2,1)} %get-tuple-element.178.refs_1_, bf16[7,128,128]{2,1,0:T(8,128)(2,1)S(1)} %add_convert_fusion.2.refs_2_), custom_call_target="tpu_custom_call" | custom-call | flops 50000000 | bytes 10000 | tf_op jit(solution)/shard_map/pallas_call | solution.py:745
  132.8 5.4 %shard_map.330 = (bf16[16,48,768]{2,1,0:T(8,128)(2,1)S(1)}, bf16[16,48,768]{2,1,0:T(8,128)(2,1)S(1)}) custom-call(s32[7]{0:T(128)S(1)} %copy-done.44, bf16[1024,768]{1,0:T(8,128)(2,1)S(1)} %copy-done.19, bf16[1024,3072]{1,0:T(8,128)(2,1)} %get-tuple-element.178.refs_1_, bf16[16,48,768]{2,1,0:T(8,128)(2,1)S(1)} %get-tuple-element.179.refs_2_), custom_call_target="tpu_custom_call" | custom-call | flops 50000000 | bytes 10000 | tf_op jit(solution)/shard_map/pallas_call | solution.py:745
  143.0 4.5 %shard_map.332.refs_12_.refs_1_ = bf16[1024,384]{1,0:T(8,128)(2,1)S(1)} custom-call(s32[7]{0:T(128)S(1)} %copy-done.44, bf16[1024,1536]{1,0:T(8,128)(2,1)S(1)} %copy-done.1, bf16[1024,1536]{1,0:T(8,128)(2,1)S(1)} %copy-done.3, bf16[1024,768]{1,0:T(8,128)(2,1)S(1)} %copy-done.5, bf16[1024,1536]{1,0:T(8,128)(2,1)S(1)} %copy-done.8, ...), custom_call_target="tpu_custom_call" | custom-call | flops 70000000 | bytes 10000 | tf_op jit(solution)/shard_map/pallas_call | solution.py:745
  147.6 2.3 collective-permute-done.13.refs_3_
  149.9 6.2 %collective-permute-done.14 = bf16[8,1,48,768]{3,2,1,0:T(8,128)(2,1)S(1)} collective-permute-done((bf16[8,1,48,768]{3,2,1,0:T(8,128)(2,1)S(1)}, bf16[8,1,48,768]{3,2,1,0:T(8,128)(2,1)S(1)}, u32[]{:S(2)}, u32[]{:S(2)}) %collective-permute-start.14) | collective-permute-done | bytes 589856 | tf_op jit(solution)/shard_map/ppermute | solution.py:642
  162.3 11.0 %shard_map.334 = (bf16[1024,384]{1,0:T(8,128)(2,1)S(1)}, bf16[16,32,768]{2,1,0:T(8,128)(2,1)S(1)}, bf16[16,32,768]{2,1,0:T(8,128)(2,1)S(1)}, bf16[16,32,768]{2,1,0:T(8,128)(2,1)}, bf16[16,32,768]{2,1,0:T(8,128)(2,1)S(1)}) custom-call(s32[7]{0:T(128)S(1)} %copy-done.44, bf16[1024,1536]{1,0:T(8,128)(2,1)S(1)} %copy-done.1, bf16[1024,1536]{1,0:T(8,128)(2,1)S(1)} %copy-done.3, ...), custom_call_target="tpu_custom_call" | custom-call | flops 90000000 | bytes 10000 | tf_op jit(solution)/shard_map/pallas_call | solution.py:745
  173.3 2.8 %collective-permute-done.16.refs_4_ = bf16[7,128,128]{2,1,0:T(8,128)(2,1)S(1)} collective-permute-done((bf16[7,128,128]{2,1,0:T(8,128)(2,1)S(1)}, bf16[7,128,128]{2,1,0:T(8,128)(2,1)S(1)}, u32[]{:S(2)}, u32[]{:S(2)}) %collective-permute-start.16) | collective-permute-done | bytes 229408 | tf_op jit(solution)/shard_map/ppermute | solution.py:642
  180.9 8.6 %shard_map.337 = (bf16[1024,384]{1,0:T(8,128)(2,1)S(1)}, bf16[1024,384]{1,0:T(8,128)(2,1)S(1)}, bf16[16,32,768]{2,1,0:T(8,128)(2,1)S(1)}, bf16[16,32,768]{2,1,0:T(8,128)(2,1)S(1)}) custom-call(s32[7]{0:T(128)S(1)} %copy-done.44, bf16[1024,1536]{1,0:T(8,128)(2,1)S(1)} %copy-done.1, bf16[1024,1536]{1,0:T(8,128)(2,1)S(1)} %copy-done.3, ...), custom_call_target="tpu_custom_call" | custom-call | flops 100000000 | bytes 10000 | tf_op jit(solution)/shard_map/pallas_call | solution.py:745
  189.6 4.6 %collective-permute-done.20.refs_9_ = bf16[4,1,96,768]{3,2,1,0:T(8,128)(2,1)S(1)} collective-permute-done((bf16[4,1,96,768]{3,2,1,0:T(8,128)(2,1)S(1)}, bf16[4,1,96,768]{3,2,1,0:T(8,128)(2,1)S(1)}, u32[]{:S(2)}, u32[]{:S(2)}) %collective-permute-start.20) | collective-permute-done | bytes 589856 | tf_op jit(solution)/shard_map/ppermute | solution.py:642
  198.9 8.8 %shard_map.339 = (bf16[1024,384]{1,0:T(8,128)(2,1)S(1)}, bf16[1024,384]{1,0:T(8,128)(2,1)S(1)}, bf16[16,32,768]{2,1,0:T(8,128)(2,1)S(1)}, bf16[16,32,768]{2,1,0:T(8,128)(2,1)S(1)}) custom-call(s32[7]{0:T(128)S(1)} %copy-done.44, bf16[1024,1536]{1,0:T(8,128)(2,1)S(1)} %copy-done.1, bf16[1024,1536]{1,0:T(8,128)(2,1)S(1)} %copy-done.3, ...), custom_call_target="tpu_custom_call" | custom-call | flops 100000000 | bytes 10000 | tf_op jit(solution)/shard_map/pallas_call | solution.py:745
  219.2 9.3 %shard_map.341.refs_8_ = bf16[1024,768]{1,0:T(8,128)(2,1)} custom-call(s32[7]{0:T(128)S(1)} %copy-done.44, f32[1024,768]{1,0:T(8,128)} %get-tuple-element.158.refs_0_, bf16[1024,384]{1,0:T(8,128)(2,1)} %copy-done.16, bf16[1024,384]{1,0:T(8,128)(2,1)} %copy-done.24, bf16[1024,384]{1,0:T(8,128)(2,1)} %copy-done.23, bf16[1024,384]{1,0:T(8,128)(2,1)} %copy-done.25, ...), custom_call_target="tpu_custom_call" | custom-call | flops 80000000 | bytes 10000 | tf_op jit(solution)/shard_map/pallas_call | solution.py:745
  235.9 3.5 %collective-permute-done.34.refs_6_ = bf16[4,1,32,768]{3,2,1,0:T(8,128)(2,1)S(1)} collective-permute-done((bf16[4,1,32,768]{3,2,1,0:T(8,128)(2,1)S(1)}, bf16[4,1,32,768]{3,2,1,0:T(8,128)(2,1)S(1)}, u32[]{:S(2)}, u32[]{:S(2)}) %collective-permute-start.34) | collective-permute-done | bytes 196640 | tf_op jit(solution)/shard_map/ppermute | solution.py:642
  245.4 2.6 %collective-permute-done.37 = bf16[1,1,64,768]{3,2,1,0:T(8,128)(2,1)S(1)} collective-permute-done((bf16[1,1,64,768]{3,2,1,0:T(8,128)(2,1)S(1)}, bf16[1,1,64,768]{3,2,1,0:T(8,128)(2,1)S(1)}, u32[]{:S(2)}, u32[]{:S(2)}) %collective-permute-start.37) | collective-permute-done | bytes 98336 | tf_op jit(solution)/shard_map/ppermute | solution.py:642
  254.0 4.4 %collective-permute-done.39 = bf16[1,1,64,768]{3,2,1,0:T(8,128)(2,1)S(1)} collective-permute-done((bf16[1,1,64,768]{3,2,1,0:T(8,128)(2,1)S(1)}, bf16[1,1,64,768]{3,2,1,0:T(8,128)(2,1)S(1)}, u32[]{:S(2)}, u32[]{:S(2)}) %collective-permute-start.39) | collective-permute-done | bytes 98336 | tf_op jit(solution)/shard_map/ppermute | solution.py:642
  (223 shorter events, 79.9 us)
Async XLA Ops:
  16.4 11.6 %collective-permute-start.1 = (bf16[7,128,128]{2,1,0:T(8,128)(2,1)S(1)}, bf16[7,128,128]{2,1,0:T(8,128)(2,1)S(1)}, u32[]{:S(2)}, u32[]{:S(2)}) collective-permute-start(bf16[7,128,128]{2,1,0:T(8,128)(2,1)S(1)} %add_convert_fusion.7.refs_4_), channel_id=1, source_target_pairs={{0,2},{1,3},{2,0},{3,1},{4,6},{5,7},{6,4},{7,5},{8,10},{9,11},{10,... | collective-permute-start | bytes 688136 | tf_op jit(solution)/shard_map/ppermute | solution.py:642
  37.6 17.3 %collective-permute-start.5 = (bf16[7,128,128]{2,1,0:T(8,128)(2,1)S(1)}, bf16[7,128,128]{2,1,0:T(8,128)(2,1)S(1)}, u32[]{:S(2)}, u32[]{:S(2)}) collective-permute-start(bf16[7,128,128]{2,1,0:T(8,128)(2,1)S(1)} %copy-done.55), channel_id=1, source_target_pairs={{0,1},{1,2},{2,3},{3,4},{4,5},{5,6},{6,7},{7,8},{8,9},{9,10},{10,1... | collective-permute-start | bytes 688136 | tf_op jit(solution)/shard_map/ppermute | solution.py:859
  45.6 14.3 %collective-permute-start.4 = (bf16[7,128,128]{2,1,0:T(8,128)(2,1)S(1)}, bf16[7,128,128]{2,1,0:T(8,128)(2,1)S(1)}, u32[]{:S(2)}, u32[]{:S(2)}) collective-permute-start(bf16[7,128,128]{2,1,0:T(8,128)(2,1)S(1)} %add_convert_fusion.4.refs_5_), channel_id=1, source_target_pairs={{0,16},{1,17},{2,18},{3,19},{4,20},{5,21},{6,22},{7,23},{8,24},{9,... | collective-permute-start | bytes 688136 | tf_op jit(solution)/shard_map/ppermute | solution.py:642
  125.9 12.3 %collective-permute-start.9 = (bf16[16,48,768]{2,1,0:T(8,128)(2,1)S(1)}, bf16[16,48,768]{2,1,0:T(8,128)(2,1)S(1)}, u32[]{:S(2)}, u32[]{:S(2)}) collective-permute-start(bf16[16,48,768]{2,1,0:T(8,128)(2,1)S(1)} %get-tuple-element.176), channel_id=1, source_target_pairs={{0,1},{1,0},{2,3},{3,2},{4,5},{5,4},{6,7},{7,6},{8,9},{9,8},{10,11... | collective-permute-start | bytes 3538952 | tf_op jit(solution)/shard_map/ppermute | solution.py:642
  126.0 12.3 %collective-permute-start.8 = (bf16[16,48,768]{2,1,0:T(8,128)(2,1)S(1)}, bf16[16,48,768]{2,1,0:T(8,128)(2,1)S(1)}, u32[]{:S(2)}, u32[]{:S(2)}) collective-permute-start(bf16[16,48,768]{2,1,0:T(8,128)(2,1)S(1)} %get-tuple-element.173), channel_id=1, source_target_pairs={{0,1},{1,0},{2,3},{3,2},{4,5},{5,4},{6,7},{7,6},{8,9},{9,8},{10,11... | collective-permute-start | bytes 3538952 | tf_op jit(solution)/shard_map/ppermute | solution.py:642
  126.5 11.7 %collective-permute-start.10 = (bf16[7,128,128]{2,1,0:T(8,128)(2,1)S(1)}, bf16[7,128,128]{2,1,0:T(8,128)(2,1)S(1)}, u32[]{:S(2)}, u32[]{:S(2)}) collective-permute-start(bf16[7,128,128]{2,1,0:T(8,128)(2,1)S(1)} %add_convert_fusion.2.refs_2_), channel_id=1, source_target_pairs={{0,4},{1,5},{2,6},{3,7},{4,0},{5,1},{6,2},{7,3},{8,12},{9,13},{10,... | collective-permute-start | bytes 688136 | tf_op jit(solution)/shard_map/ppermute | solution.py:642
  140.3 16.7 %collective-permute-start.12 = (bf16[16,48,768]{2,1,0:T(8,128)(2,1)S(1)}, bf16[16,48,768]{2,1,0:T(8,128)(2,1)S(1)}, u32[]{:S(2)}, u32[]{:S(2)}) collective-permute-start(bf16[16,48,768]{2,1,0:T(8,128)(2,1)S(1)} %get-tuple-element.190), channel_id=1, source_target_pairs={{0,1},{1,0},{2,3},{3,2},{4,5},{5,4},{6,7},{7,6},{8,9},{9,8},{10,11... | collective-permute-start | bytes 3538952 | tf_op jit(solution)/shard_map/ppermute | solution.py:642
  140.3 16.7 %collective-permute-start.11 = (bf16[16,48,768]{2,1,0:T(8,128)(2,1)S(1)}, bf16[16,48,768]{2,1,0:T(8,128)(2,1)S(1)}, u32[]{:S(2)}, u32[]{:S(2)}) collective-permute-start(bf16[16,48,768]{2,1,0:T(8,128)(2,1)S(1)} %get-tuple-element.188), channel_id=1, source_target_pairs={{0,1},{1,0},{2,3},{3,2},{4,5},{5,4},{6,7},{7,6},{8,9},{9,8},{10,11... | collective-permute-start | bytes 3538952 | tf_op jit(solution)/shard_map/ppermute | solution.py:642
  140.8 15.2 %collective-permute-start.14 = (bf16[8,1,48,768]{3,2,1,0:T(8,128)(2,1)S(1)}, bf16[8,1,48,768]{3,2,1,0:T(8,128)(2,1)S(1)}, u32[]{:S(2)}, u32[]{:S(2)}) collective-permute-start(bf16[8,1,48,768]{3,2,1,0:T(8,128)(2,1)S(1)} %get-tuple-element.191), channel_id=1, source_target_pairs={{0,2},{1,3},{2,0},{3,1},{4,6},{5,7},{6,4},{7,5},{8,10},{9,11},{10,... | collective-permute-start | bytes 1769480 | tf_op jit(solution)/shard_map/ppermute | solution.py:642
  142.1 15.0 %collective-permute-start.15 = (bf16[4,2,48,768]{3,2,1,0:T(8,128)(2,1)S(1)}, bf16[4,2,48,768]{3,2,1,0:T(8,128)(2,1)S(1)}, u32[]{:S(2)}, u32[]{:S(2)}) collective-permute-start(bf16[4,2,48,768]{3,2,1,0:T(8,128)(2,1)S(1)} %get-tuple-element.192), channel_id=1, source_target_pairs={{0,4},{1,5},{2,6},{3,7},{4,0},{5,1},{6,2},{7,3},{8,12},{9,13},{10,... | collective-permute-start | bytes 1769480 | tf_op jit(solution)/shard_map/ppermute | solution.py:642
  158.2 17.8 %collective-permute-start.18 = (bf16[8,1,48,768]{3,2,1,0:T(8,128)(2,1)S(1)}, bf16[8,1,48,768]{3,2,1,0:T(8,128)(2,1)S(1)}, u32[]{:S(2)}, u32[]{:S(2)}) collective-permute-start(bf16[8,1,48,768]{3,2,1,0:T(8,128)(2,1)S(1)} %get-tuple-element.200), channel_id=1, source_target_pairs={{0,2},{1,3},{2,0},{3,1},{4,6},{5,7},{6,4},{7,5},{8,10},{9,11},{10,... | collective-permute-start | bytes 1769480 | tf_op jit(solution)/shard_map/ppermute | solution.py:642
  159.1 17.0 %collective-permute-start.19 = (bf16[4,2,48,768]{3,2,1,0:T(8,128)(2,1)S(1)}, bf16[4,2,48,768]{3,2,1,0:T(8,128)(2,1)S(1)}, u32[]{:S(2)}, u32[]{:S(2)}) collective-permute-start(bf16[4,2,48,768]{3,2,1,0:T(8,128)(2,1)S(1)} %get-tuple-element.201), channel_id=1, source_target_pairs={{0,4},{1,5},{2,6},{3,7},{4,0},{5,1},{6,2},{7,3},{8,12},{9,13},{10,... | collective-permute-start | bytes 1769480 | tf_op jit(solution)/shard_map/ppermute | solution.py:642
  159.9 13.4 %collective-permute-start.17 = (bf16[7,128,128]{2,1,0:T(8,128)(2,1)S(1)}, bf16[7,128,128]{2,1,0:T(8,128)(2,1)S(1)}, u32[]{:S(2)}, u32[]{:S(2)}) collective-permute-start(bf16[7,128,128]{2,1,0:T(8,128)(2,1)S(1)} %copy-done.54), channel_id=1, source_target_pairs={{1,0},{2,1},{3,2},{4,3},{5,4},{6,5},{7,6},{8,7},{9,8},{10,9},{11,1... | collective-permute-start | bytes 688136 | tf_op jit(solution)/shard_map/ppermute | solution.py:1018
  161.2 14.8 %collective-permute-start.16 = (bf16[7,128,128]{2,1,0:T(8,128)(2,1)S(1)}, bf16[7,128,128]{2,1,0:T(8,128)(2,1)S(1)}, u32[]{:S(2)}, u32[]{:S(2)}) collective-permute-start(bf16[7,128,128]{2,1,0:T(8,128)(2,1)S(1)} %add_convert_fusion.refs_4_), channel_id=1, source_target_pairs={{0,16},{1,17},{2,18},{3,19},{4,20},{5,21},{6,22},{7,23},{8,24},{9,... | collective-permute-start | bytes 688136 | tf_op jit(solution)/shard_map/ppermute | solution.py:642
  178.3 15.9 %collective-permute-start.23 = (bf16[16,32,768]{2,1,0:T(8,128)(2,1)}, bf16[16,32,768]{2,1,0:T(8,128)(2,1)S(1)}, u32[]{:S(2)}, u32[]{:S(2)}) collective-permute-start(bf16[16,32,768]{2,1,0:T(8,128)(2,1)} %get-tuple-element.214), channel_id=1, source_target_pairs={{0,1},{1,0},{2,3},{3,2},{4,5},{5,4},{6,7},{7,6},{8,9},{9,8},{10,11... | collective-permute-start | bytes 2359304 | tf_op jit(solution)/shard_map/ppermute | solution.py:642
  178.4 15.8 %collective-permute-start.22 = (bf16[16,32,768]{2,1,0:T(8,128)(2,1)S(1)}, bf16[16,32,768]{2,1,0:T(8,128)(2,1)S(1)}, u32[]{:S(2)}, u32[]{:S(2)}) collective-permute-start(bf16[16,32,768]{2,1,0:T(8,128)(2,1)S(1)} %get-tuple-element.211), channel_id=1, source_target_pairs={{0,1},{1,0},{2,3},{3,2},{4,5},{5,4},{6,7},{7,6},{8,9},{9,8},{10,11... | collective-permute-start | bytes 2359304 | tf_op jit(solution)/shard_map/ppermute | solution.py:642
  178.9 15.3 %collective-permute-start.20 = (bf16[4,1,96,768]{3,2,1,0:T(8,128)(2,1)S(1)}, bf16[4,1,96,768]{3,2,1,0:T(8,128)(2,1)S(1)}, u32[]{:S(2)}, u32[]{:S(2)}) collective-permute-start(bf16[4,1,96,768]{3,2,1,0:T(8,128)(2,1)S(1)} %get-tuple-element.207), channel_id=1, source_target_pairs={{0,4},{1,5},{2,6},{3,7},{4,0},{5,1},{6,2},{7,3},{8,12},{9,13},{10,... | collective-permute-start | bytes 1769480 | tf_op jit(solution)/shard_map/ppermute | solution.py:642
  179.2 15.0 %collective-permute-start.21 = (bf16[4,1,96,768]{3,2,1,0:T(8,128)(2,1)S(1)}, bf16[4,1,96,768]{3,2,1,0:T(8,128)(2,1)S(1)}, u32[]{:S(2)}, u32[]{:S(2)}) collective-permute-start(bf16[4,1,96,768]{3,2,1,0:T(8,128)(2,1)S(1)} %get-tuple-element.208), channel_id=1, source_target_pairs={{0,2},{1,3},{2,0},{3,1},{4,6},{5,7},{6,4},{7,5},{8,10},{9,11},{10,... | collective-permute-start | bytes 1769480 | tf_op jit(solution)/shard_map/ppermute | solution.py:642
  195.4 14.5 %collective-permute-start.24 = (bf16[2,1,192,768]{3,2,1,0:T(8,128)(2,1)S(1)}, bf16[2,1,192,768]{3,2,1,0:T(8,128)(2,1)S(1)}, u32[]{:S(2)}, u32[]{:S(2)}) collective-permute-start(bf16[2,1,192,768]{3,2,1,0:T(8,128)(2,1)S(1)} %get-tuple-element.221), channel_id=1, source_target_pairs={{0,8},{1,9},{2,10},{3,11},{4,12},{5,13},{6,14},{7,15},{8,0},{9,1},... | collective-permute-start | bytes 1769480 | tf_op jit(solution)/shard_map/ppermute | solution.py:642
  214.3 16.5 %collective-permute-start.33 = (bf16[1,1,192,768]{3,2,1,0:T(8,128)(2,1)}, bf16[1,1,192,768]{3,2,1,0:T(8,128)(2,1)S(1)}, u32[]{:S(2)}, u32[]{:S(2)}) collective-permute-start(bf16[1,1,192,768]{3,2,1,0:T(8,128)(2,1)} %get-tuple-element.239), channel_id=1, source_target_pairs={{0,16},{1,17},{2,18},{3,19},{4,20},{5,21},{6,22},{7,23},{8,24},{9,... | collective-permute-start | bytes 884744 | tf_op jit(solution)/shard_map/ppermute | solution.py:642
  215.2 16.5 %collective-permute-start.29 = (bf16[8,1,32,768]{3,2,1,0:T(8,128)(2,1)}, bf16[8,1,32,768]{3,2,1,0:T(8,128)(2,1)S(1)}, u32[]{:S(2)}, u32[]{:S(2)}) collective-permute-start(bf16[8,1,32,768]{3,2,1,0:T(8,128)(2,1)} %get-tuple-element.232), channel_id=1, source_target_pairs={{0,2},{1,3},{2,0},{3,1},{4,6},{5,7},{6,4},{7,5},{8,10},{9,11},{10,... | collective-permute-start | bytes 1179656 | tf_op jit(solution)/shard_map/ppermute | solution.py:642
  216.4 15.2 %collective-permute-start.30 = (bf16[4,2,32,768]{3,2,1,0:T(8,128)(2,1)}, bf16[4,2,32,768]{3,2,1,0:T(8,128)(2,1)S(1)}, u32[]{:S(2)}, u32[]{:S(2)}) collective-permute-start(bf16[4,2,32,768]{3,2,1,0:T(8,128)(2,1)} %get-tuple-element.234), channel_id=1, source_target_pairs={{0,4},{1,5},{2,6},{3,7},{4,0},{5,1},{6,2},{7,3},{8,12},{9,13},{10,... | collective-permute-start | bytes 1179656 | tf_op jit(solution)/shard_map/ppermute | solution.py:642
  217.9 13.8 %collective-permute-start.31 = (bf16[4,1,32,768]{3,2,1,0:T(8,128)(2,1)}, bf16[4,1,32,768]{3,2,1,0:T(8,128)(2,1)S(1)}, u32[]{:S(2)}, u32[]{:S(2)}) collective-permute-start(bf16[4,1,32,768]{3,2,1,0:T(8,128)(2,1)} %get-tuple-element.236), channel_id=1, source_target_pairs={{0,4},{1,5},{2,6},{3,7},{4,0},{5,1},{6,2},{7,3},{8,12},{9,13},{10,... | collective-permute-start | bytes 589832 | tf_op jit(solution)/shard_map/ppermute | solution.py:642
  218.5 13.2 %collective-permute-start.32 = (bf16[4,1,32,768]{3,2,1,0:T(8,128)(2,1)}, bf16[4,1,32,768]{3,2,1,0:T(8,128)(2,1)S(1)}, u32[]{:S(2)}, u32[]{:S(2)}) collective-permute-start(bf16[4,1,32,768]{3,2,1,0:T(8,128)(2,1)} %get-tuple-element.238), channel_id=1, source_target_pairs={{0,2},{1,3},{2,0},{3,1},{4,6},{5,7},{6,4},{7,5},{8,10},{9,11},{10,... | collective-permute-start | bytes 589832 | tf_op jit(solution)/shard_map/ppermute | solution.py:642
  (72 other events, 612.2 us)

commit v3 on v2

--- a/solution.py
+++ b/solution.py
@@ -1000,11 +1000,13 @@
     back = joined(back, theirs[1], done)
 
     round_of(2)
+    near, *_ = lax.optimization_barrier((near, back))
+    from_next = lax.ppermute(near, AXES, [(i + 1, i) for i in range(count - 1)])
     sums["outer0"].launch(back)
     sums["outer1"].launch(back)
     done = run_inner((back,), 0)
     done = run_inner(done, 1)
-    back = joined(back, theirs[2], done + recvs("outer0", "outer1"))
+    back = joined(back, theirs[2], (from_next,) + done + recvs("outer0", "outer1"))
 
     round_of(3)
     _, done = add_step(spot, [([sums["outer0"]], b1), ([sums["outer1"]], b2)], (back,))
@@ -1014,8 +1016,6 @@
     back = joined(back, theirs[3], done + recvs("outer0", "outer1", "inner0", "inner1"))
 
     round_of(4)
-    near, *_ = lax.optimization_barrier((near, back))
-    from_next = lax.ppermute(near, AXES, [(i + 1, i) for i in range(count - 1)])
     _, done = add_step(spot, [([sums["inner0"]], b1), ([sums["inner1"]], b2)], (back,))
     done = run_query_back(1, done)
     for bit in range(5, nbits):
@@ -1098,7 +1098,7 @@
         8,
         hbm=(0, 1, 2, 3, 4, 5, 6, 7, 8, 9),
         after=done,
-        vmem=FILL,
+        vmem=18,
     )
     done = (grad_tokens, ffn.recv, q.recv, o.recv, kv0.recv, kv1.recv)
     groups = [([kv1], b2), ([kv0], b1), ([q, o], rest[0])]

time: 265 us -> 263 us (level)
  waiting for transfers between devices: 43.5 us -> 37.2 us
  starting transfers between devices: 39.9 us -> 44.3 us
    ppermute x38, waiting for transfers between devices: 43.5 us -> 37.2 us  [exchange(): return lax.ppermute(x, AXES, [(i, i ^ mask) for i in range(count)])]
    ppermute x38, starting transfers between devices: 37 us -> 41.4 us  [exchange(): return lax.ppermute(x, AXES, [(i, i ^ mask) for i in range(count)])]
    unnamed x112 -> x116, local copies, waits for them, and re-layouts: 14 us -> 14 us
  transfers between devices with their start and end apart: 40 -> 40, of which waited for: 16 -> 17; matrix products, arithmetic and copies ran while one was open for 2% -> 2% of each run, Pallas kernels for 30% -> 30%
where the time goes in v3:
time: 263 us; the launch traced here: 259 us
  Pallas kernels  151 us (57%)
  starting transfers between devices  44.3 us (17%)
  waiting for transfers between devices  37.2 us (14%)
  local copies, waits for them, and re-layouts  19.5 us (7%)
  other arithmetic  4.78 us (2%)
    pallas_call x15, Pallas kernels, call(): pl.pallas_call(body, grid_spec=pltpu.PrefetchScalarGridSpec(num_scalar_pr...  142 us
    ppermute x38, starting transfers between devices, exchange(): return lax.ppermute(x, AXES, [(i, i ^ mask) for i in range(count)])  41.4 us
    ppermute x38, waiting for transfers between devices, exchange(): return lax.ppermute(x, AXES, [(i, i ^ mask) for i in range(count)])  37.2 us
    unnamed x116, local copies, waits for them, and re-layouts  14 us
    pallas_call x8, Pallas kernels, add_step(): pl.pallas_call(body, in_specs=[pl.BlockSpec(memory_space=pltpu.SMEM)] + [...  8.63 us
  transfers between devices with their start and end apart: 40, of which 17 were waited for; matrix products, arithmetic and copies ran while one was open for 2% of the time, Pallas kernels for 30%

profile of v3, /device:TPU:0, one launch (start us, length us, event | category | flops | bytes accessed | tf_op | source)
XLA Modules:
  0.0 258.6 jit_solution(13467752938733767055)
XLA Ops:
  1.3 12.2 %shard_map.322 = (bf16[1024,768]{1,0:T(8,128)(2,1)}, bf16[1024,768]{1,0:T(8,128)(2,1)}, bf16[1024,1536]{1,0:T(8,128)(2,1)}, f32[1024,128]{1,0:T(8,128)}, s32[102...) custom-call(s32[7]{0:T(128)} %stack.31.spot_ref, ...), custom_call_target="tpu_custom_call" | custom-call | flops 120000000 | bytes 10000 | tf_op jit(solution)/shard_map/pallas_call | solution.py:745
  16.4 3.0 %collective-permute-start.1 = (bf16[7,128,128]{2,1,0:T(8,128)(2,1)S(1)}, bf16[7,128,128]{2,1,0:T(8,128)(2,1)S(1)}, u32[]{:S(2)}, u32[]{:S(2)}) collective-permute-start(bf16[7,128,128]{2,1,0:T(8,128)(2,1)S(1)} %add_convert_fusion.7.refs_4_), channel_id=1, source_target_pairs={{0,2},{1,3},{2,0},{3,1},{4,6},{5,7},{6,4},{7,5},{8,10},{9,11},{10,... | collective-permute-start | bytes 688136 | tf_op jit(solution)/shard_map/ppermute | solution.py:642
  23.9 4.1 %shard_map.323 = (bf16[1024,768]{1,0:T(8,128)(2,1)S(1)}, bf16[1024,1536]{1,0:T(8,128)(2,1)S(1)}) custom-call(s32[7]{0:T(128)S(1)} %copy-done.43, bf16[1024,768]{1,0:T(8,128)(2,1)S(1)} %copy-done.6, bf16[768,768]{1,0:T(8,128)(2,1)S(1)} %copy-done.22, f32[13,768]{1,0:T(8,128)S(1)} %copy-done.47, f32[1024,128]{1,0:T(8,128)S(1)} %copy-done.14, ...), custom_call_target="tpu_custom_call" | custom-call | flops 40000000 | bytes 10000 | tf_op jit(solution)/shard_map/pallas_call | solution.py:745
  31.8 4.1 %shard_map.324 = (f32[1024,512]{1,0:T(8,128)S(1)}, bf16[4,4,128,128]{3,2,1,0:T(8,128)(2,1)S(1)}) custom-call(s32[7]{0:T(128)S(1)} %copy-done.43, bf16[1024,1536]{1,0:T(8,128)(2,1)S(1)} %get-tuple-element.140.refs_0_.refs_3_, bf16[1024,1536]{1,0:T(8,128)(2,1)S(1)} %copy-done.2, bf16[1024,768]{1,0:T(8,128)(2,1)S(1)} %copy-done.4, s32[1024,128]{1,0:T(8,128)S(1)} %copy-done.10, ...), custom_call_target="tpu_custom_call" | custom-call | flops 40000000 | bytes 10000 | tf_op jit(solution)/shard_map/pallas_call | solution.py:745
  39.3 4.1 %shard_map.325 = (f32[1024,512]{1,0:T(8,128)S(1)}, bf16[4,4,128,128]{3,2,1,0:T(8,128)(2,1)S(1)}) custom-call(s32[7]{0:T(128)S(1)} %copy-done.43, bf16[1024,1536]{1,0:T(8,128)(2,1)S(1)} %get-tuple-element.140.refs_0_.refs_3_, bf16[1024,1536]{1,0:T(8,128)(2,1)S(1)} %copy-done.2, bf16[1024,768]{1,0:T(8,128)(2,1)S(1)} %copy-done.4, s32[1024,128]{1,0:T(8,128)S(1)} %copy-done.10, ...), custom_call_target="tpu_custom_call" | custom-call | flops 40000000 | bytes 10000 | tf_op jit(solution)/shard_map/pallas_call | solution.py:745
  45.6 3.1 %collective-permute-start.4 = (bf16[7,128,128]{2,1,0:T(8,128)(2,1)S(1)}, bf16[7,128,128]{2,1,0:T(8,128)(2,1)S(1)}, u32[]{:S(2)}, u32[]{:S(2)}) collective-permute-start(bf16[7,128,128]{2,1,0:T(8,128)(2,1)S(1)} %add_convert_fusion.4.refs_5_), channel_id=1, source_target_pairs={{0,16},{1,17},{2,18},{3,19},{4,20},{5,21},{6,22},{7,23},{8,24},{9,... | collective-permute-start | bytes 688136 | tf_op jit(solution)/shard_map/ppermute | solution.py:642
  48.7 4.1 %shard_map.326 = (f32[1024,512]{1,0:T(8,128)S(1)}, bf16[4,4,128,128]{3,2,1,0:T(8,128)(2,1)S(1)}) custom-call(s32[7]{0:T(128)S(1)} %copy-done.43, bf16[1024,1536]{1,0:T(8,128)(2,1)S(1)} %get-tuple-element.140.refs_0_.refs_3_, bf16[1024,1536]{1,0:T(8,128)(2,1)S(1)} %copy-done.2, bf16[1024,768]{1,0:T(8,128)(2,1)S(1)} %copy-done.4, s32[1024,128]{1,0:T(8,128)S(1)} %copy-done.10, ...), custom_call_target="tpu_custom_call" | custom-call | flops 40000000 | bytes 10000 | tf_op jit(solution)/shard_map/pallas_call | solution.py:745
  54.9 5.0 %collective-permute-done.4.refs_16_ = bf16[7,128,128]{2,1,0:T(8,128)(2,1)S(1)} collective-permute-done((bf16[7,128,128]{2,1,0:T(8,128)(2,1)S(1)}, bf16[7,128,128]{2,1,0:T(8,128)(2,1)S(1)}, u32[]{:S(2)}, u32[]{:S(2)}) %collective-permute-start.4) | collective-permute-done | bytes 229408 | tf_op jit(solution)/shard_map/ppermute | solution.py:642
  60.7 51.9 %shard_map.327 = (bf16[1024,768]{1,0:T(8,128)(2,1)}, bf16[1024,768]{1,0:T(8,128)(2,1)}, bf16[1024,768]{1,0:T(8,128)(2,1)}, bf16[1024,3072]{1,0:T(8,128)(2,1)}, b...) custom-call(s32[7]{0:T(128)} %stack.31.spot_ref, ...), custom_call_target="tpu_custom_call" | custom-call | flops 500000000 | bytes 10000 | tf_op jit(solution)/shard_map/pallas_call | solution.py:745
  117.6 8.3 %shard_map.328 = (bf16[16,48,768]{2,1,0:T(8,128)(2,1)S(1)}, bf16[16,48,768]{2,1,0:T(8,128)(2,1)S(1)}, bf16[16,48,768]{2,1,0:T(8,128)(2,1)S(1)}, bf16[16,48,768]{2,1,0:T(8,128)(2,1)S(1)}) custom-call(s32[7]{0:T(128)S(1)} %copy-done.44, bf16[1024,3072]{1,0:T(8,128)(2,1)} %get-tuple-element.164.refs_0_, bf16[1024,768]{1,0:T(8,128)(2,1)S(1)} %copy-done.35, ...), custom_call_target="tpu_custom_call" | custom-call | flops 90000000 | bytes 10000 | tf_op jit(solution)/shard_map/pallas_call | solution.py:745
  127.8 3.1 %collective-permute-start.10 = (bf16[7,128,128]{2,1,0:T(8,128)(2,1)S(1)}, bf16[7,128,128]{2,1,0:T(8,128)(2,1)S(1)}, u32[]{:S(2)}, u32[]{:S(2)}) collective-permute-start(bf16[7,128,128]{2,1,0:T(8,128)(2,1)S(1)} %add_convert_fusion.2.refs_2_), channel_id=1, source_target_pairs={{0,4},{1,5},{2,6},{3,7},{4,0},{5,1},{6,2},{7,3},{8,12},{9,13},{10,... | collective-permute-start | bytes 688136 | tf_op jit(solution)/shard_map/ppermute | solution.py:642
  130.9 5.1 %shard_map.329 = (bf16[16,48,768]{2,1,0:T(8,128)(2,1)S(1)}, bf16[16,48,768]{2,1,0:T(8,128)(2,1)S(1)}) custom-call(s32[7]{0:T(128)S(1)} %copy-done.44, bf16[1024,768]{1,0:T(8,128)(2,1)S(1)} %copy-done.19, bf16[1024,3072]{1,0:T(8,128)(2,1)} %get-tuple-element.180.refs_1_, bf16[7,128,128]{2,1,0:T(8,128)(2,1)S(1)} %add_convert_fusion.2.refs_2_), custom_call_target="tpu_custom_call" | custom-call | flops 50000000 | bytes 10000 | tf_op jit(solution)/shard_map/pallas_call | solution.py:745
  136.1 5.4 %shard_map.330 = (bf16[16,48,768]{2,1,0:T(8,128)(2,1)S(1)}, bf16[16,48,768]{2,1,0:T(8,128)(2,1)S(1)}) custom-call(s32[7]{0:T(128)S(1)} %copy-done.44, bf16[1024,768]{1,0:T(8,128)(2,1)S(1)} %copy-done.19, bf16[1024,3072]{1,0:T(8,128)(2,1)} %get-tuple-element.180.refs_1_, bf16[16,48,768]{2,1,0:T(8,128)(2,1)S(1)} %get-tuple-element.181.refs_2_), custom_call_target="tpu_custom_call" | custom-call | flops 50000000 | bytes 10000 | tf_op jit(solution)/shard_map/pallas_call | solution.py:745
  146.8 4.5 %shard_map.332.refs_12_.refs_1_ = bf16[1024,384]{1,0:T(8,128)(2,1)S(1)} custom-call(s32[7]{0:T(128)S(1)} %copy-done.44, bf16[1024,1536]{1,0:T(8,128)(2,1)S(1)} %copy-done.1, bf16[1024,1536]{1,0:T(8,128)(2,1)S(1)} %copy-done.3, bf16[1024,768]{1,0:T(8,128)(2,1)S(1)} %copy-done.5, bf16[1024,1536]{1,0:T(8,128)(2,1)S(1)} %copy-done.8, ...), custom_call_target="tpu_custom_call" | custom-call | flops 70000000 | bytes 10000 | tf_op jit(solution)/shard_map/pallas_call | solution.py:745
  152.4 7.0 %collective-permute-done.15 = bf16[8,1,48,768]{3,2,1,0:T(8,128)(2,1)S(1)} collective-permute-done((bf16[8,1,48,768]{3,2,1,0:T(8,128)(2,1)S(1)}, bf16[8,1,48,768]{3,2,1,0:T(8,128)(2,1)S(1)}, u32[]{:S(2)}, u32[]{:S(2)}) %collective-permute-start.15) | collective-permute-done | bytes 589856 | tf_op jit(solution)/shard_map/ppermute | solution.py:642
  164.2 11.0 %shard_map.334 = (bf16[1024,384]{1,0:T(8,128)(2,1)S(1)}, bf16[16,32,768]{2,1,0:T(8,128)(2,1)S(1)}, bf16[16,32,768]{2,1,0:T(8,128)(2,1)S(1)}, bf16[16,32,768]{2,1,0:T(8,128)(2,1)}, bf16[16,32,768]{2,1,0:T(8,128)(2,1)S(1)}) custom-call(s32[7]{0:T(128)S(1)} %copy-done.44, bf16[1024,1536]{1,0:T(8,128)(2,1)S(1)} %copy-done.1, bf16[1024,1536]{1,0:T(8,128)(2,1)S(1)} %copy-done.3, ...), custom_call_target="tpu_custom_call" | custom-call | flops 90000000 | bytes 10000 | tf_op jit(solution)/shard_map/pallas_call | solution.py:745
  180.3 8.6 %shard_map.337 = (bf16[1024,384]{1,0:T(8,128)(2,1)S(1)}, bf16[1024,384]{1,0:T(8,128)(2,1)S(1)}, bf16[16,32,768]{2,1,0:T(8,128)(2,1)S(1)}, bf16[16,32,768]{2,1,0:T(8,128)(2,1)S(1)}) custom-call(s32[7]{0:T(128)S(1)} %copy-done.44, bf16[1024,1536]{1,0:T(8,128)(2,1)S(1)} %copy-done.1, bf16[1024,1536]{1,0:T(8,128)(2,1)S(1)} %copy-done.3, ...), custom_call_target="tpu_custom_call" | custom-call | flops 100000000 | bytes 10000 | tf_op jit(solution)/shard_map/pallas_call | solution.py:745
  188.9 5.3 %collective-permute-done.20.refs_9_ = bf16[4,1,96,768]{3,2,1,0:T(8,128)(2,1)S(1)} collective-permute-done((bf16[4,1,96,768]{3,2,1,0:T(8,128)(2,1)S(1)}, bf16[4,1,96,768]{3,2,1,0:T(8,128)(2,1)S(1)}, u32[]{:S(2)}, u32[]{:S(2)}) %collective-permute-start.20) | collective-permute-done | bytes 589856 | tf_op jit(solution)/shard_map/ppermute | solution.py:642
  199.0 8.8 %shard_map.339 = (bf16[1024,384]{1,0:T(8,128)(2,1)S(1)}, bf16[1024,384]{1,0:T(8,128)(2,1)S(1)}, bf16[16,32,768]{2,1,0:T(8,128)(2,1)S(1)}, bf16[16,32,768]{2,1,0:T(8,128)(2,1)S(1)}) custom-call(s32[7]{0:T(128)S(1)} %copy-done.44, bf16[1024,1536]{1,0:T(8,128)(2,1)S(1)} %copy-done.1, bf16[1024,1536]{1,0:T(8,128)(2,1)S(1)} %copy-done.3, ...), custom_call_target="tpu_custom_call" | custom-call | flops 100000000 | bytes 10000 | tf_op jit(solution)/shard_map/pallas_call | solution.py:745
  207.9 2.4 collective-permute-done.24.refs_11_
  210.3 2.3 collective-permute-done.27
  220.2 9.3 %shard_map.341.refs_8_ = bf16[1024,768]{1,0:T(8,128)(2,1)} custom-call(s32[7]{0:T(128)S(1)} %copy-done.44, f32[1024,768]{1,0:T(8,128)} %get-tuple-element.158.refs_0_, bf16[1024,384]{1,0:T(8,128)(2,1)} %copy-done.16, bf16[1024,384]{1,0:T(8,128)(2,1)} %copy-done.24, bf16[1024,384]{1,0:T(8,128)(2,1)} %copy-done.23, bf16[1024,384]{1,0:T(8,128)(2,1)} %copy-done.25, ...), custom_call_target="tpu_custom_call" | custom-call | flops 80000000 | bytes 10000 | tf_op jit(solution)/shard_map/pallas_call | solution.py:745
  250.9 2.5 collective-permute-start.39
  254.1 2.5 collective-permute-done.39
  (227 shorter events, 79.4 us)
Async XLA Ops:
  16.4 11.6 %collective-permute-start.1 = (bf16[7,128,128]{2,1,0:T(8,128)(2,1)S(1)}, bf16[7,128,128]{2,1,0:T(8,128)(2,1)S(1)}, u32[]{:S(2)}, u32[]{:S(2)}) collective-permute-start(bf16[7,128,128]{2,1,0:T(8,128)(2,1)S(1)} %add_convert_fusion.7.refs_4_), channel_id=1, source_target_pairs={{0,2},{1,3},{2,0},{3,1},{4,6},{5,7},{6,4},{7,5},{8,10},{9,11},{10,... | collective-permute-start | bytes 688136 | tf_op jit(solution)/shard_map/ppermute | solution.py:642
  37.6 17.3 %collective-permute-start.5 = (bf16[7,128,128]{2,1,0:T(8,128)(2,1)S(1)}, bf16[7,128,128]{2,1,0:T(8,128)(2,1)S(1)}, u32[]{:S(2)}, u32[]{:S(2)}) collective-permute-start(bf16[7,128,128]{2,1,0:T(8,128)(2,1)S(1)} %copy-done.57), channel_id=1, source_target_pairs={{0,1},{1,2},{2,3},{3,4},{4,5},{5,6},{6,7},{7,8},{8,9},{9,10},{10,1... | collective-permute-start | bytes 688136 | tf_op jit(solution)/shard_map/ppermute | solution.py:859
  45.6 14.3 %collective-permute-start.4 = (bf16[7,128,128]{2,1,0:T(8,128)(2,1)S(1)}, bf16[7,128,128]{2,1,0:T(8,128)(2,1)S(1)}, u32[]{:S(2)}, u32[]{:S(2)}) collective-permute-start(bf16[7,128,128]{2,1,0:T(8,128)(2,1)S(1)} %add_convert_fusion.4.refs_5_), channel_id=1, source_target_pairs={{0,16},{1,17},{2,18},{3,19},{4,20},{5,21},{6,22},{7,23},{8,24},{9,... | collective-permute-start | bytes 688136 | tf_op jit(solution)/shard_map/ppermute | solution.py:642
  125.9 15.6 %collective-permute-start.9 = (bf16[16,48,768]{2,1,0:T(8,128)(2,1)S(1)}, bf16[16,48,768]{2,1,0:T(8,128)(2,1)S(1)}, u32[]{:S(2)}, u32[]{:S(2)}) collective-permute-start(bf16[16,48,768]{2,1,0:T(8,128)(2,1)S(1)} %get-tuple-element.176), channel_id=1, source_target_pairs={{0,1},{1,0},{2,3},{3,2},{4,5},{5,4},{6,7},{7,6},{8,9},{9,8},{10,11... | collective-permute-start | bytes 3538952 | tf_op jit(solution)/shard_map/ppermute | solution.py:642
  126.0 15.5 %collective-permute-start.8 = (bf16[16,48,768]{2,1,0:T(8,128)(2,1)S(1)}, bf16[16,48,768]{2,1,0:T(8,128)(2,1)S(1)}, u32[]{:S(2)}, u32[]{:S(2)}) collective-permute-start(bf16[16,48,768]{2,1,0:T(8,128)(2,1)S(1)} %get-tuple-element.173), channel_id=1, source_target_pairs={{0,1},{1,0},{2,3},{3,2},{4,5},{5,4},{6,7},{7,6},{8,9},{9,8},{10,11... | collective-permute-start | bytes 3538952 | tf_op jit(solution)/shard_map/ppermute | solution.py:642
  126.5 15.0 %collective-permute-start.11 = (bf16[7,128,128]{2,1,0:T(8,128)(2,1)S(1)}, bf16[7,128,128]{2,1,0:T(8,128)(2,1)S(1)}, u32[]{:S(2)}, u32[]{:S(2)}) collective-permute-start(bf16[7,128,128]{2,1,0:T(8,128)(2,1)S(1)} %copy-done.56), channel_id=1, source_target_pairs={{1,0},{2,1},{3,2},{4,3},{5,4},{6,5},{7,6},{8,7},{9,8},{10,9},{11,1... | collective-permute-start | bytes 688136 | tf_op jit(solution)/shard_map/ppermute | solution.py:1004
  127.8 13.7 %collective-permute-start.10 = (bf16[7,128,128]{2,1,0:T(8,128)(2,1)S(1)}, bf16[7,128,128]{2,1,0:T(8,128)(2,1)S(1)}, u32[]{:S(2)}, u32[]{:S(2)}) collective-permute-start(bf16[7,128,128]{2,1,0:T(8,128)(2,1)S(1)} %add_convert_fusion.2.refs_2_), channel_id=1, source_target_pairs={{0,4},{1,5},{2,6},{3,7},{4,0},{5,1},{6,2},{7,3},{8,12},{9,13},{10,... | collective-permute-start | bytes 688136 | tf_op jit(solution)/shard_map/ppermute | solution.py:642
  143.6 15.9 %collective-permute-start.13 = (bf16[16,48,768]{2,1,0:T(8,128)(2,1)S(1)}, bf16[16,48,768]{2,1,0:T(8,128)(2,1)S(1)}, u32[]{:S(2)}, u32[]{:S(2)}) collective-permute-start(bf16[16,48,768]{2,1,0:T(8,128)(2,1)S(1)} %get-tuple-element.192), channel_id=1, source_target_pairs={{0,1},{1,0},{2,3},{3,2},{4,5},{5,4},{6,7},{7,6},{8,9},{9,8},{10,11... | collective-permute-start | bytes 3538952 | tf_op jit(solution)/shard_map/ppermute | solution.py:642
  143.6 15.9 %collective-permute-start.12 = (bf16[16,48,768]{2,1,0:T(8,128)(2,1)S(1)}, bf16[16,48,768]{2,1,0:T(8,128)(2,1)S(1)}, u32[]{:S(2)}, u32[]{:S(2)}) collective-permute-start(bf16[16,48,768]{2,1,0:T(8,128)(2,1)S(1)} %get-tuple-element.190), channel_id=1, source_target_pairs={{0,1},{1,0},{2,3},{3,2},{4,5},{5,4},{6,7},{7,6},{8,9},{9,8},{10,11... | collective-permute-start | bytes 3538952 | tf_op jit(solution)/shard_map/ppermute | solution.py:642
  144.1 15.2 %collective-permute-start.15 = (bf16[8,1,48,768]{3,2,1,0:T(8,128)(2,1)S(1)}, bf16[8,1,48,768]{3,2,1,0:T(8,128)(2,1)S(1)}, u32[]{:S(2)}, u32[]{:S(2)}) collective-permute-start(bf16[8,1,48,768]{3,2,1,0:T(8,128)(2,1)S(1)} %get-tuple-element.193), channel_id=1, source_target_pairs={{0,2},{1,3},{2,0},{3,1},{4,6},{5,7},{6,4},{7,5},{8,10},{9,11},{10,... | collective-permute-start | bytes 1769480 | tf_op jit(solution)/shard_map/ppermute | solution.py:642
  144.5 15.0 %collective-permute-start.16 = (bf16[4,2,48,768]{3,2,1,0:T(8,128)(2,1)S(1)}, bf16[4,2,48,768]{3,2,1,0:T(8,128)(2,1)S(1)}, u32[]{:S(2)}, u32[]{:S(2)}) collective-permute-start(bf16[4,2,48,768]{3,2,1,0:T(8,128)(2,1)S(1)} %get-tuple-element.194), channel_id=1, source_target_pairs={{0,4},{1,5},{2,6},{3,7},{4,0},{5,1},{6,2},{7,3},{8,12},{9,13},{10,... | collective-permute-start | bytes 1769480 | tf_op jit(solution)/shard_map/ppermute | solution.py:642
  160.7 14.5 %collective-permute-start.18 = (bf16[8,1,48,768]{3,2,1,0:T(8,128)(2,1)S(1)}, bf16[8,1,48,768]{3,2,1,0:T(8,128)(2,1)S(1)}, u32[]{:S(2)}, u32[]{:S(2)}) collective-permute-start(bf16[8,1,48,768]{3,2,1,0:T(8,128)(2,1)S(1)} %get-tuple-element.200), channel_id=1, source_target_pairs={{0,2},{1,3},{2,0},{3,1},{4,6},{5,7},{6,4},{7,5},{8,10},{9,11},{10,... | collective-permute-start | bytes 1769480 | tf_op jit(solution)/shard_map/ppermute | solution.py:642
  162.3 13.8 %collective-permute-start.19 = (bf16[4,2,48,768]{3,2,1,0:T(8,128)(2,1)S(1)}, bf16[4,2,48,768]{3,2,1,0:T(8,128)(2,1)S(1)}, u32[]{:S(2)}, u32[]{:S(2)}) collective-permute-start(bf16[4,2,48,768]{3,2,1,0:T(8,128)(2,1)S(1)} %get-tuple-element.201), channel_id=1, source_target_pairs={{0,4},{1,5},{2,6},{3,7},{4,0},{5,1},{6,2},{7,3},{8,12},{9,13},{10,... | collective-permute-start | bytes 1769480 | tf_op jit(solution)/shard_map/ppermute | solution.py:642
  162.6 12.5 %collective-permute-start.17 = (bf16[7,128,128]{2,1,0:T(8,128)(2,1)S(1)}, bf16[7,128,128]{2,1,0:T(8,128)(2,1)S(1)}, u32[]{:S(2)}, u32[]{:S(2)}) collective-permute-start(bf16[7,128,128]{2,1,0:T(8,128)(2,1)S(1)} %add_convert_fusion.refs_4_), channel_id=1, source_target_pairs={{0,16},{1,17},{2,18},{3,19},{4,20},{5,21},{6,22},{7,23},{8,24},{9,... | collective-permute-start | bytes 688136 | tf_op jit(solution)/shard_map/ppermute | solution.py:642
  178.4 16.2 %collective-permute-start.23 = (bf16[16,32,768]{2,1,0:T(8,128)(2,1)}, bf16[16,32,768]{2,1,0:T(8,128)(2,1)S(1)}, u32[]{:S(2)}, u32[]{:S(2)}) collective-permute-start(bf16[16,32,768]{2,1,0:T(8,128)(2,1)} %get-tuple-element.214), channel_id=1, source_target_pairs={{0,1},{1,0},{2,3},{3,2},{4,5},{5,4},{6,7},{7,6},{8,9},{9,8},{10,11... | collective-permute-start | bytes 2359304 | tf_op jit(solution)/shard_map/ppermute | solution.py:642
  178.4 16.1 %collective-permute-start.22 = (bf16[16,32,768]{2,1,0:T(8,128)(2,1)S(1)}, bf16[16,32,768]{2,1,0:T(8,128)(2,1)S(1)}, u32[]{:S(2)}, u32[]{:S(2)}) collective-permute-start(bf16[16,32,768]{2,1,0:T(8,128)(2,1)S(1)} %get-tuple-element.211), channel_id=1, source_target_pairs={{0,1},{1,0},{2,3},{3,2},{4,5},{5,4},{6,7},{7,6},{8,9},{9,8},{10,11... | collective-permute-start | bytes 2359304 | tf_op jit(solution)/shard_map/ppermute | solution.py:642
  178.9 15.3 %collective-permute-start.20 = (bf16[4,1,96,768]{3,2,1,0:T(8,128)(2,1)S(1)}, bf16[4,1,96,768]{3,2,1,0:T(8,128)(2,1)S(1)}, u32[]{:S(2)}, u32[]{:S(2)}) collective-permute-start(bf16[4,1,96,768]{3,2,1,0:T(8,128)(2,1)S(1)} %get-tuple-element.207), channel_id=1, source_target_pairs={{0,4},{1,5},{2,6},{3,7},{4,0},{5,1},{6,2},{7,3},{8,12},{9,13},{10,... | collective-permute-start | bytes 1769480 | tf_op jit(solution)/shard_map/ppermute | solution.py:642
  179.5 15.0 %collective-permute-start.21 = (bf16[4,1,96,768]{3,2,1,0:T(8,128)(2,1)S(1)}, bf16[4,1,96,768]{3,2,1,0:T(8,128)(2,1)S(1)}, u32[]{:S(2)}, u32[]{:S(2)}) collective-permute-start(bf16[4,1,96,768]{3,2,1,0:T(8,128)(2,1)S(1)} %get-tuple-element.208), channel_id=1, source_target_pairs={{0,2},{1,3},{2,0},{3,1},{4,6},{5,7},{6,4},{7,5},{8,10},{9,11},{10,... | collective-permute-start | bytes 1769480 | tf_op jit(solution)/shard_map/ppermute | solution.py:642
  195.7 14.5 %collective-permute-start.24 = (bf16[2,1,192,768]{3,2,1,0:T(8,128)(2,1)S(1)}, bf16[2,1,192,768]{3,2,1,0:T(8,128)(2,1)S(1)}, u32[]{:S(2)}, u32[]{:S(2)}) collective-permute-start(bf16[2,1,192,768]{3,2,1,0:T(8,128)(2,1)S(1)} %get-tuple-element.221), channel_id=1, source_target_pairs={{0,8},{1,9},{2,10},{3,11},{4,12},{5,13},{6,14},{7,15},{8,0},{9,1},... | collective-permute-start | bytes 1769480 | tf_op jit(solution)/shard_map/ppermute | solution.py:642
  214.6 16.5 %collective-permute-start.33 = (bf16[1,1,192,768]{3,2,1,0:T(8,128)(2,1)}, bf16[1,1,192,768]{3,2,1,0:T(8,128)(2,1)S(1)}, u32[]{:S(2)}, u32[]{:S(2)}) collective-permute-start(bf16[1,1,192,768]{3,2,1,0:T(8,128)(2,1)} %get-tuple-element.239), channel_id=1, source_target_pairs={{0,16},{1,17},{2,18},{3,19},{4,20},{5,21},{6,22},{7,23},{8,24},{9,... | collective-permute-start | bytes 884744 | tf_op jit(solution)/shard_map/ppermute | solution.py:642
  216.2 15.8 %collective-permute-start.29 = (bf16[8,1,32,768]{3,2,1,0:T(8,128)(2,1)}, bf16[8,1,32,768]{3,2,1,0:T(8,128)(2,1)S(1)}, u32[]{:S(2)}, u32[]{:S(2)}) collective-permute-start(bf16[8,1,32,768]{3,2,1,0:T(8,128)(2,1)} %get-tuple-element.232), channel_id=1, source_target_pairs={{0,2},{1,3},{2,0},{3,1},{4,6},{5,7},{6,4},{7,5},{8,10},{9,11},{10,... | collective-permute-start | bytes 1179656 | tf_op jit(solution)/shard_map/ppermute | solution.py:642
  216.6 15.4 %collective-permute-start.30 = (bf16[4,2,32,768]{3,2,1,0:T(8,128)(2,1)}, bf16[4,2,32,768]{3,2,1,0:T(8,128)(2,1)S(1)}, u32[]{:S(2)}, u32[]{:S(2)}) collective-permute-start(bf16[4,2,32,768]{3,2,1,0:T(8,128)(2,1)} %get-tuple-element.234), channel_id=1, source_target_pairs={{0,4},{1,5},{2,6},{3,7},{4,0},{5,1},{6,2},{7,3},{8,12},{9,13},{10,... | collective-permute-start | bytes 1179656 | tf_op jit(solution)/shard_map/ppermute | solution.py:642
  217.8 14.1 %collective-permute-start.31 = (bf16[4,1,32,768]{3,2,1,0:T(8,128)(2,1)}, bf16[4,1,32,768]{3,2,1,0:T(8,128)(2,1)S(1)}, u32[]{:S(2)}, u32[]{:S(2)}) collective-permute-start(bf16[4,1,32,768]{3,2,1,0:T(8,128)(2,1)} %get-tuple-element.236), channel_id=1, source_target_pairs={{0,4},{1,5},{2,6},{3,7},{4,0},{5,1},{6,2},{7,3},{8,12},{9,13},{10,... | collective-permute-start | bytes 589832 | tf_op jit(solution)/shard_map/ppermute | solution.py:642
  218.6 13.3 %collective-permute-start.32 = (bf16[4,1,32,768]{3,2,1,0:T(8,128)(2,1)}, bf16[4,1,32,768]{3,2,1,0:T(8,128)(2,1)S(1)}, u32[]{:S(2)}, u32[]{:S(2)}) collective-permute-start(bf16[4,1,32,768]{3,2,1,0:T(8,128)(2,1)} %get-tuple-element.238), channel_id=1, source_target_pairs={{0,2},{1,3},{2,0},{3,1},{4,6},{5,7},{6,4},{7,5},{8,10},{9,11},{10,... | collective-permute-start | bytes 589832 | tf_op jit(solution)/shard_map/ppermute | solution.py:642
  (74 other events, 628.6 us)

commit v4 on v3

--- a/solution.py
+++ b/solution.py
@@ -244,17 +244,19 @@
 
     for g in range(pairs_of(v_ref.shape[1])):
         vs = extended(v_ref[:, g * LANES : (g + 1) * LANES], lo)
-        for s in range(2):
-            h = 2 * g + s
-            cols = slice(h * LANES, (h + 1) * LANES)
-            qf, kf, v = qf_ref[:, cols], kf_ref[:, cols], vs[s]
-            probs = jnp.where(mask, nt(qf, kf), 0.0).astype(bf16)
-            held = local[h].astype(bf16)
-            kept_ref[0, h] = held
-            o_ref[:, cols] = nn(probs, v) + jnp.where(carried, nn(qf, held), 0.0)
-            local[h] = jnp.where(keep, local[h], 0.0) + tn(
-                jnp.where(closing, kf, jnp.zeros_like(kf)), v
-            )
+        two = range(2)
+        cols = [slice((2 * g + s) * LANES, (2 * g + s + 1) * LANES) for s in two]
+        qf, kf = [qf_ref[:, c] for c in cols], [kf_ref[:, c] for c in cols]
+        probs = [nt(qf[s], kf[s]) for s in two]
+        probs = [jnp.where(mask, p, 0.0).astype(bf16) for p in probs]
+        before = [local[2 * g + s] for s in two]
+        held = [b.astype(bf16) for b in before]
+        more = [tn(jnp.where(closing, kf[s], jnp.zeros_like(kf[s])), vs[s]) for s in two]
+        out = [nn(probs[s], vs[s]) + jnp.where(carried, nn(qf[s], held[s]), 0.0) for s in two]
+        for s in two:
+            kept_ref[0, 2 * g + s] = held[s]
+            o_ref[:, cols[s]] = out[s]
+            local[2 * g + s] = jnp.where(keep, before[s], 0.0) + more[s]
 
 
 def gelu_and_slope(u):

time: 263 us -> 262 us (level)
  transfers between devices with their start and end apart: 40 -> 40, of which waited for: 17 -> 18; matrix products, arithmetic and copies ran while one was open for 2% -> 2% of each run, Pallas kernels for 30% -> 29%
where the time goes in v4:
time: 262 us; the launch traced here: 258 us
  Pallas kernels  149 us (57%)
  starting transfers between devices  44.2 us (17%)
  waiting for transfers between devices  38.5 us (15%)
  local copies, waits for them, and re-layouts  19.5 us (7%)
  other arithmetic  4.78 us (2%)
    pallas_call x15, Pallas kernels, call(): pl.pallas_call(body, grid_spec=pltpu.PrefetchScalarGridSpec(num_scalar_pr...  140 us
    ppermute x38, starting transfers between devices, exchange(): return lax.ppermute(x, AXES, [(i, i ^ mask) for i in range(count)])  41.4 us
    ppermute x38, waiting for transfers between devices, exchange(): return lax.ppermute(x, AXES, [(i, i ^ mask) for i in range(count)])  38.5 us
    unnamed x116, local copies, waits for them, and re-layouts  14 us
    pallas_call x8, Pallas kernels, add_step(): pl.pallas_call(body, in_specs=[pl.BlockSpec(memory_space=pltpu.SMEM)] + [...  8.63 us
  transfers between devices with their start and end apart: 40, of which 18 were waited for; matrix products, arithmetic and copies ran while one was open for 2% of the time, Pallas kernels for 29%

profile of v4, /device:TPU:0, one launch (start us, length us, event | category | flops | bytes accessed | tf_op | source)
XLA Modules:
  0.0 257.7 jit_solution(17328059049204895079)
XLA Ops:
  1.3 12.2 %shard_map.322 = (bf16[1024,768]{1,0:T(8,128)(2,1)}, bf16[1024,768]{1,0:T(8,128)(2,1)}, bf16[1024,1536]{1,0:T(8,128)(2,1)}, f32[1024,128]{1,0:T(8,128)}, s32[102...) custom-call(s32[7]{0:T(128)} %stack.31.spot_ref, ...), custom_call_target="tpu_custom_call" | custom-call | flops 120000000 | bytes 10000 | tf_op jit(solution)/shard_map/pallas_call | solution.py:747
  16.4 3.0 %collective-permute-start.1 = (bf16[7,128,128]{2,1,0:T(8,128)(2,1)S(1)}, bf16[7,128,128]{2,1,0:T(8,128)(2,1)S(1)}, u32[]{:S(2)}, u32[]{:S(2)}) collective-permute-start(bf16[7,128,128]{2,1,0:T(8,128)(2,1)S(1)} %add_convert_fusion.7.refs_4_), channel_id=1, source_target_pairs={{0,2},{1,3},{2,0},{3,1},{4,6},{5,7},{6,4},{7,5},{8,10},{9,11},{10,... | collective-permute-start | bytes 688136 | tf_op jit(solution)/shard_map/ppermute | solution.py:644
  23.9 4.1 %shard_map.323 = (bf16[1024,768]{1,0:T(8,128)(2,1)S(1)}, bf16[1024,1536]{1,0:T(8,128)(2,1)S(1)}) custom-call(s32[7]{0:T(128)S(1)} %copy-done.43, bf16[1024,768]{1,0:T(8,128)(2,1)S(1)} %copy-done.6, bf16[768,768]{1,0:T(8,128)(2,1)S(1)} %copy-done.22, f32[13,768]{1,0:T(8,128)S(1)} %copy-done.47, f32[1024,128]{1,0:T(8,128)S(1)} %copy-done.14, ...), custom_call_target="tpu_custom_call" | custom-call | flops 40000000 | bytes 10000 | tf_op jit(solution)/shard_map/pallas_call | solution.py:747
  31.8 3.4 %shard_map.324 = (f32[1024,512]{1,0:T(8,128)S(1)}, bf16[4,4,128,128]{3,2,1,0:T(8,128)(2,1)S(1)}) custom-call(s32[7]{0:T(128)S(1)} %copy-done.43, bf16[1024,1536]{1,0:T(8,128)(2,1)S(1)} %get-tuple-element.140.refs_0_.refs_3_, bf16[1024,1536]{1,0:T(8,128)(2,1)S(1)} %copy-done.2, bf16[1024,768]{1,0:T(8,128)(2,1)S(1)} %copy-done.4, s32[1024,128]{1,0:T(8,128)S(1)} %copy-done.10, ...), custom_call_target="tpu_custom_call" | custom-call | flops 40000000 | bytes 10000 | tf_op jit(solution)/shard_map/pallas_call | solution.py:747
  38.8 3.4 %shard_map.325 = (f32[1024,512]{1,0:T(8,128)S(1)}, bf16[4,4,128,128]{3,2,1,0:T(8,128)(2,1)S(1)}) custom-call(s32[7]{0:T(128)S(1)} %copy-done.43, bf16[1024,1536]{1,0:T(8,128)(2,1)S(1)} %get-tuple-element.140.refs_0_.refs_3_, bf16[1024,1536]{1,0:T(8,128)(2,1)S(1)} %copy-done.2, bf16[1024,768]{1,0:T(8,128)(2,1)S(1)} %copy-done.4, s32[1024,128]{1,0:T(8,128)S(1)} %copy-done.10, ...), custom_call_target="tpu_custom_call" | custom-call | flops 40000000 | bytes 10000 | tf_op jit(solution)/shard_map/pallas_call | solution.py:747
  44.4 3.3 %collective-permute-start.4 = (bf16[7,128,128]{2,1,0:T(8,128)(2,1)S(1)}, bf16[7,128,128]{2,1,0:T(8,128)(2,1)S(1)}, u32[]{:S(2)}, u32[]{:S(2)}) collective-permute-start(bf16[7,128,128]{2,1,0:T(8,128)(2,1)S(1)} %add_convert_fusion.4.refs_5_), channel_id=1, source_target_pairs={{0,16},{1,17},{2,18},{3,19},{4,20},{5,21},{6,22},{7,23},{8,24},{9,... | collective-permute-start | bytes 688136 | tf_op jit(solution)/shard_map/ppermute | solution.py:644
  47.7 3.4 %shard_map.326 = (f32[1024,512]{1,0:T(8,128)S(1)}, bf16[4,4,128,128]{3,2,1,0:T(8,128)(2,1)S(1)}) custom-call(s32[7]{0:T(128)S(1)} %copy-done.43, bf16[1024,1536]{1,0:T(8,128)(2,1)S(1)} %get-tuple-element.140.refs_0_.refs_3_, bf16[1024,1536]{1,0:T(8,128)(2,1)S(1)} %copy-done.2, bf16[1024,768]{1,0:T(8,128)(2,1)S(1)} %copy-done.4, s32[1024,128]{1,0:T(8,128)S(1)} %copy-done.10, ...), custom_call_target="tpu_custom_call" | custom-call | flops 40000000 | bytes 10000 | tf_op jit(solution)/shard_map/pallas_call | solution.py:747
  53.2 5.6 %collective-permute-done.4.refs_16_ = bf16[7,128,128]{2,1,0:T(8,128)(2,1)S(1)} collective-permute-done((bf16[7,128,128]{2,1,0:T(8,128)(2,1)S(1)}, bf16[7,128,128]{2,1,0:T(8,128)(2,1)S(1)}, u32[]{:S(2)}, u32[]{:S(2)}) %collective-permute-start.4) | collective-permute-done | bytes 229408 | tf_op jit(solution)/shard_map/ppermute | solution.py:644
  59.6 51.9 %shard_map.327 = (bf16[1024,768]{1,0:T(8,128)(2,1)}, bf16[1024,768]{1,0:T(8,128)(2,1)}, bf16[1024,768]{1,0:T(8,128)(2,1)}, bf16[1024,3072]{1,0:T(8,128)(2,1)}, b...) custom-call(s32[7]{0:T(128)} %stack.31.spot_ref, ...), custom_call_target="tpu_custom_call" | custom-call | flops 500000000 | bytes 10000 | tf_op jit(solution)/shard_map/pallas_call | solution.py:747
  116.3 8.3 %shard_map.328 = (bf16[16,48,768]{2,1,0:T(8,128)(2,1)S(1)}, bf16[16,48,768]{2,1,0:T(8,128)(2,1)S(1)}, bf16[16,48,768]{2,1,0:T(8,128)(2,1)S(1)}, bf16[16,48,768]{2,1,0:T(8,128)(2,1)S(1)}) custom-call(s32[7]{0:T(128)S(1)} %copy-done.44, bf16[1024,3072]{1,0:T(8,128)(2,1)} %get-tuple-element.164.refs_0_, bf16[1024,768]{1,0:T(8,128)(2,1)S(1)} %copy-done.35, ...), custom_call_target="tpu_custom_call" | custom-call | flops 90000000 | bytes 10000 | tf_op jit(solution)/shard_map/pallas_call | solution.py:747
  126.6 3.2 %collective-permute-start.10 = (bf16[7,128,128]{2,1,0:T(8,128)(2,1)S(1)}, bf16[7,128,128]{2,1,0:T(8,128)(2,1)S(1)}, u32[]{:S(2)}, u32[]{:S(2)}) collective-permute-start(bf16[7,128,128]{2,1,0:T(8,128)(2,1)S(1)} %add_convert_fusion.2.refs_2_), channel_id=1, source_target_pairs={{0,4},{1,5},{2,6},{3,7},{4,0},{5,1},{6,2},{7,3},{8,12},{9,13},{10,... | collective-permute-start | bytes 688136 | tf_op jit(solution)/shard_map/ppermute | solution.py:644
  129.8 5.1 %shard_map.329 = (bf16[16,48,768]{2,1,0:T(8,128)(2,1)S(1)}, bf16[16,48,768]{2,1,0:T(8,128)(2,1)S(1)}) custom-call(s32[7]{0:T(128)S(1)} %copy-done.44, bf16[1024,768]{1,0:T(8,128)(2,1)S(1)} %copy-done.19, bf16[1024,3072]{1,0:T(8,128)(2,1)} %get-tuple-element.180.refs_1_, bf16[7,128,128]{2,1,0:T(8,128)(2,1)S(1)} %add_convert_fusion.2.refs_2_), custom_call_target="tpu_custom_call" | custom-call | flops 50000000 | bytes 10000 | tf_op jit(solution)/shard_map/pallas_call | solution.py:747
  135.0 5.4 %shard_map.330 = (bf16[16,48,768]{2,1,0:T(8,128)(2,1)S(1)}, bf16[16,48,768]{2,1,0:T(8,128)(2,1)S(1)}) custom-call(s32[7]{0:T(128)S(1)} %copy-done.44, bf16[1024,768]{1,0:T(8,128)(2,1)S(1)} %copy-done.19, bf16[1024,3072]{1,0:T(8,128)(2,1)} %get-tuple-element.180.refs_1_, bf16[16,48,768]{2,1,0:T(8,128)(2,1)S(1)} %get-tuple-element.181.refs_2_), custom_call_target="tpu_custom_call" | custom-call | flops 50000000 | bytes 10000 | tf_op jit(solution)/shard_map/pallas_call | solution.py:747
  146.1 4.5 %shard_map.332.refs_12_.refs_1_ = bf16[1024,384]{1,0:T(8,128)(2,1)S(1)} custom-call(s32[7]{0:T(128)S(1)} %copy-done.44, bf16[1024,1536]{1,0:T(8,128)(2,1)S(1)} %copy-done.1, bf16[1024,1536]{1,0:T(8,128)(2,1)S(1)} %copy-done.3, bf16[1024,768]{1,0:T(8,128)(2,1)S(1)} %copy-done.5, bf16[1024,1536]{1,0:T(8,128)(2,1)S(1)} %copy-done.8, ...), custom_call_target="tpu_custom_call" | custom-call | flops 70000000 | bytes 10000 | tf_op jit(solution)/shard_map/pallas_call | solution.py:747
  151.5 6.7 %collective-permute-done.15 = bf16[8,1,48,768]{3,2,1,0:T(8,128)(2,1)S(1)} collective-permute-done((bf16[8,1,48,768]{3,2,1,0:T(8,128)(2,1)S(1)}, bf16[8,1,48,768]{3,2,1,0:T(8,128)(2,1)S(1)}, u32[]{:S(2)}, u32[]{:S(2)}) %collective-permute-start.15) | collective-permute-done | bytes 589856 | tf_op jit(solution)/shard_map/ppermute | solution.py:644
  163.5 11.0 %shard_map.334 = (bf16[1024,384]{1,0:T(8,128)(2,1)S(1)}, bf16[16,32,768]{2,1,0:T(8,128)(2,1)S(1)}, bf16[16,32,768]{2,1,0:T(8,128)(2,1)S(1)}, bf16[16,32,768]{2,1,0:T(8,128)(2,1)}, bf16[16,32,768]{2,1,0:T(8,128)(2,1)S(1)}) custom-call(s32[7]{0:T(128)S(1)} %copy-done.44, bf16[1024,1536]{1,0:T(8,128)(2,1)S(1)} %copy-done.1, bf16[1024,1536]{1,0:T(8,128)(2,1)S(1)} %copy-done.3, ...), custom_call_target="tpu_custom_call" | custom-call | flops 90000000 | bytes 10000 | tf_op jit(solution)/shard_map/pallas_call | solution.py:747
  179.1 8.6 %shard_map.337 = (bf16[1024,384]{1,0:T(8,128)(2,1)S(1)}, bf16[1024,384]{1,0:T(8,128)(2,1)S(1)}, bf16[16,32,768]{2,1,0:T(8,128)(2,1)S(1)}, bf16[16,32,768]{2,1,0:T(8,128)(2,1)S(1)}) custom-call(s32[7]{0:T(128)S(1)} %copy-done.44, bf16[1024,1536]{1,0:T(8,128)(2,1)S(1)} %copy-done.1, bf16[1024,1536]{1,0:T(8,128)(2,1)S(1)} %copy-done.3, ...), custom_call_target="tpu_custom_call" | custom-call | flops 100000000 | bytes 10000 | tf_op jit(solution)/shard_map/pallas_call | solution.py:747
  187.7 5.4 %collective-permute-done.20.refs_9_ = bf16[4,1,96,768]{3,2,1,0:T(8,128)(2,1)S(1)} collective-permute-done((bf16[4,1,96,768]{3,2,1,0:T(8,128)(2,1)S(1)}, bf16[4,1,96,768]{3,2,1,0:T(8,128)(2,1)S(1)}, u32[]{:S(2)}, u32[]{:S(2)}) %collective-permute-start.20) | collective-permute-done | bytes 589856 | tf_op jit(solution)/shard_map/ppermute | solution.py:644
  194.7 2.5 collective-permute-start.24
  198.4 8.8 %shard_map.339 = (bf16[1024,384]{1,0:T(8,128)(2,1)S(1)}, bf16[1024,384]{1,0:T(8,128)(2,1)S(1)}, bf16[16,32,768]{2,1,0:T(8,128)(2,1)S(1)}, bf16[16,32,768]{2,1,0:T(8,128)(2,1)S(1)}) custom-call(s32[7]{0:T(128)S(1)} %copy-done.44, bf16[1024,1536]{1,0:T(8,128)(2,1)S(1)} %copy-done.1, bf16[1024,1536]{1,0:T(8,128)(2,1)S(1)} %copy-done.3, ...), custom_call_target="tpu_custom_call" | custom-call | flops 100000000 | bytes 10000 | tf_op jit(solution)/shard_map/pallas_call | solution.py:747
  207.2 2.4 collective-permute-done.24.refs_11_
  219.1 9.3 %shard_map.341.refs_8_ = bf16[1024,768]{1,0:T(8,128)(2,1)} custom-call(s32[7]{0:T(128)S(1)} %copy-done.44, f32[1024,768]{1,0:T(8,128)} %get-tuple-element.158.refs_0_, bf16[1024,384]{1,0:T(8,128)(2,1)} %copy-done.16, bf16[1024,384]{1,0:T(8,128)(2,1)} %copy-done.24, bf16[1024,384]{1,0:T(8,128)(2,1)} %copy-done.23, bf16[1024,384]{1,0:T(8,128)(2,1)} %copy-done.25, ...), custom_call_target="tpu_custom_call" | custom-call | flops 80000000 | bytes 10000 | tf_op jit(solution)/shard_map/pallas_call | solution.py:747
  250.0 2.4 collective-permute-start.39
  253.0 2.6 %collective-permute-done.39 = bf16[1,1,64,768]{3,2,1,0:T(8,128)(2,1)S(1)} collective-permute-done((bf16[1,1,64,768]{3,2,1,0:T(8,128)(2,1)S(1)}, bf16[1,1,64,768]{3,2,1,0:T(8,128)(2,1)S(1)}, u32[]{:S(2)}, u32[]{:S(2)}) %collective-permute-start.39) | collective-permute-done | bytes 98336 | tf_op jit(solution)/shard_map/ppermute | solution.py:644
  (227 shorter events, 79.5 us)
Async XLA Ops:
  16.4 11.6 %collective-permute-start.1 = (bf16[7,128,128]{2,1,0:T(8,128)(2,1)S(1)}, bf16[7,128,128]{2,1,0:T(8,128)(2,1)S(1)}, u32[]{:S(2)}, u32[]{:S(2)}) collective-permute-start(bf16[7,128,128]{2,1,0:T(8,128)(2,1)S(1)} %add_convert_fusion.7.refs_4_), channel_id=1, source_target_pairs={{0,2},{1,3},{2,0},{3,1},{4,6},{5,7},{6,4},{7,5},{8,10},{9,11},{10,... | collective-permute-start | bytes 688136 | tf_op jit(solution)/shard_map/ppermute | solution.py:644
  37.3 15.9 %collective-permute-start.5 = (bf16[7,128,128]{2,1,0:T(8,128)(2,1)S(1)}, bf16[7,128,128]{2,1,0:T(8,128)(2,1)S(1)}, u32[]{:S(2)}, u32[]{:S(2)}) collective-permute-start(bf16[7,128,128]{2,1,0:T(8,128)(2,1)S(1)} %copy-done.57), channel_id=1, source_target_pairs={{0,1},{1,2},{2,3},{3,4},{4,5},{5,6},{6,7},{7,8},{8,9},{9,10},{10,1... | collective-permute-start | bytes 688136 | tf_op jit(solution)/shard_map/ppermute | solution.py:861
  44.4 14.4 %collective-permute-start.4 = (bf16[7,128,128]{2,1,0:T(8,128)(2,1)S(1)}, bf16[7,128,128]{2,1,0:T(8,128)(2,1)S(1)}, u32[]{:S(2)}, u32[]{:S(2)}) collective-permute-start(bf16[7,128,128]{2,1,0:T(8,128)(2,1)S(1)} %add_convert_fusion.4.refs_5_), channel_id=1, source_target_pairs={{0,16},{1,17},{2,18},{3,19},{4,20},{5,21},{6,22},{7,23},{8,24},{9,... | collective-permute-start | bytes 688136 | tf_op jit(solution)/shard_map/ppermute | solution.py:644
  124.7 15.7 %collective-permute-start.9 = (bf16[16,48,768]{2,1,0:T(8,128)(2,1)S(1)}, bf16[16,48,768]{2,1,0:T(8,128)(2,1)S(1)}, u32[]{:S(2)}, u32[]{:S(2)}) collective-permute-start(bf16[16,48,768]{2,1,0:T(8,128)(2,1)S(1)} %get-tuple-element.176), channel_id=1, source_target_pairs={{0,1},{1,0},{2,3},{3,2},{4,5},{5,4},{6,7},{7,6},{8,9},{9,8},{10,11... | collective-permute-start | bytes 3538952 | tf_op jit(solution)/shard_map/ppermute | solution.py:644
  124.8 15.7 %collective-permute-start.8 = (bf16[16,48,768]{2,1,0:T(8,128)(2,1)S(1)}, bf16[16,48,768]{2,1,0:T(8,128)(2,1)S(1)}, u32[]{:S(2)}, u32[]{:S(2)}) collective-permute-start(bf16[16,48,768]{2,1,0:T(8,128)(2,1)S(1)} %get-tuple-element.173), channel_id=1, source_target_pairs={{0,1},{1,0},{2,3},{3,2},{4,5},{5,4},{6,7},{7,6},{8,9},{9,8},{10,11... | collective-permute-start | bytes 3538952 | tf_op jit(solution)/shard_map/ppermute | solution.py:644
  125.3 15.1 %collective-permute-start.11 = (bf16[7,128,128]{2,1,0:T(8,128)(2,1)S(1)}, bf16[7,128,128]{2,1,0:T(8,128)(2,1)S(1)}, u32[]{:S(2)}, u32[]{:S(2)}) collective-permute-start(bf16[7,128,128]{2,1,0:T(8,128)(2,1)S(1)} %copy-done.56), channel_id=1, source_target_pairs={{1,0},{2,1},{3,2},{4,3},{5,4},{6,5},{7,6},{8,7},{9,8},{10,9},{11,1... | collective-permute-start | bytes 688136 | tf_op jit(solution)/shard_map/ppermute | solution.py:1006
  126.6 13.8 %collective-permute-start.10 = (bf16[7,128,128]{2,1,0:T(8,128)(2,1)S(1)}, bf16[7,128,128]{2,1,0:T(8,128)(2,1)S(1)}, u32[]{:S(2)}, u32[]{:S(2)}) collective-permute-start(bf16[7,128,128]{2,1,0:T(8,128)(2,1)S(1)} %add_convert_fusion.2.refs_2_), channel_id=1, source_target_pairs={{0,4},{1,5},{2,6},{3,7},{4,0},{5,1},{6,2},{7,3},{8,12},{9,13},{10,... | collective-permute-start | bytes 688136 | tf_op jit(solution)/shard_map/ppermute | solution.py:644
  142.5 16.4 %collective-permute-start.13 = (bf16[16,48,768]{2,1,0:T(8,128)(2,1)S(1)}, bf16[16,48,768]{2,1,0:T(8,128)(2,1)S(1)}, u32[]{:S(2)}, u32[]{:S(2)}) collective-permute-start(bf16[16,48,768]{2,1,0:T(8,128)(2,1)S(1)} %get-tuple-element.192), channel_id=1, source_target_pairs={{0,1},{1,0},{2,3},{3,2},{4,5},{5,4},{6,7},{7,6},{8,9},{9,8},{10,11... | collective-permute-start | bytes 3538952 | tf_op jit(solution)/shard_map/ppermute | solution.py:644
  142.5 16.4 %collective-permute-start.12 = (bf16[16,48,768]{2,1,0:T(8,128)(2,1)S(1)}, bf16[16,48,768]{2,1,0:T(8,128)(2,1)S(1)}, u32[]{:S(2)}, u32[]{:S(2)}) collective-permute-start(bf16[16,48,768]{2,1,0:T(8,128)(2,1)S(1)} %get-tuple-element.190), channel_id=1, source_target_pairs={{0,1},{1,0},{2,3},{3,2},{4,5},{5,4},{6,7},{7,6},{8,9},{9,8},{10,11... | collective-permute-start | bytes 3538952 | tf_op jit(solution)/shard_map/ppermute | solution.py:644
  143.0 15.2 %collective-permute-start.15 = (bf16[8,1,48,768]{3,2,1,0:T(8,128)(2,1)S(1)}, bf16[8,1,48,768]{3,2,1,0:T(8,128)(2,1)S(1)}, u32[]{:S(2)}, u32[]{:S(2)}) collective-permute-start(bf16[8,1,48,768]{3,2,1,0:T(8,128)(2,1)S(1)} %get-tuple-element.193), channel_id=1, source_target_pairs={{0,2},{1,3},{2,0},{3,1},{4,6},{5,7},{6,4},{7,5},{8,10},{9,11},{10,... | collective-permute-start | bytes 1769480 | tf_op jit(solution)/shard_map/ppermute | solution.py:644
  143.9 15.0 %collective-permute-start.16 = (bf16[4,2,48,768]{3,2,1,0:T(8,128)(2,1)S(1)}, bf16[4,2,48,768]{3,2,1,0:T(8,128)(2,1)S(1)}, u32[]{:S(2)}, u32[]{:S(2)}) collective-permute-start(bf16[4,2,48,768]{3,2,1,0:T(8,128)(2,1)S(1)} %get-tuple-element.194), channel_id=1, source_target_pairs={{0,4},{1,5},{2,6},{3,7},{4,0},{5,1},{6,2},{7,3},{8,12},{9,13},{10,... | collective-permute-start | bytes 1769480 | tf_op jit(solution)/shard_map/ppermute | solution.py:644
  160.1 14.4 %collective-permute-start.18 = (bf16[8,1,48,768]{3,2,1,0:T(8,128)(2,1)S(1)}, bf16[8,1,48,768]{3,2,1,0:T(8,128)(2,1)S(1)}, u32[]{:S(2)}, u32[]{:S(2)}) collective-permute-start(bf16[8,1,48,768]{3,2,1,0:T(8,128)(2,1)S(1)} %get-tuple-element.200), channel_id=1, source_target_pairs={{0,2},{1,3},{2,0},{3,1},{4,6},{5,7},{6,4},{7,5},{8,10},{9,11},{10,... | collective-permute-start | bytes 1769480 | tf_op jit(solution)/shard_map/ppermute | solution.py:644
  161.3 13.8 %collective-permute-start.19 = (bf16[4,2,48,768]{3,2,1,0:T(8,128)(2,1)S(1)}, bf16[4,2,48,768]{3,2,1,0:T(8,128)(2,1)S(1)}, u32[]{:S(2)}, u32[]{:S(2)}) collective-permute-start(bf16[4,2,48,768]{3,2,1,0:T(8,128)(2,1)S(1)} %get-tuple-element.201), channel_id=1, source_target_pairs={{0,4},{1,5},{2,6},{3,7},{4,0},{5,1},{6,2},{7,3},{8,12},{9,13},{10,... | collective-permute-start | bytes 1769480 | tf_op jit(solution)/shard_map/ppermute | solution.py:644
  161.6 13.0 %collective-permute-start.17 = (bf16[7,128,128]{2,1,0:T(8,128)(2,1)S(1)}, bf16[7,128,128]{2,1,0:T(8,128)(2,1)S(1)}, u32[]{:S(2)}, u32[]{:S(2)}) collective-permute-start(bf16[7,128,128]{2,1,0:T(8,128)(2,1)S(1)} %add_convert_fusion.refs_4_), channel_id=1, source_target_pairs={{0,16},{1,17},{2,18},{3,19},{4,20},{5,21},{6,22},{7,23},{8,24},{9,... | collective-permute-start | bytes 688136 | tf_op jit(solution)/shard_map/ppermute | solution.py:644
  177.3 16.2 %collective-permute-start.23 = (bf16[16,32,768]{2,1,0:T(8,128)(2,1)}, bf16[16,32,768]{2,1,0:T(8,128)(2,1)S(1)}, u32[]{:S(2)}, u32[]{:S(2)}) collective-permute-start(bf16[16,32,768]{2,1,0:T(8,128)(2,1)} %get-tuple-element.214), channel_id=1, source_target_pairs={{0,1},{1,0},{2,3},{3,2},{4,5},{5,4},{6,7},{7,6},{8,9},{9,8},{10,11... | collective-permute-start | bytes 2359304 | tf_op jit(solution)/shard_map/ppermute | solution.py:644
  177.4 16.1 %collective-permute-start.22 = (bf16[16,32,768]{2,1,0:T(8,128)(2,1)S(1)}, bf16[16,32,768]{2,1,0:T(8,128)(2,1)S(1)}, u32[]{:S(2)}, u32[]{:S(2)}) collective-permute-start(bf16[16,32,768]{2,1,0:T(8,128)(2,1)S(1)} %get-tuple-element.211), channel_id=1, source_target_pairs={{0,1},{1,0},{2,3},{3,2},{4,5},{5,4},{6,7},{7,6},{8,9},{9,8},{10,11... | collective-permute-start | bytes 2359304 | tf_op jit(solution)/shard_map/ppermute | solution.py:644
  177.9 15.3 %collective-permute-start.20 = (bf16[4,1,96,768]{3,2,1,0:T(8,128)(2,1)S(1)}, bf16[4,1,96,768]{3,2,1,0:T(8,128)(2,1)S(1)}, u32[]{:S(2)}, u32[]{:S(2)}) collective-permute-start(bf16[4,1,96,768]{3,2,1,0:T(8,128)(2,1)S(1)} %get-tuple-element.207), channel_id=1, source_target_pairs={{0,4},{1,5},{2,6},{3,7},{4,0},{5,1},{6,2},{7,3},{8,12},{9,13},{10,... | collective-permute-start | bytes 1769480 | tf_op jit(solution)/shard_map/ppermute | solution.py:644
  178.4 15.0 %collective-permute-start.21 = (bf16[4,1,96,768]{3,2,1,0:T(8,128)(2,1)S(1)}, bf16[4,1,96,768]{3,2,1,0:T(8,128)(2,1)S(1)}, u32[]{:S(2)}, u32[]{:S(2)}) collective-permute-start(bf16[4,1,96,768]{3,2,1,0:T(8,128)(2,1)S(1)} %get-tuple-element.208), channel_id=1, source_target_pairs={{0,2},{1,3},{2,0},{3,1},{4,6},{5,7},{6,4},{7,5},{8,10},{9,11},{10,... | collective-permute-start | bytes 1769480 | tf_op jit(solution)/shard_map/ppermute | solution.py:644
  194.7 14.9 %collective-permute-start.24 = (bf16[2,1,192,768]{3,2,1,0:T(8,128)(2,1)S(1)}, bf16[2,1,192,768]{3,2,1,0:T(8,128)(2,1)S(1)}, u32[]{:S(2)}, u32[]{:S(2)}) collective-permute-start(bf16[2,1,192,768]{3,2,1,0:T(8,128)(2,1)S(1)} %get-tuple-element.221), channel_id=1, source_target_pairs={{0,8},{1,9},{2,10},{3,11},{4,12},{5,13},{6,14},{7,15},{8,0},{9,1},... | collective-permute-start | bytes 1769480 | tf_op jit(solution)/shard_map/ppermute | solution.py:644
  213.9 16.5 %collective-permute-start.33 = (bf16[1,1,192,768]{3,2,1,0:T(8,128)(2,1)}, bf16[1,1,192,768]{3,2,1,0:T(8,128)(2,1)S(1)}, u32[]{:S(2)}, u32[]{:S(2)}) collective-permute-start(bf16[1,1,192,768]{3,2,1,0:T(8,128)(2,1)} %get-tuple-element.239), channel_id=1, source_target_pairs={{0,16},{1,17},{2,18},{3,19},{4,20},{5,21},{6,22},{7,23},{8,24},{9,... | collective-permute-start | bytes 884744 | tf_op jit(solution)/shard_map/ppermute | solution.py:644
  215.1 16.2 %collective-permute-start.29 = (bf16[8,1,32,768]{3,2,1,0:T(8,128)(2,1)}, bf16[8,1,32,768]{3,2,1,0:T(8,128)(2,1)S(1)}, u32[]{:S(2)}, u32[]{:S(2)}) collective-permute-start(bf16[8,1,32,768]{3,2,1,0:T(8,128)(2,1)} %get-tuple-element.232), channel_id=1, source_target_pairs={{0,2},{1,3},{2,0},{3,1},{4,6},{5,7},{6,4},{7,5},{8,10},{9,11},{10,... | collective-permute-start | bytes 1179656 | tf_op jit(solution)/shard_map/ppermute | solution.py:644
  216.0 15.3 %collective-permute-start.30 = (bf16[4,2,32,768]{3,2,1,0:T(8,128)(2,1)}, bf16[4,2,32,768]{3,2,1,0:T(8,128)(2,1)S(1)}, u32[]{:S(2)}, u32[]{:S(2)}) collective-permute-start(bf16[4,2,32,768]{3,2,1,0:T(8,128)(2,1)} %get-tuple-element.234), channel_id=1, source_target_pairs={{0,4},{1,5},{2,6},{3,7},{4,0},{5,1},{6,2},{7,3},{8,12},{9,13},{10,... | collective-permute-start | bytes 1179656 | tf_op jit(solution)/shard_map/ppermute | solution.py:644
  216.8 14.5 %collective-permute-start.31 = (bf16[4,1,32,768]{3,2,1,0:T(8,128)(2,1)}, bf16[4,1,32,768]{3,2,1,0:T(8,128)(2,1)S(1)}, u32[]{:S(2)}, u32[]{:S(2)}) collective-permute-start(bf16[4,1,32,768]{3,2,1,0:T(8,128)(2,1)} %get-tuple-element.236), channel_id=1, source_target_pairs={{0,4},{1,5},{2,6},{3,7},{4,0},{5,1},{6,2},{7,3},{8,12},{9,13},{10,... | collective-permute-start | bytes 589832 | tf_op jit(solution)/shard_map/ppermute | solution.py:644
  218.0 13.2 %collective-permute-start.32 = (bf16[4,1,32,768]{3,2,1,0:T(8,128)(2,1)}, bf16[4,1,32,768]{3,2,1,0:T(8,128)(2,1)S(1)}, u32[]{:S(2)}, u32[]{:S(2)}) collective-permute-start(bf16[4,1,32,768]{3,2,1,0:T(8,128)(2,1)} %get-tuple-element.238), channel_id=1, source_target_pairs={{0,2},{1,3},{2,0},{3,1},{4,6},{5,7},{6,4},{7,5},{8,10},{9,11},{10,... | collective-permute-start | bytes 589832 | tf_op jit(solution)/shard_map/ppermute | solution.py:644
  (74 other events, 626.6 us)
